TPU v7x, 256 devices: a whole 4x4x8 slice. The times are simulated.
256 devices in a mesh: sec: 4 (over z_hi), gx: 16 (over x, y), gy: 4 (over z_lo, core).
Axes of the slice: x: 4, y: 4, z: 8 (z_hi: 4, z_lo: 2; z = z_hi * 2 + z_lo), core: 2. Of those that a mesh axis runs over, the one named last changes fastest.
Arguments:
- reg_disp: float32 [1024, 256, 256], P(('sec', 'gx'), 'gy'), may hold values from -6 to 6
- reg_prev: float32 [1024, 256, 256], P(('sec', 'gx'), 'gy'), may hold values from -6 to 6
- reg_coef: float32 [1024, 256, 256], P(('sec', 'gx'), 'gy'), may hold values from 0.02 to 0.15
- basin_disp: float32 [4, 64, 32768], P('sec', None, ('gx', 'gy')), may hold values from -4 to 4
- face_index: int32 [4, 32768], P('sec', ('gx', 'gy')), may hold values from 0 to 65535, as said below
- soil_class: int32 [4, 64, 32768], P('sec', None, ('gx', 'gy')), may hold values from 0 to 7, as said below
- spring_count: int32 [8], replicated, may hold values from 1 to 16, as said below
- spring_modulus: float32 [8, 16], replicated, may hold values from 0.02 to 0.1
- spring_yield: float32 [8, 16], replicated, may hold values from 0.005 to 0.05
Outputs:
- reg_final: float32 [1024, 256, 256], P(('sec', 'gx'), 'gy')
- basin_final: float32 [4, 64, 32768], P('sec', None, ('gx', 'gy'))
Inputs may be any that keep to these rules, and one draw needn't show every extreme that they name: `face_index`: a cell of the quarter's face; in every quarter some column uses the first face cell and some column the last. `soil_class`: soil class ids. `spring_count`: some class has 16 springs and some class has one.
All inputs are finite; a program needn't handle non-finite values.
Results may differ from a plain program's by a relative error of at most 0.0002.
Values sent between devices are 32-bit elements; how exact they have to be, the bound alone decides.
No kernel may reach another device: no remote copies, remote signals or barrier semaphores. Data moves between devices by JAX's collectives and lax.ppermute only.
A program may use at most 128 MiB of HBM per device.

v0:
```python
import jax
import jax.numpy as jnp
from jax import lax
from jax.sharding import PartitionSpec as P

STEPS = 8


stress_rate = 0.5


def extended(block, sides, width):
    for axis, dim in sides:
        count = lax.axis_size(axis)
        forward = [(i, i + 1) for i in range(count - 1)]
        backward = [(target, source) for source, target in forward]
        low = lax.ppermute(
            lax.slice_in_dim(block, block.shape[dim] - width, None, axis=dim), axis, forward
        )
        high = lax.ppermute(lax.slice_in_dim(block, 0, width, axis=dim), axis, backward)
        block = jnp.concatenate([low, block, high], axis=dim)
    return block


def laplace_rim(padded, center):
    above = jnp.concatenate([center[:, :, :1], center[:, :, :-1]], axis=2)
    below = jnp.concatenate([center[:, :, 1:], jnp.zeros_like(center[:, :, :1])], axis=2)
    beside = padded[2:, 1:-1] + padded[:-2, 1:-1] + padded[1:-1, 2:] + padded[1:-1, :-2]
    return beside + above + below - 6.0 * center


def shards(
    reg_disp,
    reg_prev,
    reg_coef,
    basin_disp,
    face_index,
    soil_class,
    spring_count,
    spring_modulus,
    spring_yield,
):
    cells_x, cells_y, cells_z = reg_disp.shape
    face_depth = cells_z // 4
    across_y = lax.axis_size("gy")
    wide_y = cells_y * across_y
    target = face_index[0]
    pos_x = target // wide_y
    pos_y = target % wide_y
    blocked = (
        (pos_x // cells_x * across_y + pos_y // cells_y) * (cells_x * cells_y)
        + pos_x % cells_x * cells_y
        + pos_y % cells_y
    )
    soil = soil_class[0]
    classes = jnp.arange(spring_count.shape[0], dtype=jnp.int32)
    matches = soil[None] == classes[:, None, None]
    onehot = matches.astype(jnp.float32)
    modulus = jnp.einsum("ck,clx->klx", spring_modulus, onehot, precision=lax.Precision.HIGHEST)
    limits = jnp.einsum("ck,clx->klx", spring_yield, onehot, precision=lax.Precision.HIGHEST)
    count_cell = jnp.sum(jnp.where(matches, spring_count[:, None, None], 0), axis=0)
    levels = jnp.arange(spring_modulus.shape[1], dtype=jnp.int32)
    limits = limits * (levels[:, None, None] < count_cell[None]).astype(jnp.float32)
    displace = basin_disp[0]
    state = (displace, jnp.zeros_like(displace), jnp.zeros_like(modulus), jnp.zeros_like(displace))
    current, former = (reg_disp, reg_prev)
    planes = []
    for step in range(STEPS):
        padded = extended(current, ((("sec", "gx"), 0), ("gy", 1)), 1)
        following = 2.0 * current - former + reg_coef * laplace_rim(padded, current)
        current, former = (following, current)
        planes.append(current[:, :, face_depth].reshape(cells_x * cells_y))
    gathered = lax.all_gather(jnp.stack(planes), ("gx", "gy"), axis=1, tiled=True)
    base = jnp.take(gathered, blocked, axis=1)
    for step in range(STEPS):
        advance_displace, velocity, springs, strain_old = state
        lower = jnp.concatenate([advance_displace[1:], base[step][None]], axis=0)
        strain = lower - advance_displace
        increment = strain - strain_old
        springs = jnp.clip(springs + modulus * increment[None], -limits, limits)
        stress = jnp.sum(springs, axis=0)
        above = jnp.concatenate([jnp.zeros_like(stress[:1]), stress[:-1]], axis=0)
        velocity = velocity + stress_rate * (stress - above)
        state = (advance_displace + velocity, velocity, springs, strain)
    return (current, state[0][None])


def solution(mesh):
    in_specs = (
        P(("sec", "gx"), "gy", None),
        P(("sec", "gx"), "gy", None),
        P(("sec", "gx"), "gy", None),
        P("sec", None, ("gx", "gy")),
        P("sec", ("gx", "gy")),
        P("sec", None, ("gx", "gy")),
        P(),
        P(),
        P(),
    )
    out_specs = (P(("sec", "gx"), "gy", None), P("sec", None, ("gx", "gy")))
    return jax.shard_map(shards, mesh=mesh, in_specs=in_specs, out_specs=out_specs, check_vma=False)
```

profile of v0, /device:TPU:95, one launch (start us, length us, event | category | flops | bytes accessed | tf_op | source)
XLA Modules:
  0.0 459.0 jit_solution(17162231756281435694)
XLA Ops:
  8.2 5.7 %collective-permute-start.1 = (f32[1,64,256]{2,1,0:T(8,128)S(1)}, f32[1,64,256]{2,1,0:T(8,128)S(1)}, u32[]{:S(2)}, u32[]{:S(2)}) collective-permute-start(f32[1,64,256]{2,1,0:T(8,128)S(1)} %get-tuple-element.69), channel_id=1, source_target_pairs={{0,4},{4,8},{8,12},{12,16},{16,20},{20,24},{24,28},{28,32},{32,36}... | collective-permute-start | bytes 196616 | tf_op jit(solution)/shard_map/ppermute | solution.py:17
  17.3 8.5 %collective-permute-done = f32[1,64,256]{2,1,0:T(8,128)S(1)} collective-permute-done((f32[1,64,256]{2,1,0:T(8,128)S(1)}, f32[1,64,256]{2,1,0:T(8,128)S(1)}, u32[]{:S(2)}, u32[]{:S(2)}) %collective-permute-start) | collective-permute-done | bytes 65568 | tf_op jit(solution)/shard_map/ppermute | solution.py:20
  25.9 4.2 collective-permute-start.2
  36.2 9.7 %collective-permute-start.5 = (f32[1,64,256]{2,1,0:T(8,128)S(1)}, f32[1,64,256]{2,1,0:T(8,128)S(1)}, u32[]{:S(2)}, u32[]{:S(2)}) collective-permute-start(f32[1,64,256]{2,1,0:T(8,128)S(1)} %get-tuple-element.64), channel_id=1, source_target_pairs={{0,4},{4,8},{8,12},{12,16},{16,20},{20,24},{24,28},{28,32},{32,36}... | collective-permute-start | bytes 196616 | tf_op jit(solution)/shard_map/ppermute | solution.py:17
  47.3 3.2 collective-permute-start.6
  50.5 3.8 collective-permute-start.7
  55.5 2.9 fusion.74
  60.3 10.3 %collective-permute-start.9 = (f32[1,64,256]{2,1,0:T(8,128)S(1)}, f32[1,64,256]{2,1,0:T(8,128)S(1)}, u32[]{:S(2)}, u32[]{:S(2)}) collective-permute-start(f32[1,64,256]{2,1,0:T(8,128)S(1)} %get-tuple-element.60), channel_id=1, source_target_pairs={{0,4},{4,8},{8,12},{12,16},{16,20},{20,24},{24,28},{28,32},{32,36}... | collective-permute-start | bytes 196616 | tf_op jit(solution)/shard_map/ppermute | solution.py:17
  73.9 4.7 %collective-permute-start.11 = (f32[18,1,256]{2,1,0:T(1,128)S(1)}, f32[18,1,256]{2,1,0:T(1,128)S(1)}, u32[]{:S(2)}, u32[]{:S(2)}) collective-permute-start(f32[18,1,256]{2,1,0:T(1,128)S(1)} %get-tuple-element.19), channel_id=1, source_target_pairs={{0,1},{1,2},{2,3},{4,5},{5,6},{6,7},{8,9},{9,10},{10,11},{12,13},{... | collective-permute-start | bytes 55304 | tf_op jit(solution)/shard_map/ppermute | solution.py:17
  79.8 2.9 fusion.66
  84.6 10.3 %collective-permute-start.13 = (f32[1,64,256]{2,1,0:T(8,128)S(1)}, f32[1,64,256]{2,1,0:T(8,128)S(1)}, u32[]{:S(2)}, u32[]{:S(2)}) collective-permute-start(f32[1,64,256]{2,1,0:T(8,128)S(1)} %get-tuple-element.56), channel_id=1, source_target_pairs={{0,4},{4,8},{8,12},{12,16},{16,20},{20,24},{24,28},{28,32},{32,36}... | collective-permute-start | bytes 196616 | tf_op jit(solution)/shard_map/ppermute | solution.py:17
  98.3 4.7 %collective-permute-start.15 = (f32[18,1,256]{2,1,0:T(1,128)S(1)}, f32[18,1,256]{2,1,0:T(1,128)S(1)}, u32[]{:S(2)}, u32[]{:S(2)}) collective-permute-start(f32[18,1,256]{2,1,0:T(1,128)S(1)} %get-tuple-element.17), channel_id=1, source_target_pairs={{0,1},{1,2},{2,3},{4,5},{5,6},{6,7},{8,9},{9,10},{10,11},{12,13},{... | collective-permute-start | bytes 55304 | tf_op jit(solution)/shard_map/ppermute | solution.py:17
  104.2 2.9 fusion.58
  109.0 10.3 %collective-permute-start.17 = (f32[1,64,256]{2,1,0:T(8,128)S(1)}, f32[1,64,256]{2,1,0:T(8,128)S(1)}, u32[]{:S(2)}, u32[]{:S(2)}) collective-permute-start(f32[1,64,256]{2,1,0:T(8,128)S(1)} %get-tuple-element.52), channel_id=1, source_target_pairs={{0,4},{4,8},{8,12},{12,16},{16,20},{20,24},{24,28},{28,32},{32,36}... | collective-permute-start | bytes 196616 | tf_op jit(solution)/shard_map/ppermute | solution.py:17
  122.6 4.7 %collective-permute-start.19 = (f32[18,1,256]{2,1,0:T(1,128)S(1)}, f32[18,1,256]{2,1,0:T(1,128)S(1)}, u32[]{:S(2)}, u32[]{:S(2)}) collective-permute-start(f32[18,1,256]{2,1,0:T(1,128)S(1)} %get-tuple-element.15), channel_id=1, source_target_pairs={{0,1},{1,2},{2,3},{4,5},{5,6},{6,7},{8,9},{9,10},{10,11},{12,13},{... | collective-permute-start | bytes 55304 | tf_op jit(solution)/shard_map/ppermute | solution.py:17
  129.1 2.9 fusion.50
  133.9 10.3 %collective-permute-start.21 = (f32[1,64,256]{2,1,0:T(8,128)S(1)}, f32[1,64,256]{2,1,0:T(8,128)S(1)}, u32[]{:S(2)}, u32[]{:S(2)}) collective-permute-start(f32[1,64,256]{2,1,0:T(8,128)S(1)} %get-tuple-element.48), channel_id=1, source_target_pairs={{0,4},{4,8},{8,12},{12,16},{16,20},{20,24},{24,28},{28,32},{32,36}... | collective-permute-start | bytes 196616 | tf_op jit(solution)/shard_map/ppermute | solution.py:17
  147.5 4.1 collective-permute-start.23
  153.5 2.9 fusion.42
  158.3 10.3 %collective-permute-start.25 = (f32[1,64,256]{2,1,0:T(8,128)S(1)}, f32[1,64,256]{2,1,0:T(8,128)S(1)}, u32[]{:S(2)}, u32[]{:S(2)}) collective-permute-start(f32[1,64,256]{2,1,0:T(8,128)S(1)} %get-tuple-element.44), channel_id=1, source_target_pairs={{0,4},{4,8},{8,12},{12,16},{16,20},{20,24},{24,28},{28,32},{32,36}... | collective-permute-start | bytes 196616 | tf_op jit(solution)/shard_map/ppermute | solution.py:17
  171.9 4.1 collective-permute-start.27
  182.6 10.3 %collective-permute-start.29 = (f32[1,64,256]{2,1,0:T(8,128)S(1)}, f32[1,64,256]{2,1,0:T(8,128)S(1)}, u32[]{:S(2)}, u32[]{:S(2)}) collective-permute-start(f32[1,64,256]{2,1,0:T(8,128)S(1)} %get-tuple-element.40), channel_id=1, source_target_pairs={{0,4},{4,8},{8,12},{12,16},{16,20},{20,24},{24,28},{28,32},{32,36}... | collective-permute-start | bytes 196616 | tf_op jit(solution)/shard_map/ppermute | solution.py:17
  196.2 4.1 collective-permute-start.31
  212.4 186.9 %all-gather.2.cloned.1.call-done = f32[8,65536]{0,1:T(8,128)} async-done(((f32[8,1024]{0,1:T(8,128)}), f32[8,65536]{0,1:T(8,128)}) %all-gather.2.cloned.1.call-update) | async-done | bytes 2097168 | tf_op jit(solution)/shard_map/all_gather | solution.py:73
  399.4 11.6 %gather_fusion = f32[512,8]{1,0:T(8,128)S(1)} fusion(f32[8,65536]{0,1:T(8,128)} %all-gather.2.cloned.1.call-done, s32[1024]{0:T(1024)S(1)} %pad_clamp_fusion), kind=kCustom, calls=%fused_computation | custom fusion | bytes 34816 | tf_op jit(solution)/shard_map/jit(_take)/gather | solution.py:74
  412.9 3.2 fusion.16
  421.4 3.0 fusion.18
  425.6 3.3 fusion.117
  430.2 3.2 fusion.19
  435.5 3.5 fusion.116
  440.9 3.8 fusion.20
  447.4 4.1 fusion.2
  (180 shorter events, 84.2 us)
Async XLA Ops:
  7.2 392.2 %all-gather.2.cloned.1.call-start = ((), (), s32[]{:S(2)}) async-start(), calls=%async_computation | async-start | bytes 34078720 | tf_op jit(solution)/shard_map/all_gather | solution.py:73
  8.2 7.8 %collective-permute-start.1 = (f32[1,64,256]{2,1,0:T(8,128)S(1)}, f32[1,64,256]{2,1,0:T(8,128)S(1)}, u32[]{:S(2)}, u32[]{:S(2)}) collective-permute-start(f32[1,64,256]{2,1,0:T(8,128)S(1)} %get-tuple-element.69), channel_id=1, source_target_pairs={{0,4},{4,8},{8,12},{12,16},{16,20},{20,24},{24,28},{28,32},{32,36}... | collective-permute-start | bytes 196616 | tf_op jit(solution)/shard_map/ppermute | solution.py:17
  13.9 11.9 %collective-permute-start = (f32[1,64,256]{2,1,0:T(8,128)S(1)}, f32[1,64,256]{2,1,0:T(8,128)S(1)}, u32[]{:S(2)}, u32[]{:S(2)}) collective-permute-start(f32[1,64,256]{2,1,0:T(8,128)S(1)} %get-tuple-element.68), channel_id=1, source_target_pairs={{4,0},{8,4},{12,8},{16,12},{20,16},{24,20},{28,24},{32,28},{36,32}... | collective-permute-start | bytes 196616 | tf_op jit(solution)/shard_map/ppermute | solution.py:20
  25.9 6.7 %collective-permute-start.2 = (f32[18,1,256]{2,1,0:T(1,128)S(1)}, f32[18,1,256]{2,1,0:T(1,128)S(1)}, u32[]{:S(2)}, u32[]{:S(2)}) collective-permute-start(f32[18,1,256]{2,1,0:T(1,128)S(1)} %get-tuple-element.22), channel_id=1, source_target_pairs={{1,0},{2,1},{3,2},{5,4},{6,5},{7,6},{9,8},{10,9},{11,10},{13,12},{... | collective-permute-start | bytes 55304 | tf_op jit(solution)/shard_map/ppermute | solution.py:20
  34.3 13.0 %collective-permute-start.4 = (f32[1,64,256]{2,1,0:T(8,128)S(1)}, f32[1,64,256]{2,1,0:T(8,128)S(1)}, u32[]{:S(2)}, u32[]{:S(2)}) collective-permute-start(f32[1,64,256]{2,1,0:T(8,128)S(1)} %get-tuple-element.65), channel_id=1, source_target_pairs={{4,0},{8,4},{12,8},{16,12},{20,16},{24,20},{28,24},{32,28},{36,32}... | collective-permute-start | bytes 196616 | tf_op jit(solution)/shard_map/ppermute | solution.py:20
  36.2 11.0 %collective-permute-start.5 = (f32[1,64,256]{2,1,0:T(8,128)S(1)}, f32[1,64,256]{2,1,0:T(8,128)S(1)}, u32[]{:S(2)}, u32[]{:S(2)}) collective-permute-start(f32[1,64,256]{2,1,0:T(8,128)S(1)} %get-tuple-element.64), channel_id=1, source_target_pairs={{0,4},{4,8},{8,12},{12,16},{16,20},{20,24},{24,28},{28,32},{32,36}... | collective-permute-start | bytes 196616 | tf_op jit(solution)/shard_map/ppermute | solution.py:17
  47.3 8.2 %collective-permute-start.6 = (f32[18,1,256]{2,1,0:T(1,128)S(1)}, f32[18,1,256]{2,1,0:T(1,128)S(1)}, u32[]{:S(2)}, u32[]{:S(2)}) collective-permute-start(f32[18,1,256]{2,1,0:T(1,128)S(1)} %get-tuple-element.20), channel_id=1, source_target_pairs={{1,0},{2,1},{3,2},{5,4},{6,5},{7,6},{9,8},{10,9},{11,10},{13,12},{... | collective-permute-start | bytes 55304 | tf_op jit(solution)/shard_map/ppermute | solution.py:20
  50.5 5.0 %collective-permute-start.7 = (f32[18,1,256]{2,1,0:T(1,128)S(1)}, f32[18,1,256]{2,1,0:T(1,128)S(1)}, u32[]{:S(2)}, u32[]{:S(2)}) collective-permute-start(f32[18,1,256]{2,1,0:T(1,128)S(1)} %get-tuple-element.21), channel_id=1, source_target_pairs={{0,1},{1,2},{2,3},{4,5},{5,6},{6,7},{8,9},{9,10},{10,11},{12,13},{... | collective-permute-start | bytes 55304 | tf_op jit(solution)/shard_map/ppermute | solution.py:17
  58.4 13.6 %collective-permute-start.8 = (f32[1,64,256]{2,1,0:T(8,128)S(1)}, f32[1,64,256]{2,1,0:T(8,128)S(1)}, u32[]{:S(2)}, u32[]{:S(2)}) collective-permute-start(f32[1,64,256]{2,1,0:T(8,128)S(1)} %get-tuple-element.61), channel_id=1, source_target_pairs={{4,0},{8,4},{12,8},{16,12},{20,16},{24,20},{28,24},{32,28},{36,32}... | collective-permute-start | bytes 196616 | tf_op jit(solution)/shard_map/ppermute | solution.py:20
  60.3 11.7 %collective-permute-start.9 = (f32[1,64,256]{2,1,0:T(8,128)S(1)}, f32[1,64,256]{2,1,0:T(8,128)S(1)}, u32[]{:S(2)}, u32[]{:S(2)}) collective-permute-start(f32[1,64,256]{2,1,0:T(8,128)S(1)} %get-tuple-element.60), channel_id=1, source_target_pairs={{0,4},{4,8},{8,12},{12,16},{16,20},{20,24},{24,28},{28,32},{32,36}... | collective-permute-start | bytes 196616 | tf_op jit(solution)/shard_map/ppermute | solution.py:17
  72.0 7.8 %collective-permute-start.10 = (f32[18,1,256]{2,1,0:T(1,128)S(1)}, f32[18,1,256]{2,1,0:T(1,128)S(1)}, u32[]{:S(2)}, u32[]{:S(2)}) collective-permute-start(f32[18,1,256]{2,1,0:T(1,128)S(1)} %get-tuple-element.18), channel_id=1, source_target_pairs={{1,0},{2,1},{3,2},{5,4},{6,5},{7,6},{9,8},{10,9},{11,10},{13,12},{... | collective-permute-start | bytes 55304 | tf_op jit(solution)/shard_map/ppermute | solution.py:20
  73.9 5.9 %collective-permute-start.11 = (f32[18,1,256]{2,1,0:T(1,128)S(1)}, f32[18,1,256]{2,1,0:T(1,128)S(1)}, u32[]{:S(2)}, u32[]{:S(2)}) collective-permute-start(f32[18,1,256]{2,1,0:T(1,128)S(1)} %get-tuple-element.19), channel_id=1, source_target_pairs={{0,1},{1,2},{2,3},{4,5},{5,6},{6,7},{8,9},{9,10},{10,11},{12,13},{... | collective-permute-start | bytes 55304 | tf_op jit(solution)/shard_map/ppermute | solution.py:17
  82.7 13.6 %collective-permute-start.12 = (f32[1,64,256]{2,1,0:T(8,128)S(1)}, f32[1,64,256]{2,1,0:T(8,128)S(1)}, u32[]{:S(2)}, u32[]{:S(2)}) collective-permute-start(f32[1,64,256]{2,1,0:T(8,128)S(1)} %get-tuple-element.57), channel_id=1, source_target_pairs={{4,0},{8,4},{12,8},{16,12},{20,16},{24,20},{28,24},{32,28},{36,32}... | collective-permute-start | bytes 196616 | tf_op jit(solution)/shard_map/ppermute | solution.py:20
  84.6 11.7 %collective-permute-start.13 = (f32[1,64,256]{2,1,0:T(8,128)S(1)}, f32[1,64,256]{2,1,0:T(8,128)S(1)}, u32[]{:S(2)}, u32[]{:S(2)}) collective-permute-start(f32[1,64,256]{2,1,0:T(8,128)S(1)} %get-tuple-element.56), channel_id=1, source_target_pairs={{0,4},{4,8},{8,12},{12,16},{16,20},{20,24},{24,28},{28,32},{32,36}... | collective-permute-start | bytes 196616 | tf_op jit(solution)/shard_map/ppermute | solution.py:17
  96.3 7.8 %collective-permute-start.14 = (f32[18,1,256]{2,1,0:T(1,128)S(1)}, f32[18,1,256]{2,1,0:T(1,128)S(1)}, u32[]{:S(2)}, u32[]{:S(2)}) collective-permute-start(f32[18,1,256]{2,1,0:T(1,128)S(1)} %get-tuple-element.16), channel_id=1, source_target_pairs={{1,0},{2,1},{3,2},{5,4},{6,5},{7,6},{9,8},{10,9},{11,10},{13,12},{... | collective-permute-start | bytes 55304 | tf_op jit(solution)/shard_map/ppermute | solution.py:20
  98.3 5.9 %collective-permute-start.15 = (f32[18,1,256]{2,1,0:T(1,128)S(1)}, f32[18,1,256]{2,1,0:T(1,128)S(1)}, u32[]{:S(2)}, u32[]{:S(2)}) collective-permute-start(f32[18,1,256]{2,1,0:T(1,128)S(1)} %get-tuple-element.17), channel_id=1, source_target_pairs={{0,1},{1,2},{2,3},{4,5},{5,6},{6,7},{8,9},{9,10},{10,11},{12,13},{... | collective-permute-start | bytes 55304 | tf_op jit(solution)/shard_map/ppermute | solution.py:17
  107.1 13.6 %collective-permute-start.16 = (f32[1,64,256]{2,1,0:T(8,128)S(1)}, f32[1,64,256]{2,1,0:T(8,128)S(1)}, u32[]{:S(2)}, u32[]{:S(2)}) collective-permute-start(f32[1,64,256]{2,1,0:T(8,128)S(1)} %get-tuple-element.53), channel_id=1, source_target_pairs={{4,0},{8,4},{12,8},{16,12},{20,16},{24,20},{28,24},{32,28},{36,32}... | collective-permute-start | bytes 196616 | tf_op jit(solution)/shard_map/ppermute | solution.py:20
  109.0 11.7 %collective-permute-start.17 = (f32[1,64,256]{2,1,0:T(8,128)S(1)}, f32[1,64,256]{2,1,0:T(8,128)S(1)}, u32[]{:S(2)}, u32[]{:S(2)}) collective-permute-start(f32[1,64,256]{2,1,0:T(8,128)S(1)} %get-tuple-element.52), channel_id=1, source_target_pairs={{0,4},{4,8},{8,12},{12,16},{16,20},{20,24},{24,28},{28,32},{32,36}... | collective-permute-start | bytes 196616 | tf_op jit(solution)/shard_map/ppermute | solution.py:17
  120.7 8.4 %collective-permute-start.18 = (f32[18,1,256]{2,1,0:T(1,128)S(1)}, f32[18,1,256]{2,1,0:T(1,128)S(1)}, u32[]{:S(2)}, u32[]{:S(2)}) collective-permute-start(f32[18,1,256]{2,1,0:T(1,128)S(1)} %get-tuple-element.14), channel_id=1, source_target_pairs={{1,0},{2,1},{3,2},{5,4},{6,5},{7,6},{9,8},{10,9},{11,10},{13,12},{... | collective-permute-start | bytes 55304 | tf_op jit(solution)/shard_map/ppermute | solution.py:20
  122.6 6.5 %collective-permute-start.19 = (f32[18,1,256]{2,1,0:T(1,128)S(1)}, f32[18,1,256]{2,1,0:T(1,128)S(1)}, u32[]{:S(2)}, u32[]{:S(2)}) collective-permute-start(f32[18,1,256]{2,1,0:T(1,128)S(1)} %get-tuple-element.15), channel_id=1, source_target_pairs={{0,1},{1,2},{2,3},{4,5},{5,6},{6,7},{8,9},{9,10},{10,11},{12,13},{... | collective-permute-start | bytes 55304 | tf_op jit(solution)/shard_map/ppermute | solution.py:17
  132.0 13.6 %collective-permute-start.20 = (f32[1,64,256]{2,1,0:T(8,128)S(1)}, f32[1,64,256]{2,1,0:T(8,128)S(1)}, u32[]{:S(2)}, u32[]{:S(2)}) collective-permute-start(f32[1,64,256]{2,1,0:T(8,128)S(1)} %get-tuple-element.49), channel_id=1, source_target_pairs={{4,0},{8,4},{12,8},{16,12},{20,16},{24,20},{28,24},{32,28},{36,32}... | collective-permute-start | bytes 196616 | tf_op jit(solution)/shard_map/ppermute | solution.py:20
  133.9 11.7 %collective-permute-start.21 = (f32[1,64,256]{2,1,0:T(8,128)S(1)}, f32[1,64,256]{2,1,0:T(8,128)S(1)}, u32[]{:S(2)}, u32[]{:S(2)}) collective-permute-start(f32[1,64,256]{2,1,0:T(8,128)S(1)} %get-tuple-element.48), channel_id=1, source_target_pairs={{0,4},{4,8},{8,12},{12,16},{16,20},{20,24},{24,28},{28,32},{32,36}... | collective-permute-start | bytes 196616 | tf_op jit(solution)/shard_map/ppermute | solution.py:17
  145.6 7.8 %collective-permute-start.22 = (f32[18,1,256]{2,1,0:T(1,128)S(1)}, f32[18,1,256]{2,1,0:T(1,128)S(1)}, u32[]{:S(2)}, u32[]{:S(2)}) collective-permute-start(f32[18,1,256]{2,1,0:T(1,128)S(1)} %get-tuple-element.12), channel_id=1, source_target_pairs={{1,0},{2,1},{3,2},{5,4},{6,5},{7,6},{9,8},{10,9},{11,10},{13,12},{... | collective-permute-start | bytes 55304 | tf_op jit(solution)/shard_map/ppermute | solution.py:20
  147.5 5.9 %collective-permute-start.23 = (f32[18,1,256]{2,1,0:T(1,128)S(1)}, f32[18,1,256]{2,1,0:T(1,128)S(1)}, u32[]{:S(2)}, u32[]{:S(2)}) collective-permute-start(f32[18,1,256]{2,1,0:T(1,128)S(1)} %get-tuple-element.13), channel_id=1, source_target_pairs={{0,1},{1,2},{2,3},{4,5},{5,6},{6,7},{8,9},{9,10},{10,11},{12,13},{... | collective-permute-start | bytes 55304 | tf_op jit(solution)/shard_map/ppermute | solution.py:17
  156.3 13.6 %collective-permute-start.24 = (f32[1,64,256]{2,1,0:T(8,128)S(1)}, f32[1,64,256]{2,1,0:T(8,128)S(1)}, u32[]{:S(2)}, u32[]{:S(2)}) collective-permute-start(f32[1,64,256]{2,1,0:T(8,128)S(1)} %get-tuple-element.45), channel_id=1, source_target_pairs={{4,0},{8,4},{12,8},{16,12},{20,16},{24,20},{28,24},{32,28},{36,32}... | collective-permute-start | bytes 196616 | tf_op jit(solution)/shard_map/ppermute | solution.py:20
  158.3 11.7 %collective-permute-start.25 = (f32[1,64,256]{2,1,0:T(8,128)S(1)}, f32[1,64,256]{2,1,0:T(8,128)S(1)}, u32[]{:S(2)}, u32[]{:S(2)}) collective-permute-start(f32[1,64,256]{2,1,0:T(8,128)S(1)} %get-tuple-element.44), channel_id=1, source_target_pairs={{0,4},{4,8},{8,12},{12,16},{16,20},{20,24},{24,28},{28,32},{32,36}... | collective-permute-start | bytes 196616 | tf_op jit(solution)/shard_map/ppermute | solution.py:17
  170.0 7.8 %collective-permute-start.26 = (f32[18,1,256]{2,1,0:T(1,128)S(1)}, f32[18,1,256]{2,1,0:T(1,128)S(1)}, u32[]{:S(2)}, u32[]{:S(2)}) collective-permute-start(f32[18,1,256]{2,1,0:T(1,128)S(1)} %get-tuple-element.10), channel_id=1, source_target_pairs={{1,0},{2,1},{3,2},{5,4},{6,5},{7,6},{9,8},{10,9},{11,10},{13,12},{... | collective-permute-start | bytes 55304 | tf_op jit(solution)/shard_map/ppermute | solution.py:20
  171.9 5.9 %collective-permute-start.27 = (f32[18,1,256]{2,1,0:T(1,128)S(1)}, f32[18,1,256]{2,1,0:T(1,128)S(1)}, u32[]{:S(2)}, u32[]{:S(2)}) collective-permute-start(f32[18,1,256]{2,1,0:T(1,128)S(1)} %get-tuple-element.11), channel_id=1, source_target_pairs={{0,1},{1,2},{2,3},{4,5},{5,6},{6,7},{8,9},{9,10},{10,11},{12,13},{... | collective-permute-start | bytes 55304 | tf_op jit(solution)/shard_map/ppermute | solution.py:17
  180.7 12.6 %collective-permute-start.28 = (f32[1,64,256]{2,1,0:T(8,128)S(1)}, f32[1,64,256]{2,1,0:T(8,128)S(1)}, u32[]{:S(2)}, u32[]{:S(2)}) collective-permute-start(f32[1,64,256]{2,1,0:T(8,128)S(1)} %get-tuple-element.41), channel_id=1, source_target_pairs={{4,0},{8,4},{12,8},{16,12},{20,16},{24,20},{28,24},{32,28},{36,32}... | collective-permute-start | bytes 196616 | tf_op jit(solution)/shard_map/ppermute | solution.py:20
  182.6 11.6 %collective-permute-start.29 = (f32[1,64,256]{2,1,0:T(8,128)S(1)}, f32[1,64,256]{2,1,0:T(8,128)S(1)}, u32[]{:S(2)}, u32[]{:S(2)}) collective-permute-start(f32[1,64,256]{2,1,0:T(8,128)S(1)} %get-tuple-element.40), channel_id=1, source_target_pairs={{0,4},{4,8},{8,12},{12,16},{16,20},{20,24},{24,28},{28,32},{32,36}... | collective-permute-start | bytes 196616 | tf_op jit(solution)/shard_map/ppermute | solution.py:17
  194.3 7.8 %collective-permute-start.30 = (f32[18,1,256]{2,1,0:T(1,128)S(1)}, f32[18,1,256]{2,1,0:T(1,128)S(1)}, u32[]{:S(2)}, u32[]{:S(2)}) collective-permute-start(f32[18,1,256]{2,1,0:T(1,128)S(1)} %get-tuple-element.8), channel_id=1, source_target_pairs={{1,0},{2,1},{3,2},{5,4},{6,5},{7,6},{9,8},{10,9},{11,10},{13,12},{... | collective-permute-start | bytes 55304 | tf_op jit(solution)/shard_map/ppermute | solution.py:20
  196.2 5.9 %collective-permute-start.31 = (f32[18,1,256]{2,1,0:T(1,128)S(1)}, f32[18,1,256]{2,1,0:T(1,128)S(1)}, u32[]{:S(2)}, u32[]{:S(2)}) collective-permute-start(f32[18,1,256]{2,1,0:T(1,128)S(1)} %get-tuple-element.9), channel_id=1, source_target_pairs={{0,1},{1,2},{2,3},{4,5},{5,6},{6,7},{8,9},{9,10},{10,11},{12,13},{... | collective-permute-start | bytes 55304 | tf_op jit(solution)/shard_map/ppermute | solution.py:17
  (23 other events, 614.9 us)
Sparse Core Ops, SparseCore 0:
  208.8 190.5 all-gather.1
where the time goes:
time: 463 us; the launch traced here: 459 us
  waiting for transfers between devices  197 us (43%)
  starting transfers between devices  144 us (31%)
  other arithmetic  51.1 us (11%)
  local copies, waits for them, and re-layouts  47.6 us (10%)
  between operations  14.9 us (3%)
    all_gather x1, waiting for transfers between devices, shards(): lax.all_gather(jnp.stack(planes), ('gx', 'gy'), axis=1, tiled=True)  187 us
    ppermute x16, starting transfers between devices, extended(): lax.ppermute(lax.slice_in_dim(block, block.shape[dim] - width, None, axis...  109 us
    ppermute x16, starting transfers between devices, extended(): lax.ppermute(lax.slice_in_dim(block, 0, width, axis=dim), axis, backward)  34.3 us
    reduce_sum x7, other arithmetic, shards(): stress = jnp.sum(springs, axis=0)  23.6 us
    add x8, other arithmetic, shards(): following = 2.0 * current - former + reg_coef * laplace_rim(padded, current)  20.7 us
    gather x1, local copies, waits for them, and re-layouts, shards(): base = jnp.take(gathered, blocked, axis=1)  11.6 us
    slice x17, local copies, waits for them, and re-layouts, shards(): lower = jnp.concatenate([advance_displace[1:], base[step][None]], axis=0)  10.1 us
  transfers between devices with their start and end apart: 33, of which 5 were waited for; matrix products, arithmetic and copies ran while one was open for 5% of the time, Pallas kernels for 0%

commit v1 on v0

v1 whole, which is shorter than its diff:
```python
import functools
import jax
import jax.numpy as jnp
from jax import lax
from jax.experimental import pallas as pl
from jax.experimental.pallas import tpu as pltpu
from jax.sharding import PartitionSpec as P

STEPS = 8
HALO = 8
FDEP = 64
stress_rate = 0.5
XAX = ("sec", "gx")
F32 = jnp.float32
ANY = pl.BlockSpec(memory_space=pl.ANY)
VM = pl.BlockSpec(memory_space=pltpu.VMEM)
SM = pl.BlockSpec(memory_space=pltpu.SMEM)
PARAMS = pltpu.CompilerParams(vmem_limit_bytes=48 * 1024 * 1024)


def sds(*shape):
    return jax.ShapeDtypeStruct(shape, F32)


def x_edges():
    at = lax.axis_index("sec") * lax.axis_size("gx") + lax.axis_index("gx")
    return at == 0, at == lax.axis_size("sec") * lax.axis_size("gx") - 1


def y_edges():
    at = lax.axis_index("gy")
    return at == 0, at == lax.axis_size("gy") - 1


def lanes(shape):
    return lax.broadcasted_iota(jnp.int32, shape, len(shape) - 1)


def band_kernel(u, p, c, band, to_right, to_left):
    lane = lanes((64, 128))
    for x in range(8):
        halves = []
        for row in (x, x + 8):
            halves.append(
                jnp.where(
                    lane < 73,
                    u[row],
                    jnp.where(lane < 88, pltpu.roll(p[row], 16, 1), pltpu.roll(c[row], 31, 1)),
                )
            )
        turned = jnp.concatenate(halves, axis=0).T
        band[:, x, :] = turned[56:104]
    first = lanes((8, 128)) < 64
    for k in range(24):
        a, b = band[k], band[k + 24]
        ra, rb = pltpu.roll(a, 64, 1), pltpu.roll(b, 64, 1)
        to_right[k] = jnp.where(first, ra, b)
        to_left[k] = jnp.where(first, a, rb)


def band_edges_kernel(band, from_left, from_right, ext, send_a, send_b):
    low_edge, high_edge = x_edges()
    even = lax.rem(lax.axis_index("gy"), 2) == 0
    lane = lanes((8, 128))
    first = lane < 64
    group = lanes((32, 128)) // 8
    for g in range(3):
        high = jnp.zeros((32, 128), F32)
        low = jnp.zeros((32, 128), F32)
        for q in range(16):
            level = g * 16 + q
            own = band[level]
            near = from_right[level % 24]
            far = from_left[level % 24]
            if level >= 24:
                near, far = pltpu.roll(near, 64, 1), pltpu.roll(far, 64, 1)
            near = jnp.where(high_edge, 0.0, near)
            far = jnp.where(low_edge, 0.0, far)
            full = jnp.concatenate([own, pltpu.roll(own, 64, 1), near, far], axis=0)
            ext[level] = full
            high = jnp.where(group == q, pltpu.roll(full, (q * 8 - 56) % 128, 1), high)
            low = jnp.where(group == q, pltpu.roll(full, q * 8, 1), low)
        send_a[g] = jnp.where(even, high, low)
        send_b[g] = jnp.where(even, low, high)


def band_steps_kernel(ext, recv_a, recv_b, trace, one, two, coef):
    low_edge, high_edge = y_edges()
    even = lax.rem(lax.axis_index("gy"), 2) == 0
    lane = lanes((32, 128))
    for g in range(3):
        a, b = recv_a[g], recv_b[g]
        high = jnp.where(high_edge, 0.0, jnp.where(even, a, b))
        low = jnp.where(low_edge, 0.0, jnp.where(even, b, a))
        for q in range(16):
            level = g * 16 + q
            if level > 46:
                continue
            full = jnp.where(
                lane < 64,
                ext[level],
                jnp.where(
                    lane < 72,
                    pltpu.roll(high, (64 - q * 8) % 128, 1),
                    jnp.where(lane >= 120, pltpu.roll(low, (120 - q * 8) % 128, 1), 0.0),
                ),
            )
            if level < 17:
                one[level] = full
            elif level < 32:
                two[level - 16] = full
            else:
                coef[level - 31] = full
    first = lanes((8, 128)) < 64
    now, old = one, two
    for step in range(1, STEPS + 1):
        for j in range(step, 17 - step):
            u = now[j]
            beside = pltpu.roll(u, 1, 0) + pltpu.roll(u, 31, 0) + pltpu.roll(u, 1, 1) + pltpu.roll(u, 127, 1)
            lap = beside + now[j - 1] + now[j + 1] - 6.0 * u
            old[j] = 2.0 * u - old[j] + coef[j] * lap
        now, old = old, now
        plane = now[8]
        trace[:, step - 1, :] = jnp.where(first, plane[0:8], pltpu.roll(plane[8:16], 64, 1))


def pick_kernel(table, index, out):
    me = lax.axis_index("gx")

    def tile(t, carry):
        cell = jnp.broadcast_to(index[pl.ds(t, 1), :], (8, 128))
        x, y = cell >> 8, cell & 255
        place = ((y >> 6) << 3) + (x & 7)
        place = jnp.where((x >> 4) == me, place, -1)
        lane = (((x >> 3) & 1) << 6) + (y & 63)
        acc = jnp.zeros((8, 128), F32)
        for k in range(32):
            acc = jnp.where(place == k, jnp.take_along_axis(table[k], lane, axis=1), acc)
        out[t] = acc
        return carry

    lax.fori_loop(0, index.shape[0], tile, 0)


def spring_values(cls, k, count, modulus, yields):
    mod = jnp.zeros(cls.shape, F32)
    lim = jnp.zeros(cls.shape, F32)
    for c in range(8):
        hit = cls == c
        mod = jnp.where(hit, modulus[c, k], mod)
        lim = jnp.where(hit, jnp.where(k < count[c], yields[c, k], 0.0), lim)
    return mod, lim


def columns_kernel(count, modulus, yields, soil, start, out, edge, mods, lims, springs):
    def rows(r, carry):
        at = pl.ds(pl.multiple_of(r * 8, 8), 8)
        cls = soil[at, :]
        for k in range(16):
            mod, lim = spring_values(cls, k, count, modulus, yields)
            mods[k, at, :] = mod
            lims[k, at, :] = lim
            springs[k, at, :] = jnp.zeros((8, 128), F32)
        return carry

    lax.fori_loop(0, 8, rows, 0)
    row = lax.broadcasted_iota(jnp.int32, (64, 128), 0)

    def step(s, state):
        disp, vel, old = state
        strain = pltpu.roll(disp, 63, 0) - disp
        inc = strain - old
        stress = jnp.zeros((64, 128), F32)
        for k in range(16):
            lim = lims[k]
            value = jnp.minimum(jnp.maximum(springs[k] + mods[k] * inc, -lim), lim)
            springs[k] = value
            stress = stress + value
        edge[pl.ds(s, 1), :] = stress[55:56]
        above = jnp.where(row == 0, 0.0, pltpu.roll(stress, 1, 0))
        vel = vel + stress_rate * (stress - above)
        return disp + vel, vel, strain

    zero = jnp.zeros((64, 128), F32)
    out[...] = lax.fori_loop(0, STEPS, step, (start[...], zero, zero))[0]


def last_rows_kernel(count, modulus, yields, soil, start, edge, arrived, done, out):
    del done
    row = lax.broadcasted_iota(jnp.int32, (8, 128), 0)
    for t in range(4):
        cols = slice(t * 128, (t + 1) * 128)
        base = arrived[0, t * 8 : t * 8 + 8]
        for source in range(1, arrived.shape[0]):
            base = base + arrived[source, t * 8 : t * 8 + 8]
        cls = soil[:, cols]
        pairs = [spring_values(cls, k, count, modulus, yields) for k in range(16)]
        springs = [jnp.zeros((8, 128), F32) for _ in range(16)]
        disp = start[:, cols]
        vel = jnp.zeros((8, 128), F32)
        old = jnp.zeros((8, 128), F32)
        for s in range(STEPS):
            strain = jnp.where(row == 7, base[s : s + 1], pltpu.roll(disp, 7, 0)) - disp
            inc = strain - old
            old = strain
            for k in range(16):
                mod, lim = pairs[k]
                springs[k] = jnp.minimum(jnp.maximum(springs[k] + mod * inc, -lim), lim)
            sums = springs
            while len(sums) > 1:
                sums = [sums[i] + sums[i + 1] for i in range(0, len(sums), 2)]
            stress = sums[0]
            above = jnp.where(row == 0, edge[s : s + 1, cols], pltpu.roll(stress, 1, 0))
            vel = vel + stress_rate * (stress - above)
            disp = disp + vel
        out[:, cols] = disp


RIGHT = ((8, 8, 0), (9, 7, 8), (9, 7, 15))
LEFT = ((0, 8, 0), (0, 7, 8), (0, 7, 15))


def run_copies(pairs, sems):
    copies = [pltpu.make_async_copy(src, dst, sems.at[n]) for n, (src, dst) in enumerate(pairs)]
    for copy in copies:
        copy.start()
    for copy in copies:
        copy.wait()


def pack_x_kernel(u, p, c, edge_right, edge_left, mid_right, mid_left, sems):
    pairs = []
    for plan, edge, mid in ((RIGHT, edge_right, mid_right), (LEFT, edge_left, mid_left)):
        for ref, (x0, n, at) in zip((u, p, c), plan):
            pairs.append((ref.at[x0 : x0 + n, 0:8, :], edge.at[at : at + n, 0:8, :]))
            pairs.append((ref.at[x0 : x0 + n, 56:64, :], edge.at[at : at + n, 8:16, :]))
            pairs.append((ref.at[x0 : x0 + n, 8:56, :], mid.at[at : at + n, :, :]))
    run_copies(pairs, sems)


def pack_y_kernel(u, p, c, from_left, from_right, send_a, send_b, sems):
    odd = lax.rem(lax.axis_index("gy"), 2)
    pairs = []
    for send, side in ((send_a, 1 - odd), (send_b, odd)):
        own = pl.ds(pl.multiple_of(side * 56, 8), 8)
        corner = pl.ds(pl.multiple_of(side * 8, 8), 8)
        for n, ref in enumerate((u, p, c)):
            pairs.append((ref.at[:, own, :], send.at[16 * n : 16 * n + 16]))
        pairs.append((from_left.at[:, corner, :], send.at[48:70]))
        pairs.append((from_right.at[:, corner, :], send.at[70:92]))
    run_copies(pairs, sems)


def region_kernel(u, p, c, el, er, ml, mr, ya, yb, out, one, two, coef, sems):
    low_x, high_x = x_edges()
    low_y, high_y = y_edges()
    even = lax.rem(lax.axis_index("gy"), 2) == 0
    bufs = (one, two, coef)
    always = jnp.bool_(True)
    jobs = []

    def job(cond, src, dst):
        jobs.append((cond, pltpu.make_async_copy(src, dst, sems.at[len(jobs)])))

    for ref, buf in zip((u, p, c), bufs):
        job(None, ref, buf.at[0:16, 16:80, :])
    left_at = ((24, 8, 0), (25, 7, 8), (25, 7, 15))
    right_at = ((16, 8, 0), (16, 7, 8), (16, 7, 15))
    for cond, plan, edge, mid in ((~low_x, left_at, el, ml), (~high_x, right_at, er, mr)):
        for buf, (x0, n, at) in zip(bufs, plan):
            job(cond, mid.at[at : at + n], buf.at[x0 : x0 + n, 24:72, :])
            job(cond, edge.at[at : at + n, 0:8, :], buf.at[x0 : x0 + n, 16:24, :])
            job(cond, edge.at[at : at + n, 8:16, :], buf.at[x0 : x0 + n, 72:80, :])
    for msg, is_high in ((ya, even), (yb, ~even)):
        for rows, cond in (((80, 88), is_high & ~high_y), ((8, 16), ~is_high & ~low_y)):
            for n, buf in enumerate(bufs):
                job(cond, msg.at[16 * n : 16 * n + 16], buf.at[0:16, rows[0] : rows[1], :])
            for more, plan, base in ((~low_x, left_at, 48), (~high_x, right_at, 70)):
                for buf, (x0, n, at) in zip(bufs, plan):
                    job(
                        cond & more,
                        msg.at[base + at : base + at + n],
                        buf.at[x0 : x0 + n, rows[0] : rows[1], :],
                    )
    for cond, copy in jobs:
        if cond is None:
            copy.start()
        else:
            pl.when(cond)(copy.start)
    for edge, x0, n, y0, m in (
        (low_x, 24, 8, 8, 80),
        (high_x, 16, 8, 8, 80),
        (low_y, 0, 32, 8, 8),
        (high_y, 0, 32, 80, 8),
    ):

        @pl.when(edge)
        def _():
            for buf in bufs:
                buf[x0 : x0 + n, y0 : y0 + m, :] = jnp.zeros((n, m, 256), F32)

    for cond, copy in jobs:
        if cond is None:
            copy.wait()
        else:
            pl.when(cond)(copy.wait)

    now, old = one, two
    for step in range(1, STEPS + 1):
        last = step == STEPS
        y0, rows = (16, 64) if last else (8, 80)
        lane = lanes((rows, 128))
        top, end = lane == 0, lane == 127

        def row(i, carry, now=now, old=old, step=step, y0=y0, rows=rows, top=top, end=end, last=last):
            x = i + (step - HALO)
            at, lower, upper = (x + 32) & 31, (x + 31) & 31, (x + 33) & 31
            here = slice(y0, y0 + rows)
            halves = (slice(0, 128), slice(128, 256))
            a, b = (now[at, here, h] for h in halves)
            ra, rb = pltpu.roll(a, 1, 1), pltpu.roll(b, 1, 1)
            la, lb = pltpu.roll(a, 127, 1), pltpu.roll(b, 127, 1)
            depth = (
                jnp.where(top, a, ra) + jnp.where(end, lb, la),
                jnp.where(top, ra, rb) + jnp.where(end, 0.0, lb),
            )
            for h, v, dz in zip(halves, (a, b), depth):
                beside = now[lower, here, h] + now[upper, here, h]
                beside = beside + (now[at, y0 - 1 : y0 - 1 + rows, h] + now[at, y0 + 1 : y0 + 1 + rows, h])
                lap = beside + dz - 6.0 * v
                value = (2.0 * v - old[at, here, h]) + coef[at, here, h] * lap
                if last:
                    out[x, :, h] = value
                else:
                    old[at, here, h] = value
            return carry

        lax.fori_loop(0, 32 - 2 * step, row, 0)
        now, old = old, now


def shards(
    reg_disp,
    reg_prev,
    reg_coef,
    basin_disp,
    face_index,
    soil_class,
    spring_count,
    spring_modulus,
    spring_yield,
):
    n_gx = lax.axis_size("gx")
    n_x = lax.axis_size("sec") * n_gx
    right = [(i, (i + 1) % n_x) for i in range(n_x)]
    left = [(i, (i - 1) % n_x) for i in range(n_x)]
    swap_a = [(0, 1), (1, 0), (2, 3), (3, 2)]
    swap_b = [(0, 0), (1, 2), (2, 1), (3, 3)]
    regional = (reg_disp, reg_prev, reg_coef)

    half = pl.BlockSpec((16, 64, 128), lambda i: (0, 0, 0))
    whole = lambda *s: pl.BlockSpec(s, lambda i: (0,) * len(s))
    band, band_right, band_left = pl.pallas_call(
        band_kernel,
        grid=(1,),
        out_shape=(sds(48, 8, 128), sds(24, 8, 128), sds(24, 8, 128)),
        in_specs=[half] * 3,
        out_specs=(whole(48, 8, 128), whole(24, 8, 128), whole(24, 8, 128)),
        compiler_params=PARAMS,
        name="band",
    )(*regional)
    band_from_left = lax.ppermute(band_right, XAX, right)
    band_from_right = lax.ppermute(band_left, XAX, left)

    edge_right, edge_left, mid_right, mid_left = pl.pallas_call(
        pack_x_kernel,
        out_shape=(sds(22, 16, 256), sds(22, 16, 256), sds(22, 48, 256), sds(22, 48, 256)),
        in_specs=[ANY] * 3,
        out_specs=(ANY,) * 4,
        scratch_shapes=[pltpu.SemaphoreType.DMA((18,))],
        compiler_params=PARAMS,
        name="pack_x",
    )(*regional)
    edge_from_left = lax.ppermute(edge_right, XAX, right)
    edge_from_right = lax.ppermute(edge_left, XAX, left)
    mid_from_left = lax.ppermute(mid_right, XAX, right)
    mid_from_right = lax.ppermute(mid_left, XAX, left)

    ext, band_a, band_b = pl.pallas_call(
        band_edges_kernel,
        out_shape=(sds(48, 32, 128), sds(3, 32, 128), sds(3, 32, 128)),
        in_specs=[VM] * 3,
        out_specs=(VM,) * 3,
        compiler_params=PARAMS,
        name="band_edges",
    )(band, band_from_left, band_from_right)
    band_a = lax.ppermute(band_a, "gy", swap_a)
    band_b = lax.ppermute(band_b, "gy", swap_b)
    trace = pl.pallas_call(
        band_steps_kernel,
        out_shape=sds(8, 8, 128),
        in_specs=[VM] * 3,
        out_specs=VM,
        scratch_shapes=[pltpu.VMEM((17, 32, 128), F32)] * 3,
        compiler_params=PARAMS,
        name="band_steps",
    )(ext, band_a, band_b)

    table = lax.all_gather(trace, "gy").reshape(32, 8, 128)
    index = lax.all_gather(face_index.reshape(4, 128), "gx").reshape(n_gx * 4, 128)
    picked = pl.pallas_call(
        pick_kernel,
        out_shape=sds(n_gx * 4, 8, 128),
        in_specs=[VM] * 2,
        out_specs=VM,
        compiler_params=PARAMS,
        name="pick",
    )(table, index)
    arrived = lax.all_to_all(picked.reshape(n_gx, 32, 128), "gx", 0, 0)

    y_a, y_b = pl.pallas_call(
        pack_y_kernel,
        out_shape=(sds(92, 8, 256), sds(92, 8, 256)),
        in_specs=[ANY] * 5,
        out_specs=(ANY,) * 2,
        scratch_shapes=[pltpu.SemaphoreType.DMA((10,))],
        compiler_params=PARAMS,
        name="pack_y",
    )(*regional, edge_from_left, edge_from_right)
    y_a = lax.ppermute(y_a, "gy", swap_a)
    y_b = lax.ppermute(y_b, "gy", swap_b)

    soil = soil_class[0]
    start = basin_disp[0]
    tables = (spring_count, spring_modulus, spring_yield)
    block = pl.BlockSpec((64, 128), lambda i: (0, i))
    upper, edge = pl.pallas_call(
        columns_kernel,
        grid=(4,),
        out_shape=(sds(64, 512), sds(8, 512)),
        in_specs=[SM] * 3 + [block] * 2,
        out_specs=(block, pl.BlockSpec((8, 128), lambda i: (0, i))),
        scratch_shapes=[pltpu.VMEM((16, 64, 128), F32)] * 3,
        compiler_params=PARAMS,
        name="columns",
    )(*tables, soil, start)

    tail = pl.BlockSpec((8, 512), lambda i: (7, 0))
    basin = pl.pallas_call(
        last_rows_kernel,
        grid=(1,),
        out_shape=sds(64, 512),
        in_specs=[SM] * 3 + [tail, tail, whole(8, 512), whole(n_gx, 32, 128), ANY],
        out_specs=tail,
        input_output_aliases={7: 0},
        compiler_params=PARAMS,
        name="last_rows",
    )(*tables, soil, start, edge, arrived, upper)

    final = pl.pallas_call(
        region_kernel,
        out_shape=sds(16, 64, 256),
        in_specs=[ANY] * 9,
        out_specs=VM,
        scratch_shapes=[pltpu.VMEM((32, 96, 256), F32)] * 3 + [pltpu.SemaphoreType.DMA((64,))],
        compiler_params=PARAMS,
        name="region",
    )(*regional, edge_from_left, edge_from_right, mid_from_left, mid_from_right, y_a, y_b)
    return (final, basin[None])


def solution(mesh):
    in_specs = (
        P(("sec", "gx"), "gy", None),
        P(("sec", "gx"), "gy", None),
        P(("sec", "gx"), "gy", None),
        P("sec", None, ("gx", "gy")),
        P("sec", ("gx", "gy")),
        P("sec", None, ("gx", "gy")),
        P(),
        P(),
        P(),
    )
    out_specs = (P(("sec", "gx"), "gy", None), P("sec", None, ("gx", "gy")))
    return jax.shard_map(shards, mesh=mesh, in_specs=in_specs, out_specs=out_specs, check_vma=False)
```

time: 463 us -> 188 us (0.41)
  waiting for transfers between devices: 197 us -> 72.4 us
  starting transfers between devices: 144 us -> 25 us
  Pallas kernels: 0 us -> 52.8 us
  other arithmetic: 51.1 us -> 0 us
  local copies, waits for them, and re-layouts: 47.6 us -> 9.02 us
  blocking collectives: 0 us -> 26 us
  between operations: 14.9 us -> 0.86 us
    all_gather x1 -> x0, waiting for transfers between devices: 187 us -> none  [shards(): lax.all_gather(jnp.stack(planes), ('gx', 'gy'), axis=1, tiled=True)]
    ppermute x32 -> x10, starting transfers between devices: 144 us -> 17.5 us  [the longest x1 7.79 us: shards(): mid_from_left = lax.ppermute(mid_right, XAX, right)]
    ppermute x32 -> x10, waiting for transfers between devices: 10.4 us -> 72.4 us  [the longest x1 37.2 us: shards(): edge_from_right = lax.ppermute(edge_left, XAX, left)]
    pallas_call x0 -> x9, Pallas kernels: none -> 52.8 us  [the longest x1 26.3 us: shards(): pl.pallas_call(region_kernel, out_shape=sds(16, 64, 256), in_specs=[ANY]...]
    slice x44 -> x0, local copies, waits for them, and re-layouts: 28.3 us -> none  [the longest x17 10.1 us: shards(): lower = jnp.concatenate([advance_displace[1:], base[step][None]], axis=0)]
    all_gather x0 -> x2, blocking collectives: none -> 26 us  [the longest x1 15.2 us: shards(): lax.all_gather(face_index.reshape(4, 128), 'gx').reshape(n_gx * 4, 128)]
    reduce_sum x8 -> x0, other arithmetic: 24.6 us -> none  [the longest x7 23.6 us: shards(): stress = jnp.sum(springs, axis=0)]
    add x15 -> x0, other arithmetic: 21.7 us -> none  [the longest x8 20.7 us: shards(): following = 2.0 * current - former + reg_coef * laplace_rim(padded, current)]
  transfers between devices with their start and end apart: 33 -> 11, of which waited for: 5 -> 5; matrix products, arithmetic and copies ran while one was open for 5% -> 0% of each run, Pallas kernels for 0% -> 13%
where the time goes in v1:
time: 188 us; the launch traced here: 186 us
  waiting for transfers between devices  72.4 us (39%)
  Pallas kernels  52.8 us (28%)
  blocking collectives  26 us (14%)
  starting transfers between devices  25 us (13%)
  local copies, waits for them, and re-layouts  9.02 us (5%)
    ppermute x1, waiting for transfers between devices, shards(): edge_from_right = lax.ppermute(edge_left, XAX, left)  37.2 us
    pallas_call x1, Pallas kernels, shards(): pl.pallas_call(region_kernel, out_shape=sds(16, 64, 256), in_specs=[ANY]...  26.3 us
    ppermute x1, waiting for transfers between devices, shards(): band_from_left = lax.ppermute(band_right, XAX, right)  21.8 us
    all_gather x1, blocking collectives, shards(): lax.all_gather(face_index.reshape(4, 128), 'gx').reshape(n_gx * 4, 128)  15.2 us
    all_gather x1, blocking collectives, shards(): table = lax.all_gather(trace, 'gy').reshape(32, 8, 128)  10.9 us
    ppermute x1, waiting for transfers between devices, shards(): band_from_right = lax.ppermute(band_left, XAX, left)  10.2 us
    pallas_call x1, Pallas kernels, shards(): pl.pallas_call(columns_kernel, grid=(4,), out_shape=(sds(64, 512), sds(8,...  9.97 us
    unnamed x34, local copies, waits for them, and re-layouts  9.02 us
  transfers between devices with their start and end apart: 11, of which 5 were waited for; matrix products, arithmetic and copies ran while one was open for 0% of the time, Pallas kernels for 13%

profile of v1, /device:TPU:95, one launch (start us, length us, event | category | flops | bytes accessed | tf_op | source)
XLA Modules:
  0.0 186.1 jit_solution(5155104770099685259)
XLA Ops:
  0.6 1.2 copy-done
  1.9 1.2 copy-done.2
  3.1 1.2 copy-done.4
  4.3 1.5 pack_x.1
  5.8 3.9 %collective-permute-start = (f32[22,16,256]{2,1,0:T(8,128)S(1)}, f32[22,16,256]{2,1,0:T(8,128)S(1)}, u32[]{:S(2)}, u32[]{:S(2)}) collective-permute-start(f32[22,16,256]{2,1,0:T(8,128)S(1)} %get-tuple-element.16), channel_id=1, source_target_pairs={{0,4},{4,8},{8,12},{12,16},{16,20},{20,24},{24,28},{28,32},{32,36}... | collective-permute-start | bytes 1081352 | tf_op jit(solution)/shard_map/ppermute | solution.py:384
  9.7 7.8 %collective-permute-start.2 = (f32[22,48,256]{2,1,0:T(8,128)}, f32[22,48,256]{2,1,0:T(8,128)}, u32[]{:S(2)}, u32[]{:S(2)}) collective-permute-start(f32[22,48,256]{2,1,0:T(8,128)} %get-tuple-element.18), channel_id=1, source_target_pairs={{0,4},{4,8},{8,12},{12,16},{16,20},{20,24},{24,28},{28,32},{32,36}... | collective-permute-start | bytes 3244040 | tf_op jit(solution)/shard_map/ppermute | solution.py:386
  17.5 2.0 %collective-permute-done.from_left.el = f32[22,16,256]{2,1,0:T(8,128)S(1)} collective-permute-done((f32[22,16,256]{2,1,0:T(8,128)S(1)}, f32[22,16,256]{2,1,0:T(8,128)S(1)}, u32[]{:S(2)}, u32[]{:S(2)}) %collective-permute-start) | collective-permute-done | bytes 360480 | tf_op jit(solution)/shard_map/ppermute | solution.py:384
  19.5 37.2 %collective-permute-done.1.from_right.er = f32[22,16,256]{2,1,0:T(8,128)S(1)} collective-permute-done((f32[22,16,256]{2,1,0:T(8,128)S(1)}, f32[22,16,256]{2,1,0:T(8,128)S(1)}, u32[]{:S(2)}, u32[]{:S(2)}) %collective-permute-start.1) | collective-permute-done | bytes 360480 | tf_op jit(solution)/shard_map/ppermute | solution.py:385
  56.7 1.2 pack_y.1
  57.9 1.7 collective-permute-start.4
  59.6 2.0 %collective-permute-start.5 = (f32[92,8,256]{2,1,0:T(8,128)}, f32[92,8,256]{2,1,0:T(8,128)}, u32[]{:S(2)}, u32[]{:S(2)}) collective-permute-start(f32[92,8,256]{2,1,0:T(8,128)} %get-tuple-element.21), channel_id=1, source_target_pairs={{0,0},{1,2},{2,1},{3,3},{4,4},{5,6},{6,5},{7,7},{8,8},{9,10},{10,9... | collective-permute-start | bytes 2261000 | tf_op jit(solution)/shard_map/ppermute | solution.py:431
  61.6 0.7 band.1
  62.4 21.8 %collective-permute-done.6.from_left = f32[24,8,128]{2,1,0:T(8,128)S(1)} collective-permute-done((f32[24,8,128]{2,1,0:T(8,128)S(1)}, f32[24,8,128]{2,1,0:T(8,128)S(1)}, u32[]{:S(2)}, u32[]{:S(2)}) %collective-permute-start.6) | collective-permute-done | bytes 98336 | tf_op jit(solution)/shard_map/ppermute | solution.py:372
  84.2 10.2 %collective-permute-done.7.from_right = f32[24,8,128]{2,1,0:T(8,128)S(1)} collective-permute-done((f32[24,8,128]{2,1,0:T(8,128)S(1)}, f32[24,8,128]{2,1,0:T(8,128)S(1)}, u32[]{:S(2)}, u32[]{:S(2)}) %collective-permute-start.7) | collective-permute-done | bytes 98336 | tf_op jit(solution)/shard_map/ppermute | solution.py:373
  94.4 2.3 %band_edges.1 = (f32[48,32,128]{2,1,0:T(8,128)S(1)}, f32[3,32,128]{2,1,0:T(8,128)S(1)}, f32[3,32,128]{2,1,0:T(8,128)S(1)}) custom-call(f32[48,8,128]{2,1,0:T(8,128)S(1)} %get-tuple-element.23.band, f32[24,8,128]{2,1,0:T(8,128)S(1)} %collective-permute-done.6.from_left, f32[24,8,128]{2,1,0:T(8,128)S(1)} %collective-permute-done.7.from_right), custom_call_target="tpu_custom_call" | custom-call | tf_op jit(solution)/shard_map/band_edges/pallas_call | solution.py:389
  96.8 0.1 collective-permute-start.8
  96.9 1.2 collective-permute-done.8.recv_a
  98.1 1.9 %collective-permute-start.9 = (f32[3,32,128]{2,1,0:T(8,128)S(1)}, f32[3,32,128]{2,1,0:T(8,128)S(1)}, u32[]{:S(2)}, u32[]{:S(2)}) collective-permute-start(f32[3,32,128]{2,1,0:T(8,128)S(1)} %get-tuple-element.28), channel_id=1, source_target_pairs={{0,0},{1,2},{2,1},{3,3},{4,4},{5,6},{6,5},{7,7},{8,8},{9,10},{10,9... | collective-permute-start | bytes 147464 | tf_op jit(solution)/shard_map/ppermute | solution.py:398
  100.0 15.2 %all_gather.11 = s32[16,4,128]{2,1,0:T(4,128)S(1)} all-gather(s32[1,4,128]{2,1,0:T(4,128)S(1)} %bitcast.13), channel_id=1, replica_groups=mesh['sec'=4,'gx'=16,'gy'=4] {'gx'}, dimensions={0}, use_global_device_ids=true | all-gather | bytes 34816 | tf_op jit(solution)/shard_map/all_gather | solution.py:410
  115.2 1.1 band_steps.1
  116.4 10.9 %all-gather.table = f32[32,8,128]{2,1,0:T(8,128)S(1)} all-gather(f32[8,8,128]{2,1,0:T(8,128)S(1)} %band_steps.1), channel_id=2, replica_groups=mesh['sec'=4,'gx'=16,'gy'=4] {'gy'}, dimensions={0}, use_global_device_ids=true | all-gather | bytes 163840 | tf_op jit(solution)/shard_map/all_gather | solution.py:409
  127.2 7.1 %pick.1 = f32[64,8,128]{2,1,0:T(8,128)S(1)} custom-call(f32[32,8,128]{2,1,0:T(8,128)S(1)} %all-gather.table, s32[64,128]{1,0:T(8,128)S(1)} %bitcast.11), custom_call_target="tpu_custom_call" | custom-call | tf_op jit(solution)/shard_map/pick/pallas_call | solution.py:411
  134.3 0.7 copy-done.8
  135.0 7.5 %all-to-all-start = ((f32[16,32,128]{2,1,0:T(8,128)}), f32[16,32,128]{2,1,0:T(8,128)}, u32[]{:S(2)}, u32[]{:S(2)}) async-start(f32[16,32,128]{2,1,0:T(8,128)} %bitcast.6), calls=%async_computation | async-start | bytes 524288 | tf_op jit(solution)/shard_map/all_to_all | solution.py:419
  142.6 0.9 copy-done.9
  143.5 0.9 copy-done.11
  144.4 10.0 %columns.1 = (f32[64,512]{1,0:T(8,128)}, f32[8,512]{1,0:T(8,128)S(1)}) custom-call(s32[8]{0:T(128)S(1)} %copy-done.15, f32[8,16]{1,0:T(8,128)S(1)} %copy-done.13, f32[8,16]{1,0:T(8,128)S(1)} %copy-done.14, s32[64,512]{1,0:T(8,128)S(1)} %bitcast.7, f32[64,512]{1,0:T(8,128)S(1)} %bitcast.9), custom_call_target="tpu_custom_call" | custom-call | tf_op jit(solution)/shard_map/columns/pallas_call | solution.py:437
  154.4 0.9 copy-done.10
  155.3 0.9 copy-done.12
  156.2 2.5 %last_rows.1 = f32[64,512]{1,0:T(8,128)} custom-call(s32[8]{0:T(128)S(1)} %copy-done.15, f32[8,16]{1,0:T(8,128)S(1)} %copy-done.13, f32[8,16]{1,0:T(8,128)S(1)} %copy-done.14, s32[64,512]{1,0:T(8,128)S(1)} %bitcast.8, f32[64,512]{1,0:T(8,128)S(1)} %bitcast.10, f32[8,512]{1,0:T(8,128)S(1)} %get-tuple-element.22.edge, ...), custom_call_target="tpu_custom_call", output_to_operand_aliasing={{}: (7, {})} | custom-call | tf_op jit(solution)/shard_map/last_rows/pallas_call | solution.py:449
  158.7 1.0 copy-done.7
  159.7 26.3 %region.1 = f32[16,64,256]{2,1,0:T(8,128)} custom-call(f32[16,64,256]{2,1,0:T(8,128)S(1)} %copy-done.1, f32[16,64,256]{2,1,0:T(8,128)S(1)} %copy-done.3, f32[16,64,256]{2,1,0:T(8,128)S(1)} %copy-done.5, f32[22,16,256]{2,1,0:T(8,128)S(1)} %collective-permute-done.from_left.el, f32[22,16,256]{2,1,0:T(8,128)S(1)} %copy-done.7, ...), custom_call_target="tpu_custom_call" | custom-call | tf_op jit(solution)/shard_map/region/pallas_call | solution.py:460
  (35 shorter events, 0.2 us)
Async XLA Ops:
  0.6 1.2 copy-start
  1.9 1.2 copy-start.2
  3.1 1.2 copy-start.4
  5.8 13.6 %collective-permute-start = (f32[22,16,256]{2,1,0:T(8,128)S(1)}, f32[22,16,256]{2,1,0:T(8,128)S(1)}, u32[]{:S(2)}, u32[]{:S(2)}) collective-permute-start(f32[22,16,256]{2,1,0:T(8,128)S(1)} %get-tuple-element.16), channel_id=1, source_target_pairs={{0,4},{4,8},{8,12},{12,16},{16,20},{20,24},{24,28},{28,32},{32,36}... | collective-permute-start | bytes 1081352 | tf_op jit(solution)/shard_map/ppermute | solution.py:384
  9.7 47.0 %collective-permute-start.1 = (f32[22,16,256]{2,1,0:T(8,128)S(1)}, f32[22,16,256]{2,1,0:T(8,128)S(1)}, u32[]{:S(2)}, u32[]{:S(2)}) collective-permute-start(f32[22,16,256]{2,1,0:T(8,128)S(1)} %get-tuple-element.17), channel_id=1, source_target_pairs={{0,252},{4,0},{8,4},{12,8},{16,12},{20,16},{24,20},{28,24},{32,28}... | collective-permute-start | bytes 1081352 | tf_op jit(solution)/shard_map/ppermute | solution.py:385
  9.7 149.0 %collective-permute-start.2 = (f32[22,48,256]{2,1,0:T(8,128)}, f32[22,48,256]{2,1,0:T(8,128)}, u32[]{:S(2)}, u32[]{:S(2)}) collective-permute-start(f32[22,48,256]{2,1,0:T(8,128)} %get-tuple-element.18), channel_id=1, source_target_pairs={{0,4},{4,8},{8,12},{12,16},{16,20},{20,24},{24,28},{28,32},{32,36}... | collective-permute-start | bytes 3244040 | tf_op jit(solution)/shard_map/ppermute | solution.py:386
  17.5 141.2 %collective-permute-start.3 = (f32[22,48,256]{2,1,0:T(8,128)}, f32[22,48,256]{2,1,0:T(8,128)}, u32[]{:S(2)}, u32[]{:S(2)}) collective-permute-start(f32[22,48,256]{2,1,0:T(8,128)} %get-tuple-element.19), channel_id=1, source_target_pairs={{0,252},{4,0},{8,4},{12,8},{16,12},{20,16},{24,20},{28,24},{32,28}... | collective-permute-start | bytes 3244040 | tf_op jit(solution)/shard_map/ppermute | solution.py:387
  56.7 1.2 copy-start.6
  57.9 100.8 %collective-permute-start.4 = (f32[92,8,256]{2,1,0:T(8,128)}, f32[92,8,256]{2,1,0:T(8,128)}, u32[]{:S(2)}, u32[]{:S(2)}) collective-permute-start(f32[92,8,256]{2,1,0:T(8,128)} %get-tuple-element.20), channel_id=1, source_target_pairs={{0,1},{1,0},{2,3},{3,2},{4,5},{5,4},{6,7},{7,6},{8,9},{9,8},{10,11... | collective-permute-start | bytes 2261000 | tf_op jit(solution)/shard_map/ppermute | solution.py:430
  59.6 40.4 %copy-start.16 = (s32[1,512]{1,0:T(1,128)S(1)}, s32[1,512]{1,0:T(1,128)}, u32[]{:S(2)}) copy-start(s32[1,512]{1,0:T(1,128)} %param.13) | copy-start | bytes 6148
  59.6 99.1 %collective-permute-start.5 = (f32[92,8,256]{2,1,0:T(8,128)}, f32[92,8,256]{2,1,0:T(8,128)}, u32[]{:S(2)}, u32[]{:S(2)}) collective-permute-start(f32[92,8,256]{2,1,0:T(8,128)} %get-tuple-element.21), channel_id=1, source_target_pairs={{0,0},{1,2},{2,1},{3,3},{4,4},{5,6},{6,5},{7,7},{8,8},{9,10},{10,9... | collective-permute-start | bytes 2261000 | tf_op jit(solution)/shard_map/ppermute | solution.py:431
  62.3 21.9 %collective-permute-start.6 = (f32[24,8,128]{2,1,0:T(8,128)S(1)}, f32[24,8,128]{2,1,0:T(8,128)S(1)}, u32[]{:S(2)}, u32[]{:S(2)}) collective-permute-start(f32[24,8,128]{2,1,0:T(8,128)S(1)} %get-tuple-element.24), channel_id=1, source_target_pairs={{0,4},{4,8},{8,12},{12,16},{16,20},{20,24},{24,28},{28,32},{32,36}... | collective-permute-start | bytes 294920 | tf_op jit(solution)/shard_map/ppermute | solution.py:372
  84.2 10.2 %collective-permute-start.7 = (f32[24,8,128]{2,1,0:T(8,128)S(1)}, f32[24,8,128]{2,1,0:T(8,128)S(1)}, u32[]{:S(2)}, u32[]{:S(2)}) collective-permute-start(f32[24,8,128]{2,1,0:T(8,128)S(1)} %get-tuple-element.25), channel_id=1, source_target_pairs={{0,252},{4,0},{8,4},{12,8},{16,12},{20,16},{24,20},{28,24},{32,28}... | collective-permute-start | bytes 294920 | tf_op jit(solution)/shard_map/ppermute | solution.py:373
  94.4 48.1 %copy-start.14 = (f32[8,16]{1,0:T(8,128)S(1)}, f32[8,16]{1,0:T(8,128)}, u32[]{:S(2)}) copy-start(f32[8,16]{1,0:T(8,128)} %yields.3) | copy-start | bytes 1540
  96.7 45.8 %copy-start.13 = (f32[8,16]{1,0:T(8,128)S(1)}, f32[8,16]{1,0:T(8,128)}, u32[]{:S(2)}) copy-start(f32[8,16]{1,0:T(8,128)} %modulus.3) | copy-start | bytes 1540
  96.7 45.8 %copy-start.15 = (s32[8]{0:T(128)S(1)}, s32[8]{0:T(128)}, u32[]{:S(2)}) copy-start(s32[8]{0:T(128)} %count.3) | copy-start | bytes 100
  96.8 1.3 collective-permute-start.8
  98.1 17.1 %collective-permute-start.9 = (f32[3,32,128]{2,1,0:T(8,128)S(1)}, f32[3,32,128]{2,1,0:T(8,128)S(1)}, u32[]{:S(2)}, u32[]{:S(2)}) collective-permute-start(f32[3,32,128]{2,1,0:T(8,128)S(1)} %get-tuple-element.28), channel_id=1, source_target_pairs={{0,0},{1,2},{2,1},{3,3},{4,4},{5,6},{6,5},{7,7},{8,8},{9,10},{10,9... | collective-permute-start | bytes 147464 | tf_op jit(solution)/shard_map/ppermute | solution.py:398
  100.0 58.7 %copy-start.5 = (f32[16,64,256]{2,1,0:T(8,128)S(1)}, f32[16,64,256]{2,1,0:T(8,128)}, u32[]{:S(2)}) copy-start(f32[16,64,256]{2,1,0:T(8,128)} %c.7) | copy-start | bytes 3145732
  116.3 42.4 %copy-start.1 = (f32[16,64,256]{2,1,0:T(8,128)S(1)}, f32[16,64,256]{2,1,0:T(8,128)}, u32[]{:S(2)}) copy-start(f32[16,64,256]{2,1,0:T(8,128)} %u.7) | copy-start | bytes 3145732
  116.4 42.4 %copy-start.3 = (f32[16,64,256]{2,1,0:T(8,128)S(1)}, f32[16,64,256]{2,1,0:T(8,128)}, u32[]{:S(2)}) copy-start(f32[16,64,256]{2,1,0:T(8,128)} %p.7) | copy-start | bytes 3145732
  134.3 0.7 copy-start.8
  135.0 19.3 %all-to-all-start = ((f32[16,32,128]{2,1,0:T(8,128)}), f32[16,32,128]{2,1,0:T(8,128)}, u32[]{:S(2)}, u32[]{:S(2)}) async-start(f32[16,32,128]{2,1,0:T(8,128)} %bitcast.6), calls=%async_computation | async-start | bytes 524288 | tf_op jit(solution)/shard_map/all_to_all | solution.py:419
  142.6 0.9 copy-start.9
  143.5 0.9 copy-start.11
  154.4 0.9 copy-start.10
  155.3 0.9 copy-start.12
  158.7 1.0 copy-start.7

commit v2 on v1

--- a/solution.py
+++ b/solution.py
@@ -11,11 +11,13 @@
 FDEP = 64
 stress_rate = 0.5
 XAX = ("sec", "gx")
+ALL = ("sec", "gx", "gy")
 F32 = jnp.float32
 ANY = pl.BlockSpec(memory_space=pl.ANY)
 VM = pl.BlockSpec(memory_space=pltpu.VMEM)
 SM = pl.BlockSpec(memory_space=pltpu.SMEM)
-PARAMS = pltpu.CompilerParams(vmem_limit_bytes=48 * 1024 * 1024)
+PARAMS = pltpu.CompilerParams(vmem_limit_bytes=40 * 1024 * 1024)
+LARGE = pltpu.CompilerParams(vmem_limit_bytes=60 * 1024 * 1024)
 
 
 def sds(*shape):
@@ -125,21 +127,27 @@
 
 
 def pick_kernel(table, index, out):
-    me = lax.axis_index("gx")
-
-    def tile(t, carry):
+    me = lax.axis_index("gy")
+    count = table.shape[0]
+
+    def tile(t):
         cell = jnp.broadcast_to(index[pl.ds(t, 1), :], (8, 128))
         x, y = cell >> 8, cell & 255
-        place = ((y >> 6) << 3) + (x & 7)
-        place = jnp.where((x >> 4) == me, place, -1)
+        place = ((x >> 4) << 3) + (x & 7)
+        place = jnp.where((y >> 6) == me, place, -1)
         lane = (((x >> 3) & 1) << 6) + (y & 63)
-        acc = jnp.zeros((8, 128), F32)
-        for k in range(32):
-            acc = jnp.where(place == k, jnp.take_along_axis(table[k], lane, axis=1), acc)
-        out[t] = acc
+        accs = [jnp.zeros((8, 128), F32) for _ in range(4)]
+        for k in range(count):
+            found = jnp.take_along_axis(table[k], lane, axis=1)
+            accs[k % 4] = jnp.where(place == k, found, accs[k % 4])
+        out[t] = (accs[0] + accs[1]) + (accs[2] + accs[3])
+
+    def tiles(i, carry):
+        for t in range(2):
+            tile(i * 2 + t)
         return carry
 
-    lax.fori_loop(0, index.shape[0], tile, 0)
+    lax.fori_loop(0, index.shape[0] // 2, tiles, 0)
 
 
 def spring_values(cls, k, count, modulus, yields):
@@ -153,6 +161,8 @@
 
 
 def columns_kernel(count, modulus, yields, soil, start, out, edge, mods, lims, springs):
+    width = soil.shape[1]
+
     def rows(r, carry):
         at = pl.ds(pl.multiple_of(r * 8, 8), 8)
         cls = soil[at, :]
@@ -160,28 +170,34 @@
             mod, lim = spring_values(cls, k, count, modulus, yields)
             mods[k, at, :] = mod
             lims[k, at, :] = lim
-            springs[k, at, :] = jnp.zeros((8, 128), F32)
+            springs[k, at, :] = jnp.zeros((8, width), F32)
         return carry
 
     lax.fori_loop(0, 8, rows, 0)
-    row = lax.broadcasted_iota(jnp.int32, (64, 128), 0)
+    row = lax.broadcasted_iota(jnp.int32, (64, width), 0)
 
     def step(s, state):
         disp, vel, old = state
         strain = pltpu.roll(disp, 63, 0) - disp
         inc = strain - old
-        stress = jnp.zeros((64, 128), F32)
-        for k in range(16):
-            lim = lims[k]
-            value = jnp.minimum(jnp.maximum(springs[k] + mods[k] * inc, -lim), lim)
-            springs[k] = value
-            stress = stress + value
+        parts = []
+        for r in range(0, 64, 16):
+            here = slice(r, r + 16)
+            change = inc[here]
+            stress = jnp.zeros((16, width), F32)
+            for k in range(16):
+                lim = lims[k, here, :]
+                value = jnp.minimum(jnp.maximum(springs[k, here, :] + mods[k, here, :] * change, -lim), lim)
+                springs[k, here, :] = value
+                stress = stress + value
+            parts.append(stress)
+        stress = jnp.concatenate(parts, axis=0)
         edge[pl.ds(s, 1), :] = stress[55:56]
         above = jnp.where(row == 0, 0.0, pltpu.roll(stress, 1, 0))
         vel = vel + stress_rate * (stress - above)
         return disp + vel, vel, strain
 
-    zero = jnp.zeros((64, 128), F32)
+    zero = jnp.zeros((64, width), F32)
     out[...] = lax.fori_loop(0, STEPS, step, (start[...], zero, zero))[0]
 
 
@@ -220,22 +236,42 @@
 LEFT = ((0, 8, 0), (0, 7, 8), (0, 7, 15))
 
 
-def run_copies(pairs, sems):
-    copies = [pltpu.make_async_copy(src, dst, sems.at[n]) for n, (src, dst) in enumerate(pairs)]
-    for copy in copies:
-        copy.start()
-    for copy in copies:
-        copy.wait()
-
-
-def pack_x_kernel(u, p, c, edge_right, edge_left, mid_right, mid_left, sems):
-    pairs = []
-    for plan, edge, mid in ((RIGHT, edge_right, mid_right), (LEFT, edge_left, mid_left)):
+def start_jobs(jobs, sems):
+    copies = [(cond, pltpu.make_async_copy(src, dst, sems.at[n])) for n, (cond, src, dst) in enumerate(jobs)]
+    for cond, copy in copies:
+        if cond is None:
+            copy.start()
+        else:
+            pl.when(cond)(copy.start)
+    return copies
+
+
+def wait_jobs(copies):
+    for cond, copy in copies:
+        if cond is None:
+            copy.wait()
+        else:
+            pl.when(cond)(copy.wait)
+
+
+def run_jobs(jobs, sems):
+    wait_jobs(start_jobs(jobs, sems))
+
+
+def pack_x_kernel(u, p, c, edge_right, edge_left, mid_right, mid_left, mid_far, sems):
+    jobs = []
+    gx = lax.axis_index("gx")
+    for plan, edge, mid, ends in (
+        (RIGHT, edge_right, mid_right, gx == lax.axis_size("gx") - 1),
+        (LEFT, edge_left, mid_left, gx == 0),
+    ):
         for ref, (x0, n, at) in zip((u, p, c), plan):
-            pairs.append((ref.at[x0 : x0 + n, 0:8, :], edge.at[at : at + n, 0:8, :]))
-            pairs.append((ref.at[x0 : x0 + n, 56:64, :], edge.at[at : at + n, 8:16, :]))
-            pairs.append((ref.at[x0 : x0 + n, 8:56, :], mid.at[at : at + n, :, :]))
-    run_copies(pairs, sems)
+            middle = ref.at[x0 : x0 + n, 8:56, :]
+            jobs.append((None, ref.at[x0 : x0 + n, 0:8, :], edge.at[at : at + n, 0:8, :]))
+            jobs.append((None, ref.at[x0 : x0 + n, 56:64, :], edge.at[at : at + n, 8:16, :]))
+            jobs.append((None, middle, mid.at[at : at + n, :, :]))
+            jobs.append((ends, middle, mid_far.at[at : at + n, :, :]))
+    run_jobs(jobs, sems)
 
 
 def pack_y_kernel(u, p, c, from_left, from_right, send_a, send_b, sems):
@@ -245,30 +281,32 @@
         own = pl.ds(pl.multiple_of(side * 56, 8), 8)
         corner = pl.ds(pl.multiple_of(side * 8, 8), 8)
         for n, ref in enumerate((u, p, c)):
-            pairs.append((ref.at[:, own, :], send.at[16 * n : 16 * n + 16]))
-        pairs.append((from_left.at[:, corner, :], send.at[48:70]))
-        pairs.append((from_right.at[:, corner, :], send.at[70:92]))
-    run_copies(pairs, sems)
-
-
-def region_kernel(u, p, c, el, er, ml, mr, ya, yb, out, one, two, coef, sems):
+            pairs.append((None, ref.at[:, own, :], send.at[16 * n : 16 * n + 16]))
+        pairs.append((None, from_left.at[:, corner, :], send.at[48:70]))
+        pairs.append((None, from_right.at[:, corner, :], send.at[70:92]))
+    run_jobs(pairs, sems)
+
+
+def region_kernel(u, p, c, el, er, ml, mr, relayed, ya, yb, out, one, two, coef, sems):
     low_x, high_x = x_edges()
     low_y, high_y = y_edges()
     even = lax.rem(lax.axis_index("gy"), 2) == 0
     bufs = (one, two, coef)
-    always = jnp.bool_(True)
+    gx = lax.axis_index("gx")
+    first, final = gx == 0, gx == lax.axis_size("gx") - 1
     jobs = []
 
     def job(cond, src, dst):
-        jobs.append((cond, pltpu.make_async_copy(src, dst, sems.at[len(jobs)])))
+        jobs.append((cond, src, dst))
 
     for ref, buf in zip((u, p, c), bufs):
         job(None, ref, buf.at[0:16, 16:80, :])
     left_at = ((24, 8, 0), (25, 7, 8), (25, 7, 15))
     right_at = ((16, 8, 0), (16, 7, 8), (16, 7, 15))
-    for cond, plan, edge, mid in ((~low_x, left_at, el, ml), (~high_x, right_at, er, mr)):
+    for cond, far, plan, edge, mid in ((~low_x, first, left_at, el, ml), (~high_x, final, right_at, er, mr)):
         for buf, (x0, n, at) in zip(bufs, plan):
-            job(cond, mid.at[at : at + n], buf.at[x0 : x0 + n, 24:72, :])
+            job(~far, mid.at[at : at + n], buf.at[x0 : x0 + n, 24:72, :])
+            job(far & cond, relayed.at[at : at + n], buf.at[x0 : x0 + n, 24:72, :])
             job(cond, edge.at[at : at + n, 0:8, :], buf.at[x0 : x0 + n, 16:24, :])
             job(cond, edge.at[at : at + n, 8:16, :], buf.at[x0 : x0 + n, 72:80, :])
     for msg, is_high in ((ya, even), (yb, ~even)):
@@ -282,11 +320,7 @@
                         msg.at[base + at : base + at + n],
                         buf.at[x0 : x0 + n, rows[0] : rows[1], :],
                     )
-    for cond, copy in jobs:
-        if cond is None:
-            copy.start()
-        else:
-            pl.when(cond)(copy.start)
+    copies = start_jobs(jobs, sems)
     for edge, x0, n, y0, m in (
         (low_x, 24, 8, 8, 80),
         (high_x, 16, 8, 8, 80),
@@ -299,44 +333,53 @@
             for buf in bufs:
                 buf[x0 : x0 + n, y0 : y0 + m, :] = jnp.zeros((n, m, 256), F32)
 
-    for cond, copy in jobs:
-        if cond is None:
-            copy.wait()
-        else:
-            pl.when(cond)(copy.wait)
+    wait_jobs(copies)
 
     now, old = one, two
+    halves = (slice(0, 128), slice(128, 256))
+    rows = 16
+    lane = lanes((rows, 128))
+    top, end = lane == 0, lane == 127
     for step in range(1, STEPS + 1):
         last = step == STEPS
-        y0, rows = (16, 64) if last else (8, 80)
-        lane = lanes((rows, 128))
-        top, end = lane == 0, lane == 127
-
-        def row(i, carry, now=now, old=old, step=step, y0=y0, rows=rows, top=top, end=end, last=last):
-            x = i + (step - HALO)
-            at, lower, upper = (x + 32) & 31, (x + 31) & 31, (x + 33) & 31
-            here = slice(y0, y0 + rows)
-            halves = (slice(0, 128), slice(128, 256))
-            a, b = (now[at, here, h] for h in halves)
-            ra, rb = pltpu.roll(a, 1, 1), pltpu.roll(b, 1, 1)
-            la, lb = pltpu.roll(a, 127, 1), pltpu.roll(b, 127, 1)
-            depth = (
-                jnp.where(top, a, ra) + jnp.where(end, lb, la),
-                jnp.where(top, ra, rb) + jnp.where(end, 0.0, lb),
-            )
-            for h, v, dz in zip(halves, (a, b), depth):
-                beside = now[lower, here, h] + now[upper, here, h]
-                beside = beside + (now[at, y0 - 1 : y0 - 1 + rows, h] + now[at, y0 + 1 : y0 + 1 + rows, h])
-                lap = beside + dz - 6.0 * v
-                value = (2.0 * v - old[at, here, h]) + coef[at, here, h] * lap
-                if last:
-                    out[x, :, h] = value
-                else:
-                    old[at, here, h] = value
-            return carry
-
-        lax.fori_loop(0, 32 - 2 * step, row, 0)
+        for x in range(step - HALO, 16 + HALO - step):
+            at, lower, upper = x % 32, (x - 1) % 32, (x + 1) % 32
+            for y0 in range(16, 80, rows) if last else range(8, 88, rows):
+                here = slice(y0, y0 + rows)
+                a, b = (now[at, here, h] for h in halves)
+                ra, rb = pltpu.roll(a, 1, 1), pltpu.roll(b, 1, 1)
+                la, lb = pltpu.roll(a, 127, 1), pltpu.roll(b, 127, 1)
+                depth = (
+                    jnp.where(top, a, ra) + jnp.where(end, lb, la),
+                    jnp.where(top, ra, rb) + jnp.where(end, 0.0, lb),
+                )
+                for h, v, dz in zip(halves, (a, b), depth):
+                    beside = now[lower, here, h] + now[upper, here, h]
+                    beside = beside + (now[at, y0 - 1 : y0 - 1 + rows, h] + now[at, y0 + 1 : y0 + 1 + rows, h])
+                    lap = beside + dz - 6.0 * v
+                    value = (2.0 * v - old[at, here, h]) + coef[at, here, h] * lap
+                    if last:
+                        out[x, y0 - 16 : y0 - 16 + rows, h] = value
+                    else:
+                        old[at, here, h] = value
         now, old = old, now
+
+
+def relays(n_sec, n_gx):
+    def at(sec, gx, gy):
+        return (sec % n_sec * n_gx + gx) * 4 + gy
+
+    top = n_gx - 1
+    out, into = [], []
+    for sec in range(n_sec):
+        for gy in range(4):
+            up, down = ((3, 12), (11, 4))[gy % 2]
+            out += [(at(sec, top, gy), at(sec, up, gy)), (at(sec, 0, gy), at(sec, down, gy))]
+            if sec < n_sec - 1:
+                into.append((at(sec, up, gy), at(sec + 1, 0, gy)))
+            if sec > 0:
+                into.append((at(sec, down, gy), at(sec - 1, top, gy)))
+    return out, into
 
 
 def shards(
@@ -357,7 +400,6 @@
     swap_a = [(0, 1), (1, 0), (2, 3), (3, 2)]
     swap_b = [(0, 0), (1, 2), (2, 1), (3, 3)]
     regional = (reg_disp, reg_prev, reg_coef)
-
     half = pl.BlockSpec((16, 64, 128), lambda i: (0, 0, 0))
     whole = lambda *s: pl.BlockSpec(s, lambda i: (0,) * len(s))
     band, band_right, band_left = pl.pallas_call(
@@ -366,25 +408,31 @@
         out_shape=(sds(48, 8, 128), sds(24, 8, 128), sds(24, 8, 128)),
         in_specs=[half] * 3,
         out_specs=(whole(48, 8, 128), whole(24, 8, 128), whole(24, 8, 128)),
-        compiler_params=PARAMS,
+        compiler_params=LARGE,
         name="band",
     )(*regional)
     band_from_left = lax.ppermute(band_right, XAX, right)
     band_from_right = lax.ppermute(band_left, XAX, left)
-
-    edge_right, edge_left, mid_right, mid_left = pl.pallas_call(
+    index, _ = lax.optimization_barrier((face_index.reshape(1, 4, 128), band_right))
+    index = lax.all_gather(index, "gy").reshape(16, 128)
+
+    regional, index = lax.optimization_barrier((regional, index))
+    edge_right, edge_left, mid_right, mid_left, mid_far = pl.pallas_call(
         pack_x_kernel,
-        out_shape=(sds(22, 16, 256), sds(22, 16, 256), sds(22, 48, 256), sds(22, 48, 256)),
+        out_shape=(sds(22, 16, 256), sds(22, 16, 256), sds(22, 48, 256), sds(22, 48, 256), sds(22, 48, 256)),
         in_specs=[ANY] * 3,
-        out_specs=(ANY,) * 4,
-        scratch_shapes=[pltpu.SemaphoreType.DMA((18,))],
+        out_specs=(ANY,) * 5,
+        scratch_shapes=[pltpu.SemaphoreType.DMA((24,))],
         compiler_params=PARAMS,
         name="pack_x",
     )(*regional)
     edge_from_left = lax.ppermute(edge_right, XAX, right)
     edge_from_right = lax.ppermute(edge_left, XAX, left)
-    mid_from_left = lax.ppermute(mid_right, XAX, right)
-    mid_from_right = lax.ppermute(mid_left, XAX, left)
+    relay_out, relay_in = relays(lax.axis_size("sec"), n_gx)
+    mid_relay = lax.ppermute(mid_far, ALL, relay_out)
+    mid_from_left = lax.ppermute(mid_right, "gx", [(i, i + 1) for i in range(n_gx - 1)])
+    mid_from_right = lax.ppermute(mid_left, "gx", [(i + 1, i) for i in range(n_gx - 1)])
+    mid_relay = lax.ppermute(mid_relay, ALL, relay_in)
 
     ext, band_a, band_b = pl.pallas_call(
         band_edges_kernel,
@@ -406,17 +454,17 @@
         name="band_steps",
     )(ext, band_a, band_b)
 
-    table = lax.all_gather(trace, "gy").reshape(32, 8, 128)
-    index = lax.all_gather(face_index.reshape(4, 128), "gx").reshape(n_gx * 4, 128)
+    table = lax.all_to_all(jnp.broadcast_to(trace.reshape(1, 64, 128), (n_gx, 64, 128)), "gx", 0, 0)
+    table = table.reshape(n_gx * 8, 8, 128)
     picked = pl.pallas_call(
         pick_kernel,
-        out_shape=sds(n_gx * 4, 8, 128),
+        out_shape=sds(16, 8, 128),
         in_specs=[VM] * 2,
         out_specs=VM,
         compiler_params=PARAMS,
         name="pick",
     )(table, index)
-    arrived = lax.all_to_all(picked.reshape(n_gx, 32, 128), "gx", 0, 0)
+    arrived = lax.all_to_all(picked.reshape(4, 32, 128), "gy", 0, 0)
 
     y_a, y_b = pl.pallas_call(
         pack_y_kernel,
@@ -433,14 +481,14 @@
     soil = soil_class[0]
     start = basin_disp[0]
     tables = (spring_count, spring_modulus, spring_yield)
-    block = pl.BlockSpec((64, 128), lambda i: (0, i))
+    block = pl.BlockSpec((64, 256), lambda i: (0, i))
     upper, edge = pl.pallas_call(
         columns_kernel,
-        grid=(4,),
+        grid=(2,),
         out_shape=(sds(64, 512), sds(8, 512)),
         in_specs=[SM] * 3 + [block] * 2,
-        out_specs=(block, pl.BlockSpec((8, 128), lambda i: (0, i))),
-        scratch_shapes=[pltpu.VMEM((16, 64, 128), F32)] * 3,
+        out_specs=(block, pl.BlockSpec((8, 256), lambda i: (0, i))),
+        scratch_shapes=[pltpu.VMEM((16, 64, 256), F32)] * 3,
         compiler_params=PARAMS,
         name="columns",
     )(*tables, soil, start)
@@ -450,7 +498,7 @@
         last_rows_kernel,
         grid=(1,),
         out_shape=sds(64, 512),
-        in_specs=[SM] * 3 + [tail, tail, whole(8, 512), whole(n_gx, 32, 128), ANY],
+        in_specs=[SM] * 3 + [tail, tail, whole(8, 512), whole(4, 32, 128), ANY],
         out_specs=tail,
         input_output_aliases={7: 0},
         compiler_params=PARAMS,
@@ -460,12 +508,12 @@
     final = pl.pallas_call(
         region_kernel,
         out_shape=sds(16, 64, 256),
-        in_specs=[ANY] * 9,
+        in_specs=[ANY] * 10,
         out_specs=VM,
         scratch_shapes=[pltpu.VMEM((32, 96, 256), F32)] * 3 + [pltpu.SemaphoreType.DMA((64,))],
         compiler_params=PARAMS,
         name="region",
-    )(*regional, edge_from_left, edge_from_right, mid_from_left, mid_from_right, y_a, y_b)
+    )(*regional, edge_from_left, edge_from_right, mid_from_left, mid_from_right, mid_relay, y_a, y_b)
     return (final, basin[None])
 
 

time: 188 us -> 120 us (0.64)
  the two profiles are of different devices: /device:TPU:95 before, /device:TPU:224 now
where the time goes in v2:
time: 120 us; the launch traced here: 119 us
  starting transfers between devices  39.5 us (33%)
  Pallas kernels  34.9 us (29%)
  blocking collectives  26.5 us (22%)
  waiting for transfers between devices  11.9 us (10%)
  local copies, waits for them, and re-layouts  5.29 us (4%)
    all_to_all x1, blocking collectives, shards(): lax.all_to_all(jnp.broadcast_to(trace.reshape(1, 64, 128), (n_gx, 64, 128...  21.3 us
    pallas_call x1, Pallas kernels, shards(): pl.pallas_call(region_kernel, out_shape=sds(16, 64, 256), in_specs=[ANY]...  12.9 us
    ppermute x1, starting transfers between devices, shards(): band_b = lax.ppermute(band_b, 'gy', swap_b)  9.93 us
    ppermute x1, waiting for transfers between devices, shards(): band_from_left = lax.ppermute(band_right, XAX, right)  9.17 us
    pallas_call x1, Pallas kernels, shards(): pl.pallas_call(columns_kernel, grid=(2,), out_shape=(sds(64, 512), sds(8,...  7.5 us
    ppermute x1, starting transfers between devices, shards(): edge_from_right = lax.ppermute(edge_left, XAX, left)  7.17 us
    ppermute x1, starting transfers between devices, shards(): mid_relay = lax.ppermute(mid_far, ALL, relay_out)  5.67 us
    unnamed x34, local copies, waits for them, and re-layouts  5.25 us
  transfers between devices with their start and end apart: 13, of which 3 were waited for; matrix products, arithmetic and copies ran while one was open for 0% of the time, Pallas kernels for 15%

profile of v2, /device:TPU:224, one launch (start us, length us, event | category | flops | bytes accessed | tf_op | source)
XLA Modules:
  0.0 119.1 jit_solution(3812745498404322497)
XLA Ops:
  0.7 2.9 %band.1 = (f32[48,8,128]{2,1,0:T(8,128)}, f32[24,8,128]{2,1,0:T(8,128)}, f32[24,8,128]{2,1,0:T(8,128)}) custom-call(f32[16,64,256]{2,1,0:T(8,128)} %u.4, f32[16,64,256]{2,1,0:T(8,128)} %p.4, f32[16,64,256]{2,1,0:T(8,128)} %c.4), custom_call_target="tpu_custom_call" | custom-call | tf_op jit(solution)/shard_map/band/pallas_call | solution.py:405
  3.5 5.2 %all-gather = s32[4,4,128]{2,1,0:T(4,128)S(1)} all-gather(s32[1,4,128]{2,1,0:T(4,128)S(1)} %bitcast.17), channel_id=2, replica_groups=mesh['sec'=4,'gx'=16,'gy'=4] {'gy'}, dimensions={0}, use_global_device_ids=true | all-gather | bytes 10240 | tf_op jit(solution)/shard_map/all_gather | solution.py:417
  8.7 0.0 copy-start.15
  8.7 1.6 %pack_x.1 = (f32[22,16,256]{2,1,0:T(8,128)S(1)}, f32[22,16,256]{2,1,0:T(8,128)S(1)}, f32[22,48,256]{2,1,0:T(8,128)}, f32[22,48,256]{2,1,0:T(8,128)}, f32[22,48,256]{2,1,0:T(8,128)S(1)}) custom-call(f32[16,64,256]{2,1,0:T(8,128)S(1)} %copy-done, f32[16,64,256]{2,1,0:T(8,128)S(1)} %copy-done.1, f32[16,64,256]{2,1,0:T(8,128)S(1)} %copy-done.2), custom_call_target="tpu_custom_call" | custom-call | tf_op jit(solution)/shard_map/pack_x/pallas_call | solution.py:420
  10.4 5.7 %collective-permute-start.4 = (f32[22,48,256]{2,1,0:T(8,128)S(1)}, f32[22,48,256]{2,1,0:T(8,128)}, u32[]{:S(2)}, u32[]{:S(2)}) collective-permute-start(f32[22,48,256]{2,1,0:T(8,128)S(1)} %get-tuple-element.31), channel_id=1, source_target_pairs={{60,12},{0,48},{61,45},{1,17},{62,14},{2,50},{63,47},{3,19},{124,7... | collective-permute-start | bytes 3244040 | tf_op jit(solution)/shard_map/ppermute | solution.py:432
  16.0 3.8 %collective-permute-start.9 = (f32[24,8,128]{2,1,0:T(8,128)S(1)}, f32[24,8,128]{2,1,0:T(8,128)S(1)}, u32[]{:S(2)}, u32[]{:S(2)}) collective-permute-start(f32[24,8,128]{2,1,0:T(8,128)S(1)} %copy-done.16), channel_id=1, source_target_pairs={{0,252},{4,0},{8,4},{12,8},{16,12},{20,16},{24,20},{28,24},{32,28}... | collective-permute-start | bytes 294920 | tf_op jit(solution)/shard_map/ppermute | solution.py:415
  19.9 7.2 %collective-permute-start.1 = (f32[22,16,256]{2,1,0:T(8,128)S(1)}, f32[22,16,256]{2,1,0:T(8,128)S(1)}, u32[]{:S(2)}, u32[]{:S(2)}) collective-permute-start(f32[22,16,256]{2,1,0:T(8,128)S(1)} %get-tuple-element.28), channel_id=1, source_target_pairs={{0,252},{4,0},{8,4},{12,8},{16,12},{20,16},{24,20},{28,24},{32,28}... | collective-permute-start | bytes 1081352 | tf_op jit(solution)/shard_map/ppermute | solution.py:430
  27.1 2.3 %collective-permute-start.2 = (f32[22,48,256]{2,1,0:T(8,128)}, f32[22,48,256]{2,1,0:T(8,128)}, u32[]{:S(2)}, u32[]{:S(2)}) collective-permute-start(f32[22,48,256]{2,1,0:T(8,128)} %get-tuple-element.29), channel_id=1, source_target_pairs={{0,4},{4,8},{8,12},{12,16},{16,20},{20,24},{24,28},{28,32},{32,36}... | collective-permute-start | bytes 3244040 | tf_op jit(solution)/shard_map/ppermute | solution.py:433
  29.3 9.2 %collective-permute-done.8.from_left = f32[24,8,128]{2,1,0:T(8,128)S(1)} collective-permute-done((f32[24,8,128]{2,1,0:T(8,128)S(1)}, f32[24,8,128]{2,1,0:T(8,128)S(1)}, u32[]{:S(2)}, u32[]{:S(2)}) %collective-permute-start.8) | collective-permute-done | bytes 98336 | tf_op jit(solution)/shard_map/ppermute | solution.py:414
  38.5 1.3 %collective-permute-start.3 = (f32[22,48,256]{2,1,0:T(8,128)}, f32[22,48,256]{2,1,0:T(8,128)}, u32[]{:S(2)}, u32[]{:S(2)}) collective-permute-start(f32[22,48,256]{2,1,0:T(8,128)} %get-tuple-element.30), channel_id=1, source_target_pairs={{4,0},{8,4},{12,8},{16,12},{20,16},{24,20},{28,24},{32,28},{36,32}... | collective-permute-start | bytes 3244040 | tf_op jit(solution)/shard_map/ppermute | solution.py:434
  39.8 1.3 %collective-permute-start.5 = (f32[22,48,256]{2,1,0:T(8,128)}, f32[22,48,256]{2,1,0:T(8,128)}, u32[]{:S(2)}, u32[]{:S(2)}) collective-permute-start(f32[22,48,256]{2,1,0:T(8,128)} %collective-permute-done.4), channel_id=1, source_target_pairs={{12,64},{45,65},{14,66},{47,67},{76,128},{112,60},{109,129},{81,61... | collective-permute-start | bytes 3244040 | tf_op jit(solution)/shard_map/ppermute | solution.py:435
  41.1 2.3 %band_edges.1 = (f32[48,32,128]{2,1,0:T(8,128)S(1)}, f32[3,32,128]{2,1,0:T(8,128)S(1)}, f32[3,32,128]{2,1,0:T(8,128)S(1)}) custom-call(f32[48,8,128]{2,1,0:T(8,128)S(1)} %copy-done.10, f32[24,8,128]{2,1,0:T(8,128)S(1)} %collective-permute-done.8.from_left, f32[24,8,128]{2,1,0:T(8,128)S(1)} %collective-permute-done.9.from_right), custom_call_target="tpu_custom_call" | custom-call | tf_op jit(solution)/shard_map/band_edges/pallas_call | solution.py:437
  43.4 2.3 %collective-permute-done.from_left.el = f32[22,16,256]{2,1,0:T(8,128)S(1)} collective-permute-done((f32[22,16,256]{2,1,0:T(8,128)S(1)}, f32[22,16,256]{2,1,0:T(8,128)S(1)}, u32[]{:S(2)}, u32[]{:S(2)}) %collective-permute-start) | collective-permute-done | bytes 360480 | tf_op jit(solution)/shard_map/ppermute | solution.py:429
  45.7 9.9 %collective-permute-start.11 = (f32[3,32,128]{2,1,0:T(8,128)S(1)}, f32[3,32,128]{2,1,0:T(8,128)S(1)}, u32[]{:S(2)}, u32[]{:S(2)}) collective-permute-start(f32[3,32,128]{2,1,0:T(8,128)S(1)} %get-tuple-element.39), channel_id=1, source_target_pairs={{0,0},{1,2},{2,1},{3,3},{4,4},{5,6},{6,5},{7,7},{8,8},{9,10},{10,9... | collective-permute-start | bytes 147464 | tf_op jit(solution)/shard_map/ppermute | solution.py:446
  55.7 1.2 %pack_y.1 = (f32[92,8,256]{2,1,0:T(8,128)}, f32[92,8,256]{2,1,0:T(8,128)}) custom-call(f32[16,64,256]{2,1,0:T(8,128)S(1)} %copy-done, f32[16,64,256]{2,1,0:T(8,128)S(1)} %copy-done.1, f32[16,64,256]{2,1,0:T(8,128)S(1)} %copy-done.2, f32[22,16,256]{2,1,0:T(8,128)S(1)} %collective-permute-done.from_left.el, f32[22,16,256]{2,1,0:T(8,128)S(1)} %collective-permute-done.1.from_right.er), custom_call_target="tpu_custom_call" | custom-call | tf_op jit(solution)/shard_map/pack_y/pallas_call | solution.py:469
  56.9 0.1 collective-permute-start.6
  57.0 0.4 collective-permute-done.11.recv_b
  57.4 4.0 %collective-permute-start.7 = (f32[92,8,256]{2,1,0:T(8,128)}, f32[92,8,256]{2,1,0:T(8,128)}, u32[]{:S(2)}, u32[]{:S(2)}) collective-permute-start(f32[92,8,256]{2,1,0:T(8,128)} %get-tuple-element.33), channel_id=1, source_target_pairs={{0,0},{1,2},{2,1},{3,3},{4,4},{5,6},{6,5},{7,7},{8,8},{9,10},{10,9... | collective-permute-start | bytes 2261000 | tf_op jit(solution)/shard_map/ppermute | solution.py:479
  61.5 1.1 band_steps.1
  62.6 0.0 copy-start.11
  62.7 21.3 %all_to_all.10 = f32[16,64,128]{2,1,0:T(8,128)S(1)} all-to-all(f32[16,64,128]{2,1,0:T(8,128)S(1)} %broadcast_in_dim.11), channel_id=1, replica_groups=mesh['sec'=4,'gx'=16,'gy'=4] {'gx'}, dimensions={0} | all-to-all | bytes 1048576 | tf_op jit(solution)/shard_map/all_to_all | solution.py:457
  84.0 2.9 %pick.1 = f32[16,8,128]{2,1,0:T(8,128)S(1)} custom-call(f32[128,8,128]{2,1,0:T(8,128)S(1)} %bitcast.8, s32[16,128]{1,0:T(8,128)S(1)} %bitcast.15), custom_call_target="tpu_custom_call" | custom-call | tf_op jit(solution)/shard_map/pick/pallas_call | solution.py:459
  86.9 0.6 copy-done.9
  87.5 3.9 %all-to-all-start.1 = ((f32[4,32,128]{2,1,0:T(8,128)}), f32[4,32,128]{2,1,0:T(8,128)}, u32[]{:S(2)}, u32[]{:S(2)}) async-start(f32[4,32,128]{2,1,0:T(8,128)} %bitcast.13), calls=%async_computation.1 | async-start | bytes 131072 | tf_op jit(solution)/shard_map/all_to_all | solution.py:467
  91.5 0.9 copy-done.5
  92.4 0.9 copy-done.7
  93.3 7.5 %columns.1 = (f32[64,512]{1,0:T(8,128)}, f32[8,512]{1,0:T(8,128)S(1)}) custom-call(s32[8]{0:T(128)S(1)} %copy-done.13, f32[8,16]{1,0:T(8,128)S(1)} %copy-done.11, f32[8,16]{1,0:T(8,128)S(1)} %copy-done.12, s32[64,512]{1,0:T(8,128)S(1)} %bitcast.9, f32[64,512]{1,0:T(8,128)S(1)} %bitcast.11), custom_call_target="tpu_custom_call" | custom-call | tf_op jit(solution)/shard_map/columns/pallas_call | solution.py:485
  100.8 0.9 copy-done.6
  101.7 0.9 copy-done.8
  102.6 2.4 %last_rows.1 = f32[64,512]{1,0:T(8,128)} custom-call(s32[8]{0:T(128)S(1)} %copy-done.13, f32[8,16]{1,0:T(8,128)S(1)} %copy-done.11, f32[8,16]{1,0:T(8,128)S(1)} %copy-done.12, s32[64,512]{1,0:T(8,128)S(1)} %bitcast.10, f32[64,512]{1,0:T(8,128)S(1)} %bitcast.12, f32[8,512]{1,0:T(8,128)S(1)} %get-tuple-element.34.edge, ...), custom_call_target="tpu_custom_call", output_to_operand_aliasing={{}: (7, {})} | custom-call | tf_op jit(solution)/shard_map/last_rows/pallas_call | solution.py:497
  105.0 1.0 copy-done.4
  106.0 12.9 %region.1 = f32[16,64,256]{2,1,0:T(8,128)} custom-call(f32[16,64,256]{2,1,0:T(8,128)S(1)} %copy-done, f32[16,64,256]{2,1,0:T(8,128)S(1)} %copy-done.1, f32[16,64,256]{2,1,0:T(8,128)S(1)} %copy-done.2, f32[22,16,256]{2,1,0:T(8,128)S(1)} %collective-permute-done.from_left.el, f32[22,16,256]{2,1,0:T(8,128)S(1)} %copy-done.4, ...), custom_call_target="tpu_custom_call" | custom-call | tf_op jit(solution)/shard_map/region/pallas_call | solution.py:508
  (40 shorter events, 0.1 us)
Async XLA Ops:
  0.6 8.1 %copy-start.2 = (f32[16,64,256]{2,1,0:T(8,128)S(1)}, f32[16,64,256]{2,1,0:T(8,128)}, u32[]{:S(2)}) copy-start(f32[16,64,256]{2,1,0:T(8,128)} %c.4) | copy-start | bytes 3145732
  0.6 8.0 %copy-start.1 = (f32[16,64,256]{2,1,0:T(8,128)S(1)}, f32[16,64,256]{2,1,0:T(8,128)}, u32[]{:S(2)}) copy-start(f32[16,64,256]{2,1,0:T(8,128)} %p.4) | copy-start | bytes 3145732
  0.7 8.0 %copy-start = (f32[16,64,256]{2,1,0:T(8,128)S(1)}, f32[16,64,256]{2,1,0:T(8,128)}, u32[]{:S(2)}) copy-start(f32[16,64,256]{2,1,0:T(8,128)} %u.4) | copy-start | bytes 3145732
  0.7 2.9 %copy-start.14 = (s32[1,512]{1,0:T(1,128)S(1)}, s32[1,512]{1,0:T(1,128)}, u32[]{:S(2)}) copy-start(s32[1,512]{1,0:T(1,128)} %param.13) | copy-start | bytes 6148
  8.7 7.3 %copy-start.16 = (f32[24,8,128]{2,1,0:T(8,128)S(1)}, f32[24,8,128]{2,1,0:T(8,128)}, u32[]{:S(2)}) copy-start(f32[24,8,128]{2,1,0:T(8,128)} %get-tuple-element.36) | copy-start | bytes 294916
  8.7 11.2 %copy-start.15 = (f32[24,8,128]{2,1,0:T(8,128)S(1)}, f32[24,8,128]{2,1,0:T(8,128)}, u32[]{:S(2)}) copy-start(f32[24,8,128]{2,1,0:T(8,128)} %get-tuple-element.22) | copy-start | bytes 294916
  8.7 32.4 %copy-start.10 = (f32[48,8,128]{2,1,0:T(8,128)S(1)}, f32[48,8,128]{2,1,0:T(8,128)}, u32[]{:S(2)}) copy-start(f32[48,8,128]{2,1,0:T(8,128)} %get-tuple-element.35.band) | copy-start | bytes 589828
  10.4 29.4 %collective-permute-start.4 = (f32[22,48,256]{2,1,0:T(8,128)S(1)}, f32[22,48,256]{2,1,0:T(8,128)}, u32[]{:S(2)}, u32[]{:S(2)}) collective-permute-start(f32[22,48,256]{2,1,0:T(8,128)S(1)} %get-tuple-element.31), channel_id=1, source_target_pairs={{60,12},{0,48},{61,45},{1,17},{62,14},{2,50},{63,47},{3,19},{124,7... | collective-permute-start | bytes 3244040 | tf_op jit(solution)/shard_map/ppermute | solution.py:432
  16.0 11.0 %collective-permute-start.9 = (f32[24,8,128]{2,1,0:T(8,128)S(1)}, f32[24,8,128]{2,1,0:T(8,128)S(1)}, u32[]{:S(2)}, u32[]{:S(2)}) collective-permute-start(f32[24,8,128]{2,1,0:T(8,128)S(1)} %copy-done.16), channel_id=1, source_target_pairs={{0,252},{4,0},{8,4},{12,8},{16,12},{20,16},{24,20},{28,24},{32,28}... | collective-permute-start | bytes 294920 | tf_op jit(solution)/shard_map/ppermute | solution.py:415
  19.9 18.6 %collective-permute-start.8 = (f32[24,8,128]{2,1,0:T(8,128)S(1)}, f32[24,8,128]{2,1,0:T(8,128)S(1)}, u32[]{:S(2)}, u32[]{:S(2)}) collective-permute-start(f32[24,8,128]{2,1,0:T(8,128)S(1)} %copy-done.15), channel_id=1, source_target_pairs={{0,4},{4,8},{8,12},{12,16},{16,20},{20,24},{24,28},{28,32},{32,36}... | collective-permute-start | bytes 294920 | tf_op jit(solution)/shard_map/ppermute | solution.py:414
  19.9 25.8 %collective-permute-start = (f32[22,16,256]{2,1,0:T(8,128)S(1)}, f32[22,16,256]{2,1,0:T(8,128)S(1)}, u32[]{:S(2)}, u32[]{:S(2)}) collective-permute-start(f32[22,16,256]{2,1,0:T(8,128)S(1)} %get-tuple-element.27), channel_id=1, source_target_pairs={{0,4},{4,8},{8,12},{12,16},{16,20},{20,24},{24,28},{28,32},{32,36}... | collective-permute-start | bytes 1081352 | tf_op jit(solution)/shard_map/ppermute | solution.py:429
  19.9 25.8 %collective-permute-start.1 = (f32[22,16,256]{2,1,0:T(8,128)S(1)}, f32[22,16,256]{2,1,0:T(8,128)S(1)}, u32[]{:S(2)}, u32[]{:S(2)}) collective-permute-start(f32[22,16,256]{2,1,0:T(8,128)S(1)} %get-tuple-element.28), channel_id=1, source_target_pairs={{0,252},{4,0},{8,4},{12,8},{16,12},{20,16},{24,20},{28,24},{32,28}... | collective-permute-start | bytes 1081352 | tf_op jit(solution)/shard_map/ppermute | solution.py:430
  27.1 77.9 %collective-permute-start.2 = (f32[22,48,256]{2,1,0:T(8,128)}, f32[22,48,256]{2,1,0:T(8,128)}, u32[]{:S(2)}, u32[]{:S(2)}) collective-permute-start(f32[22,48,256]{2,1,0:T(8,128)} %get-tuple-element.29), channel_id=1, source_target_pairs={{0,4},{4,8},{8,12},{12,16},{16,20},{20,24},{24,28},{28,32},{32,36}... | collective-permute-start | bytes 3244040 | tf_op jit(solution)/shard_map/ppermute | solution.py:433
  38.5 66.5 %collective-permute-start.3 = (f32[22,48,256]{2,1,0:T(8,128)}, f32[22,48,256]{2,1,0:T(8,128)}, u32[]{:S(2)}, u32[]{:S(2)}) collective-permute-start(f32[22,48,256]{2,1,0:T(8,128)} %get-tuple-element.30), channel_id=1, source_target_pairs={{4,0},{8,4},{12,8},{16,12},{20,16},{24,20},{28,24},{32,28},{36,32}... | collective-permute-start | bytes 3244040 | tf_op jit(solution)/shard_map/ppermute | solution.py:434
  39.8 65.2 %collective-permute-start.5 = (f32[22,48,256]{2,1,0:T(8,128)}, f32[22,48,256]{2,1,0:T(8,128)}, u32[]{:S(2)}, u32[]{:S(2)}) collective-permute-start(f32[22,48,256]{2,1,0:T(8,128)} %collective-permute-done.4), channel_id=1, source_target_pairs={{12,64},{45,65},{14,66},{47,67},{76,128},{112,60},{109,129},{81,61... | collective-permute-start | bytes 3244040 | tf_op jit(solution)/shard_map/ppermute | solution.py:435
  45.7 11.2 %collective-permute-start.10 = (f32[3,32,128]{2,1,0:T(8,128)S(1)}, f32[3,32,128]{2,1,0:T(8,128)S(1)}, u32[]{:S(2)}, u32[]{:S(2)}) collective-permute-start(f32[3,32,128]{2,1,0:T(8,128)S(1)} %get-tuple-element.38), channel_id=1, source_target_pairs={{0,1},{1,0},{2,3},{3,2},{4,5},{5,4},{6,7},{7,6},{8,9},{9,8},{10,11... | collective-permute-start | bytes 147464 | tf_op jit(solution)/shard_map/ppermute | solution.py:445
  45.7 11.2 %copy-start.3 = (f32[22,16,256]{2,1,0:T(8,128)}, f32[22,16,256]{2,1,0:T(8,128)S(1)}, u32[]{:S(2)}) copy-start(f32[22,16,256]{2,1,0:T(8,128)S(1)} %collective-permute-done.1.from_right.er) | copy-start | bytes 1081348
  45.7 11.7 %collective-permute-start.11 = (f32[3,32,128]{2,1,0:T(8,128)S(1)}, f32[3,32,128]{2,1,0:T(8,128)S(1)}, u32[]{:S(2)}, u32[]{:S(2)}) collective-permute-start(f32[3,32,128]{2,1,0:T(8,128)S(1)} %get-tuple-element.39), channel_id=1, source_target_pairs={{0,0},{1,2},{2,1},{3,3},{4,4},{5,6},{6,5},{7,7},{8,8},{9,10},{10,9... | collective-permute-start | bytes 147464 | tf_op jit(solution)/shard_map/ppermute | solution.py:446
  56.9 48.1 %collective-permute-start.6 = (f32[92,8,256]{2,1,0:T(8,128)}, f32[92,8,256]{2,1,0:T(8,128)}, u32[]{:S(2)}, u32[]{:S(2)}) collective-permute-start(f32[92,8,256]{2,1,0:T(8,128)} %get-tuple-element.32), channel_id=1, source_target_pairs={{0,1},{1,0},{2,3},{3,2},{4,5},{5,4},{6,7},{7,6},{8,9},{9,8},{10,11... | collective-permute-start | bytes 2261000 | tf_op jit(solution)/shard_map/ppermute | solution.py:478
  57.4 47.6 %collective-permute-start.7 = (f32[92,8,256]{2,1,0:T(8,128)}, f32[92,8,256]{2,1,0:T(8,128)}, u32[]{:S(2)}, u32[]{:S(2)}) collective-permute-start(f32[92,8,256]{2,1,0:T(8,128)} %get-tuple-element.33), channel_id=1, source_target_pairs={{0,0},{1,2},{2,1},{3,3},{4,4},{5,6},{6,5},{7,7},{8,8},{9,10},{10,9... | collective-permute-start | bytes 2261000 | tf_op jit(solution)/shard_map/ppermute | solution.py:479
  62.6 28.8 %copy-start.11 = (f32[8,16]{1,0:T(8,128)S(1)}, f32[8,16]{1,0:T(8,128)}, u32[]{:S(2)}) copy-start(f32[8,16]{1,0:T(8,128)} %modulus.3) | copy-start | bytes 1540
  62.6 28.8 %copy-start.12 = (f32[8,16]{1,0:T(8,128)S(1)}, f32[8,16]{1,0:T(8,128)}, u32[]{:S(2)}) copy-start(f32[8,16]{1,0:T(8,128)} %yields.3) | copy-start | bytes 1540
  62.6 28.8 %copy-start.13 = (s32[8]{0:T(128)S(1)}, s32[8]{0:T(128)}, u32[]{:S(2)}) copy-start(s32[8]{0:T(128)} %count.3) | copy-start | bytes 100
  86.9 0.6 copy-start.9
  87.5 13.3 %all-to-all-start.1 = ((f32[4,32,128]{2,1,0:T(8,128)}), f32[4,32,128]{2,1,0:T(8,128)}, u32[]{:S(2)}, u32[]{:S(2)}) async-start(f32[4,32,128]{2,1,0:T(8,128)} %bitcast.13), calls=%async_computation.1 | async-start | bytes 131072 | tf_op jit(solution)/shard_map/all_to_all | solution.py:467
  91.5 0.9 copy-start.5
  92.4 0.9 copy-start.7
  100.8 0.9 copy-start.6
  101.7 0.9 copy-start.8
  105.0 1.0 copy-start.4

commit v3 on v2

--- a/solution.py
+++ b/solution.py
@@ -428,10 +428,29 @@
     )(*regional)
     edge_from_left = lax.ppermute(edge_right, XAX, right)
     edge_from_right = lax.ppermute(edge_left, XAX, left)
-    relay_out, relay_in = relays(lax.axis_size("sec"), n_gx)
-    mid_relay = lax.ppermute(mid_far, ALL, relay_out)
     mid_from_left = lax.ppermute(mid_right, "gx", [(i, i + 1) for i in range(n_gx - 1)])
     mid_from_right = lax.ppermute(mid_left, "gx", [(i + 1, i) for i in range(n_gx - 1)])
+
+    soil = soil_class[0]
+    start = basin_disp[0]
+    soil, start, _ = lax.optimization_barrier((soil, start, index))
+    tables = (spring_count, spring_modulus, spring_yield)
+    block = pl.BlockSpec((64, 256), lambda i: (0, i))
+    upper, edge = pl.pallas_call(
+        columns_kernel,
+        grid=(2,),
+        out_shape=(sds(64, 512), sds(8, 512)),
+        in_specs=[SM] * 3 + [block] * 2,
+        out_specs=(block, pl.BlockSpec((8, 256), lambda i: (0, i))),
+        scratch_shapes=[pltpu.VMEM((16, 64, 256), F32)] * 3,
+        compiler_params=PARAMS,
+        name="columns",
+    )(*tables, soil, start)
+
+    upper, band_from_left, band_from_right = lax.optimization_barrier((upper, band_from_left, band_from_right))
+    relay_out, relay_in = relays(lax.axis_size("sec"), n_gx)
+    mid_far, band_from_left, band_from_right = lax.optimization_barrier((mid_far, band_from_left, band_from_right))
+    mid_relay = lax.ppermute(mid_far, ALL, relay_out)
     mid_relay = lax.ppermute(mid_relay, ALL, relay_in)
 
     ext, band_a, band_b = pl.pallas_call(
@@ -456,16 +475,7 @@
 
     table = lax.all_to_all(jnp.broadcast_to(trace.reshape(1, 64, 128), (n_gx, 64, 128)), "gx", 0, 0)
     table = table.reshape(n_gx * 8, 8, 128)
-    picked = pl.pallas_call(
-        pick_kernel,
-        out_shape=sds(16, 8, 128),
-        in_specs=[VM] * 2,
-        out_specs=VM,
-        compiler_params=PARAMS,
-        name="pick",
-    )(table, index)
-    arrived = lax.all_to_all(picked.reshape(4, 32, 128), "gy", 0, 0)
-
+    table, edge_from_left, edge_from_right = lax.optimization_barrier((table, edge_from_left, edge_from_right))
     y_a, y_b = pl.pallas_call(
         pack_y_kernel,
         out_shape=(sds(92, 8, 256), sds(92, 8, 256)),
@@ -475,23 +485,19 @@
         compiler_params=PARAMS,
         name="pack_y",
     )(*regional, edge_from_left, edge_from_right)
+    table, y_a, y_b = lax.optimization_barrier((table, y_a, y_b))
     y_a = lax.ppermute(y_a, "gy", swap_a)
     y_b = lax.ppermute(y_b, "gy", swap_b)
 
-    soil = soil_class[0]
-    start = basin_disp[0]
-    tables = (spring_count, spring_modulus, spring_yield)
-    block = pl.BlockSpec((64, 256), lambda i: (0, i))
-    upper, edge = pl.pallas_call(
-        columns_kernel,
-        grid=(2,),
-        out_shape=(sds(64, 512), sds(8, 512)),
-        in_specs=[SM] * 3 + [block] * 2,
-        out_specs=(block, pl.BlockSpec((8, 256), lambda i: (0, i))),
-        scratch_shapes=[pltpu.VMEM((16, 64, 256), F32)] * 3,
-        compiler_params=PARAMS,
-        name="columns",
-    )(*tables, soil, start)
+    picked = pl.pallas_call(
+        pick_kernel,
+        out_shape=sds(16, 8, 128),
+        in_specs=[VM] * 2,
+        out_specs=VM,
+        compiler_params=PARAMS,
+        name="pick",
+    )(table, index)
+    arrived = lax.all_to_all(picked.reshape(4, 32, 128), "gy", 0, 0)
 
     tail = pl.BlockSpec((8, 512), lambda i: (7, 0))
     basin = pl.pallas_call(

time: 120 us -> 114 us (0.950)
  the two profiles are of different devices: /device:TPU:224 before, /device:TPU:4 now
where the time goes in v3:
time: 114 us; the launch traced here: 113 us
  starting transfers between devices  59 us (52%)
  Pallas kernels  33.5 us (29%)
  blocking collectives  14.4 us (13%)
  local copies, waits for them, and re-layouts  2.95 us (3%)
  waiting for transfers between devices  2.18 us (2%)
    ppermute x1, starting transfers between devices, shards(): y_a = lax.ppermute(y_a, 'gy', swap_a)  25.1 us
    all_to_all x1, starting transfers between devices, shards(): lax.all_to_all(jnp.broadcast_to(trace.reshape(1, 64, 128), (n_gx, 64, 128...  13.7 us
    pallas_call x1, Pallas kernels, shards(): pl.pallas_call(region_kernel, out_shape=sds(16, 64, 256), in_specs=[ANY]...  12.6 us
    all_to_all x1, blocking collectives, shards(): arrived = lax.all_to_all(picked.reshape(4, 32, 128), 'gy', 0, 0)  9.22 us
    pallas_call x1, Pallas kernels, shards(): pl.pallas_call(columns_kernel, grid=(2,), out_shape=(sds(64, 512), sds(8,...  7.53 us
    ppermute x1, starting transfers between devices, shards(): lax.ppermute(mid_left, 'gx', [(i + 1, i) for i in range(n_gx - 1)])  6.03 us
    all_gather x1, blocking collectives, shards(): index = lax.all_gather(index, 'gy').reshape(16, 128)  5.15 us
    pallas_call x1, Pallas kernels, shards(): pl.pallas_call(pick_kernel, out_shape=sds(16, 8, 128), in_specs=[VM] * 2,...  3.92 us
  transfers between devices with their start and end apart: 13, of which 2 were waited for; matrix products, arithmetic and copies ran while one was open for 1% of the time, Pallas kernels for 16%

profile of v3, /device:TPU:4, one launch (start us, length us, event | category | flops | bytes accessed | tf_op | source)
XLA Modules:
  0.0 113.0 jit_solution(1032163770800001951)
XLA Ops:
  0.7 2.9 %band.1 = (f32[48,8,128]{2,1,0:T(8,128)}, f32[24,8,128]{2,1,0:T(8,128)}, f32[24,8,128]{2,1,0:T(8,128)}) custom-call(f32[16,64,256]{2,1,0:T(8,128)} %u.4, f32[16,64,256]{2,1,0:T(8,128)} %p.4, f32[16,64,256]{2,1,0:T(8,128)} %c.4), custom_call_target="tpu_custom_call" | custom-call | tf_op jit(solution)/shard_map/band/pallas_call | solution.py:405
  3.5 3.0 %collective-permute-start.1 = (f32[24,8,128]{2,1,0:T(8,128)}, f32[24,8,128]{2,1,0:T(8,128)S(1)}, u32[]{:S(2)}, u32[]{:S(2)}) collective-permute-start(f32[24,8,128]{2,1,0:T(8,128)} %get-tuple-element.47), channel_id=1, source_target_pairs={{0,252},{4,0},{8,4},{12,8},{16,12},{20,16},{24,20},{28,24},{32,28}... | collective-permute-start | bytes 294920 | tf_op jit(solution)/shard_map/ppermute | solution.py:415
  6.5 5.2 %all-gather = s32[4,4,128]{2,1,0:T(4,128)S(1)} all-gather(s32[1,4,128]{2,1,0:T(4,128)S(1)} %bitcast.16), channel_id=2, replica_groups=mesh['sec'=4,'gx'=16,'gy'=4] {'gy'}, dimensions={0}, use_global_device_ids=true | all-gather | bytes 10240 | tf_op jit(solution)/shard_map/all_gather | solution.py:417
  11.7 0.0 copy-start.8
  11.7 0.0 copy-start.11
  11.8 0.6 pack_x.1
  12.3 0.3 copy-done.6
  12.6 0.1 copy-done.8
  12.7 7.5 %columns.1 = (f32[64,512]{1,0:T(8,128)}, f32[8,512]{1,0:T(8,128)S(1)}) custom-call(s32[8]{0:T(128)S(1)} %copy-done.13, f32[8,16]{1,0:T(8,128)S(1)} %copy-done.11, f32[8,16]{1,0:T(8,128)S(1)} %copy-done.12, s32[64,512]{1,0:T(8,128)S(1)} %bitcast.8, f32[64,512]{1,0:T(8,128)S(1)} %bitcast.10), custom_call_target="tpu_custom_call" | custom-call | tf_op jit(solution)/shard_map/columns/pallas_call | solution.py:439
  20.2 1.7 %collective-permute-start.8 = (f32[22,48,256]{2,1,0:T(8,128)}, f32[22,48,256]{2,1,0:T(8,128)}, u32[]{:S(2)}, u32[]{:S(2)}) collective-permute-start(f32[22,48,256]{2,1,0:T(8,128)} %get-tuple-element.61), channel_id=1, source_target_pairs={{60,12},{0,48},{61,45},{1,17},{62,14},{2,50},{63,47},{3,19},{124,7... | collective-permute-start | bytes 3244040 | tf_op jit(solution)/shard_map/ppermute | solution.py:453
  21.9 2.3 %band_edges.1 = (f32[48,32,128]{2,1,0:T(8,128)S(1)}, f32[3,32,128]{2,1,0:T(8,128)S(1)}, f32[3,32,128]{2,1,0:T(8,128)S(1)}) custom-call(f32[48,8,128]{2,1,0:T(8,128)S(1)} %copy-done.10, f32[24,8,128]{2,1,0:T(8,128)S(1)} %collective-permute-done.from_left, f32[24,8,128]{2,1,0:T(8,128)S(1)} %collective-permute-done.1.from_right), custom_call_target="tpu_custom_call" | custom-call | tf_op jit(solution)/shard_map/band_edges/pallas_call | solution.py:456
  24.2 0.4 collective-permute-start.2
  24.6 0.7 collective-permute-start.3
  25.3 0.3 collective-permute-done.2.recv_a
  25.6 1.2 %band_steps.1 = f32[8,8,128]{2,1,0:T(8,128)S(1)} custom-call(f32[48,32,128]{2,1,0:T(8,128)S(1)} %get-tuple-element.52.ext, f32[3,32,128]{2,1,0:T(8,128)S(1)} %collective-permute-done.2.recv_a, f32[3,32,128]{2,1,0:T(8,128)S(1)} %collective-permute-done.3.recv_b), custom_call_target="tpu_custom_call" | custom-call | tf_op jit(solution)/shard_map/band_steps/pallas_call | solution.py:466
  26.7 0.8 broadcast_in_dim.11
  27.6 13.7 %all-to-all-start = ((f32[16,64,128]{2,1,0:T(8,128)}), f32[16,64,128]{2,1,0:T(8,128)}, u32[]{:S(2)}, u32[]{:S(2)}) async-start(f32[16,64,128]{2,1,0:T(8,128)} %broadcast_in_dim.11), calls=%async_computation | async-start | bytes 1048576 | tf_op jit(solution)/shard_map/all_to_all | solution.py:476
  41.3 1.5 %collective-permute-start.4 = (f32[22,16,256]{2,1,0:T(8,128)}, f32[22,16,256]{2,1,0:T(8,128)S(1)}, u32[]{:S(2)}, u32[]{:S(2)}) collective-permute-start(f32[22,16,256]{2,1,0:T(8,128)} %copy-done.17), channel_id=1, source_target_pairs={{0,4},{4,8},{8,12},{12,16},{16,20},{20,24},{24,28},{28,32},{32,36}... | collective-permute-start | bytes 1081352 | tf_op jit(solution)/shard_map/ppermute | solution.py:429
  42.8 2.7 %collective-permute-start.5 = (f32[22,16,256]{2,1,0:T(8,128)}, f32[22,16,256]{2,1,0:T(8,128)S(1)}, u32[]{:S(2)}, u32[]{:S(2)}) collective-permute-start(f32[22,16,256]{2,1,0:T(8,128)} %copy-done.16), channel_id=1, source_target_pairs={{0,252},{4,0},{8,4},{12,8},{16,12},{20,16},{24,20},{28,24},{32,28}... | collective-permute-start | bytes 1081352 | tf_op jit(solution)/shard_map/ppermute | solution.py:430
  45.4 1.9 %collective-permute-start.6 = (f32[22,48,256]{2,1,0:T(8,128)}, f32[22,48,256]{2,1,0:T(8,128)}, u32[]{:S(2)}, u32[]{:S(2)}) collective-permute-start(f32[22,48,256]{2,1,0:T(8,128)} %copy-done.15), channel_id=1, source_target_pairs={{0,4},{4,8},{8,12},{12,16},{16,20},{20,24},{24,28},{28,32},{32,36}... | collective-permute-start | bytes 3244040 | tf_op jit(solution)/shard_map/ppermute | solution.py:431
  47.3 6.0 %collective-permute-start.7 = (f32[22,48,256]{2,1,0:T(8,128)}, f32[22,48,256]{2,1,0:T(8,128)}, u32[]{:S(2)}, u32[]{:S(2)}) collective-permute-start(f32[22,48,256]{2,1,0:T(8,128)} %copy-done.14), channel_id=1, source_target_pairs={{4,0},{8,4},{12,8},{16,12},{20,16},{24,20},{28,24},{32,28},{36,32}... | collective-permute-start | bytes 3244040 | tf_op jit(solution)/shard_map/ppermute | solution.py:432
  53.4 1.7 %collective-permute-start.9 = (f32[22,48,256]{2,1,0:T(8,128)}, f32[22,48,256]{2,1,0:T(8,128)}, u32[]{:S(2)}, u32[]{:S(2)}) collective-permute-start(f32[22,48,256]{2,1,0:T(8,128)} %collective-permute-done.8), channel_id=1, source_target_pairs={{12,64},{45,65},{14,66},{47,67},{76,128},{112,60},{109,129},{81,61... | collective-permute-start | bytes 3244040 | tf_op jit(solution)/shard_map/ppermute | solution.py:454
  55.0 1.9 %collective-permute-done.4.from_left.el = f32[22,16,256]{2,1,0:T(8,128)S(1)} collective-permute-done((f32[22,16,256]{2,1,0:T(8,128)}, f32[22,16,256]{2,1,0:T(8,128)S(1)}, u32[]{:S(2)}, u32[]{:S(2)}) %collective-permute-start.4) | collective-permute-done | bytes 360480 | tf_op jit(solution)/shard_map/ppermute | solution.py:429
  56.9 0.7 copy-done.3
  57.7 1.0 copy-done.4
  58.7 0.3 pack_y.1
  59.0 25.1 %collective-permute-start.10 = (f32[92,8,256]{2,1,0:T(8,128)S(1)}, f32[92,8,256]{2,1,0:T(8,128)S(1)}, u32[]{:S(2)}, u32[]{:S(2)}) collective-permute-start(f32[92,8,256]{2,1,0:T(8,128)S(1)} %get-tuple-element.65), channel_id=1, source_target_pairs={{0,1},{1,0},{2,3},{3,2},{4,5},{5,4},{6,7},{7,6},{8,9},{9,8},{10,11... | collective-permute-start | bytes 2261000 | tf_op jit(solution)/shard_map/ppermute | solution.py:489
  84.1 0.7 collective-permute-start.11
  84.8 3.9 %pick.1 = f32[16,8,128]{2,1,0:T(8,128)S(1)} custom-call(f32[128,8,128]{2,1,0:T(8,128)} %bitcast.5.table, s32[16,128]{1,0:T(8,128)S(1)} %bitcast.14), custom_call_target="tpu_custom_call" | custom-call | tf_op jit(solution)/shard_map/pick/pallas_call | solution.py:492
  88.8 9.2 %all_to_all.10.arrived = f32[4,32,128]{2,1,0:T(8,128)S(1)} all-to-all(f32[4,32,128]{2,1,0:T(8,128)S(1)} %bitcast.12), channel_id=1, replica_groups=mesh['sec'=4,'gx'=16,'gy'=4] {'gy'}, dimensions={0} | all-to-all | bytes 131072 | tf_op jit(solution)/shard_map/all_to_all | solution.py:500
  98.0 2.2 %last_rows.1 = f32[64,512]{1,0:T(8,128)} custom-call(s32[8]{0:T(128)S(1)} %copy-done.13, f32[8,16]{1,0:T(8,128)S(1)} %copy-done.11, f32[8,16]{1,0:T(8,128)S(1)} %copy-done.12, s32[64,512]{1,0:T(8,128)S(1)} %bitcast.9, f32[64,512]{1,0:T(8,128)S(1)} %bitcast.11, f32[8,512]{1,0:T(8,128)S(1)} %get-tuple-element.67.edge, ...), custom_call_target="tpu_custom_call", output_to_operand_aliasing={{}: (7, {})} | custom-call | tf_op jit(solution)/shard_map/last_rows/pallas_call | solution.py:503
  100.3 12.6 %region.1 = f32[16,64,256]{2,1,0:T(8,128)} custom-call(f32[16,64,256]{2,1,0:T(8,128)S(1)} %copy-done, f32[16,64,256]{2,1,0:T(8,128)S(1)} %copy-done.1, f32[16,64,256]{2,1,0:T(8,128)S(1)} %copy-done.2, f32[22,16,256]{2,1,0:T(8,128)S(1)} %collective-permute-done.4.from_left.el, f32[22,16,256]{2,1,0:T(8,128)S(1)} %copy-done.5, ...), custom_call_target="tpu_custom_call" | custom-call | tf_op jit(solution)/shard_map/region/pallas_call | solution.py:514
  (44 shorter events, 0.1 us)
Async XLA Ops:
  0.6 11.1 %copy-start.2 = (f32[16,64,256]{2,1,0:T(8,128)S(1)}, f32[16,64,256]{2,1,0:T(8,128)}, u32[]{:S(2)}) copy-start(f32[16,64,256]{2,1,0:T(8,128)} %c.4) | copy-start | bytes 3145732
  0.6 11.0 %copy-start.1 = (f32[16,64,256]{2,1,0:T(8,128)S(1)}, f32[16,64,256]{2,1,0:T(8,128)}, u32[]{:S(2)}) copy-start(f32[16,64,256]{2,1,0:T(8,128)} %p.4) | copy-start | bytes 3145732
  0.7 11.0 %copy-start = (f32[16,64,256]{2,1,0:T(8,128)S(1)}, f32[16,64,256]{2,1,0:T(8,128)}, u32[]{:S(2)}) copy-start(f32[16,64,256]{2,1,0:T(8,128)} %u.4) | copy-start | bytes 3145732
  0.7 5.9 %copy-start.18 = (s32[1,512]{1,0:T(1,128)S(1)}, s32[1,512]{1,0:T(1,128)}, u32[]{:S(2)}) copy-start(s32[1,512]{1,0:T(1,128)} %param.13) | copy-start | bytes 6148
  3.5 16.7 %collective-permute-start.1 = (f32[24,8,128]{2,1,0:T(8,128)}, f32[24,8,128]{2,1,0:T(8,128)S(1)}, u32[]{:S(2)}, u32[]{:S(2)}) collective-permute-start(f32[24,8,128]{2,1,0:T(8,128)} %get-tuple-element.47), channel_id=1, source_target_pairs={{0,252},{4,0},{8,4},{12,8},{16,12},{20,16},{24,20},{28,24},{32,28}... | collective-permute-start | bytes 294920 | tf_op jit(solution)/shard_map/ppermute | solution.py:415
  6.5 13.7 %collective-permute-start = (f32[24,8,128]{2,1,0:T(8,128)}, f32[24,8,128]{2,1,0:T(8,128)S(1)}, u32[]{:S(2)}, u32[]{:S(2)}) collective-permute-start(f32[24,8,128]{2,1,0:T(8,128)} %get-tuple-element.36), channel_id=1, source_target_pairs={{0,4},{4,8},{8,12},{12,16},{16,20},{20,24},{24,28},{28,32},{32,36}... | collective-permute-start | bytes 294920 | tf_op jit(solution)/shard_map/ppermute | solution.py:414
  11.7 0.9 copy-start.6
  11.7 1.0 copy-start.8
  11.7 1.0 copy-start.11
  11.7 0.9 copy-start.12
  11.7 0.9 copy-start.13
  11.7 10.2 %copy-start.10 = (f32[48,8,128]{2,1,0:T(8,128)S(1)}, f32[48,8,128]{2,1,0:T(8,128)}, u32[]{:S(2)}) copy-start(f32[48,8,128]{2,1,0:T(8,128)} %get-tuple-element.41.band) | copy-start | bytes 589828
  12.7 9.3 %copy-start.17 = (f32[22,16,256]{2,1,0:T(8,128)}, f32[22,16,256]{2,1,0:T(8,128)S(1)}, u32[]{:S(2)}) copy-start(f32[22,16,256]{2,1,0:T(8,128)S(1)} %get-tuple-element.55) | copy-start | bytes 1081348
  12.7 14.0 %copy-start.14 = (f32[22,48,256]{2,1,0:T(8,128)}, f32[22,48,256]{2,1,0:T(8,128)S(1)}, u32[]{:S(2)}) copy-start(f32[22,48,256]{2,1,0:T(8,128)S(1)} %get-tuple-element.60) | copy-start | bytes 3244036
  12.7 14.0 %copy-start.15 = (f32[22,48,256]{2,1,0:T(8,128)}, f32[22,48,256]{2,1,0:T(8,128)S(1)}, u32[]{:S(2)}) copy-start(f32[22,48,256]{2,1,0:T(8,128)S(1)} %get-tuple-element.59) | copy-start | bytes 3244036
  12.7 14.0 %copy-start.16 = (f32[22,16,256]{2,1,0:T(8,128)}, f32[22,16,256]{2,1,0:T(8,128)S(1)}, u32[]{:S(2)}) copy-start(f32[22,16,256]{2,1,0:T(8,128)S(1)} %get-tuple-element.56) | copy-start | bytes 1081348
  20.2 33.1 %collective-permute-start.8 = (f32[22,48,256]{2,1,0:T(8,128)}, f32[22,48,256]{2,1,0:T(8,128)}, u32[]{:S(2)}, u32[]{:S(2)}) collective-permute-start(f32[22,48,256]{2,1,0:T(8,128)} %get-tuple-element.61), channel_id=1, source_target_pairs={{60,12},{0,48},{61,45},{1,17},{62,14},{2,50},{63,47},{3,19},{124,7... | collective-permute-start | bytes 3244040 | tf_op jit(solution)/shard_map/ppermute | solution.py:453
  24.2 1.3 %collective-permute-start.2 = (f32[3,32,128]{2,1,0:T(8,128)S(1)}, f32[3,32,128]{2,1,0:T(8,128)S(1)}, u32[]{:S(2)}, u32[]{:S(2)}) collective-permute-start(f32[3,32,128]{2,1,0:T(8,128)S(1)} %get-tuple-element.53), channel_id=1, source_target_pairs={{0,1},{1,0},{2,3},{3,2},{4,5},{5,4},{6,7},{7,6},{8,9},{9,8},{10,11... | collective-permute-start | bytes 147464 | tf_op jit(solution)/shard_map/ppermute | solution.py:464
  24.6 0.9 collective-permute-start.3
  27.6 30.1 %all-to-all-start = ((f32[16,64,128]{2,1,0:T(8,128)}), f32[16,64,128]{2,1,0:T(8,128)}, u32[]{:S(2)}, u32[]{:S(2)}) async-start(f32[16,64,128]{2,1,0:T(8,128)} %broadcast_in_dim.11), calls=%async_computation | async-start | bytes 1048576 | tf_op jit(solution)/shard_map/all_to_all | solution.py:476
  41.3 15.6 %collective-permute-start.4 = (f32[22,16,256]{2,1,0:T(8,128)}, f32[22,16,256]{2,1,0:T(8,128)S(1)}, u32[]{:S(2)}, u32[]{:S(2)}) collective-permute-start(f32[22,16,256]{2,1,0:T(8,128)} %copy-done.17), channel_id=1, source_target_pairs={{0,4},{4,8},{8,12},{12,16},{16,20},{20,24},{24,28},{28,32},{32,36}... | collective-permute-start | bytes 1081352 | tf_op jit(solution)/shard_map/ppermute | solution.py:429
  42.8 14.2 %collective-permute-start.5 = (f32[22,16,256]{2,1,0:T(8,128)}, f32[22,16,256]{2,1,0:T(8,128)S(1)}, u32[]{:S(2)}, u32[]{:S(2)}) collective-permute-start(f32[22,16,256]{2,1,0:T(8,128)} %copy-done.16), channel_id=1, source_target_pairs={{0,252},{4,0},{8,4},{12,8},{16,12},{20,16},{24,20},{28,24},{32,28}... | collective-permute-start | bytes 1081352 | tf_op jit(solution)/shard_map/ppermute | solution.py:430
  45.4 54.8 %collective-permute-start.6 = (f32[22,48,256]{2,1,0:T(8,128)}, f32[22,48,256]{2,1,0:T(8,128)}, u32[]{:S(2)}, u32[]{:S(2)}) collective-permute-start(f32[22,48,256]{2,1,0:T(8,128)} %copy-done.15), channel_id=1, source_target_pairs={{0,4},{4,8},{8,12},{12,16},{16,20},{20,24},{24,28},{28,32},{32,36}... | collective-permute-start | bytes 3244040 | tf_op jit(solution)/shard_map/ppermute | solution.py:431
  47.3 52.9 %collective-permute-start.7 = (f32[22,48,256]{2,1,0:T(8,128)}, f32[22,48,256]{2,1,0:T(8,128)}, u32[]{:S(2)}, u32[]{:S(2)}) collective-permute-start(f32[22,48,256]{2,1,0:T(8,128)} %copy-done.14), channel_id=1, source_target_pairs={{4,0},{8,4},{12,8},{16,12},{20,16},{24,20},{28,24},{32,28},{36,32}... | collective-permute-start | bytes 3244040 | tf_op jit(solution)/shard_map/ppermute | solution.py:432
  53.4 46.9 %collective-permute-start.9 = (f32[22,48,256]{2,1,0:T(8,128)}, f32[22,48,256]{2,1,0:T(8,128)}, u32[]{:S(2)}, u32[]{:S(2)}) collective-permute-start(f32[22,48,256]{2,1,0:T(8,128)} %collective-permute-done.8), channel_id=1, source_target_pairs={{12,64},{45,65},{14,66},{47,67},{76,128},{112,60},{109,129},{81,61... | collective-permute-start | bytes 3244040 | tf_op jit(solution)/shard_map/ppermute | solution.py:454
  56.9 0.7 copy-start.3
  57.7 1.0 copy-start.4
  58.7 39.3 %copy-start.7 = (s32[1,64,512]{2,1,0:T(8,128)S(1)}, s32[1,64,512]{2,1,0:T(8,128)}, u32[]{:S(2)}) copy-start(s32[1,64,512]{2,1,0:T(8,128)} %param.14) | copy-start | bytes 393220
  58.7 39.3 %copy-start.9 = (f32[1,64,512]{2,1,0:T(8,128)S(1)}, f32[1,64,512]{2,1,0:T(8,128)}, u32[]{:S(2)}) copy-start(f32[1,64,512]{2,1,0:T(8,128)} %param.12) | copy-start | bytes 393220
  59.0 41.3 %copy-start.5 = (f32[22,16,256]{2,1,0:T(8,128)S(1)}, f32[22,16,256]{2,1,0:T(8,128)}, u32[]{:S(2)}) copy-start(f32[22,16,256]{2,1,0:T(8,128)} %copy-done.3) | copy-start | bytes 1081348
  59.0 41.2 %collective-permute-start.10 = (f32[92,8,256]{2,1,0:T(8,128)S(1)}, f32[92,8,256]{2,1,0:T(8,128)S(1)}, u32[]{:S(2)}, u32[]{:S(2)}) collective-permute-start(f32[92,8,256]{2,1,0:T(8,128)S(1)} %get-tuple-element.65), channel_id=1, source_target_pairs={{0,1},{1,0},{2,3},{3,2},{4,5},{5,4},{6,7},{7,6},{8,9},{9,8},{10,11... | collective-permute-start | bytes 2261000 | tf_op jit(solution)/shard_map/ppermute | solution.py:489
  84.1 16.1 %collective-permute-start.11 = (f32[92,8,256]{2,1,0:T(8,128)S(1)}, f32[92,8,256]{2,1,0:T(8,128)S(1)}, u32[]{:S(2)}, u32[]{:S(2)}) collective-permute-start(f32[92,8,256]{2,1,0:T(8,128)S(1)} %get-tuple-element.66), channel_id=1, source_target_pairs={{0,0},{1,2},{2,1},{3,3},{4,4},{5,6},{6,5},{7,7},{8,8},{9,10},{10,9... | collective-permute-start | bytes 2261000 | tf_op jit(solution)/shard_map/ppermute | solution.py:490

commit v4 on v3

--- a/solution.py
+++ b/solution.py
@@ -126,12 +126,12 @@
         trace[:, step - 1, :] = jnp.where(first, plane[0:8], pltpu.roll(plane[8:16], 64, 1))
 
 
-def pick_kernel(table, index, out):
+def pick_kernel(table, index, *outs):
     me = lax.axis_index("gy")
     count = table.shape[0]
 
-    def tile(t):
-        cell = jnp.broadcast_to(index[pl.ds(t, 1), :], (8, 128))
+    def tile(row):
+        cell = jnp.broadcast_to(index[pl.ds(row, 1), :], (8, 128))
         x, y = cell >> 8, cell & 255
         place = ((x >> 4) << 3) + (x & 7)
         place = jnp.where((y >> 6) == me, place, -1)
@@ -140,14 +140,14 @@
         for k in range(count):
             found = jnp.take_along_axis(table[k], lane, axis=1)
             accs[k % 4] = jnp.where(place == k, found, accs[k % 4])
-        out[t] = (accs[0] + accs[1]) + (accs[2] + accs[3])
-
-    def tiles(i, carry):
-        for t in range(2):
-            tile(i * 2 + t)
+        return (accs[0] + accs[1]) + (accs[2] + accs[3])
+
+    def tiles(t, carry):
+        for j, out in enumerate(outs):
+            out[t] = tile(lax.rem(me + j, 4) * 4 + t)
         return carry
 
-    lax.fori_loop(0, index.shape[0] // 2, tiles, 0)
+    lax.fori_loop(0, 4, tiles, 0)
 
 
 def spring_values(cls, k, count, modulus, yields):
@@ -201,14 +201,12 @@
     out[...] = lax.fori_loop(0, STEPS, step, (start[...], zero, zero))[0]
 
 
-def last_rows_kernel(count, modulus, yields, soil, start, edge, arrived, done, out):
+def last_rows_kernel(count, modulus, yields, soil, start, edge, own, next1, next2, next3, done, out):
     del done
     row = lax.broadcasted_iota(jnp.int32, (8, 128), 0)
     for t in range(4):
         cols = slice(t * 128, (t + 1) * 128)
-        base = arrived[0, t * 8 : t * 8 + 8]
-        for source in range(1, arrived.shape[0]):
-            base = base + arrived[source, t * 8 : t * 8 + 8]
+        base = (own[t] + next1[t]) + (next2[t] + next3[t])
         cls = soil[:, cols]
         pairs = [spring_values(cls, k, count, modulus, yields) for k in range(16)]
         springs = [jnp.zeros((8, 128), F32) for _ in range(16)]
@@ -428,8 +426,6 @@
     )(*regional)
     edge_from_left = lax.ppermute(edge_right, XAX, right)
     edge_from_right = lax.ppermute(edge_left, XAX, left)
-    mid_from_left = lax.ppermute(mid_right, "gx", [(i, i + 1) for i in range(n_gx - 1)])
-    mid_from_right = lax.ppermute(mid_left, "gx", [(i + 1, i) for i in range(n_gx - 1)])
 
     soil = soil_class[0]
     start = basin_disp[0]
@@ -475,7 +471,9 @@
 
     table = lax.all_to_all(jnp.broadcast_to(trace.reshape(1, 64, 128), (n_gx, 64, 128)), "gx", 0, 0)
     table = table.reshape(n_gx * 8, 8, 128)
-    table, edge_from_left, edge_from_right = lax.optimization_barrier((table, edge_from_left, edge_from_right))
+    mid_from_left = lax.ppermute(mid_right, "gx", [(i, i + 1) for i in range(n_gx - 1)])
+    mid_from_right = lax.ppermute(mid_left, "gx", [(i + 1, i) for i in range(n_gx - 1)])
+    trace, edge_from_left, edge_from_right = lax.optimization_barrier((trace, edge_from_left, edge_from_right))
     y_a, y_b = pl.pallas_call(
         pack_y_kernel,
         out_shape=(sds(92, 8, 256), sds(92, 8, 256)),
@@ -485,31 +483,21 @@
         compiler_params=PARAMS,
         name="pack_y",
     )(*regional, edge_from_left, edge_from_right)
-    table, y_a, y_b = lax.optimization_barrier((table, y_a, y_b))
     y_a = lax.ppermute(y_a, "gy", swap_a)
     y_b = lax.ppermute(y_b, "gy", swap_b)
 
     picked = pl.pallas_call(
         pick_kernel,
-        out_shape=sds(16, 8, 128),
+        out_shape=(sds(4, 8, 128),) * 4,
         in_specs=[VM] * 2,
-        out_specs=VM,
+        out_specs=(VM,) * 4,
         compiler_params=PARAMS,
         name="pick",
     )(table, index)
-    arrived = lax.all_to_all(picked.reshape(4, 32, 128), "gy", 0, 0)
-
-    tail = pl.BlockSpec((8, 512), lambda i: (7, 0))
-    basin = pl.pallas_call(
-        last_rows_kernel,
-        grid=(1,),
-        out_shape=sds(64, 512),
-        in_specs=[SM] * 3 + [tail, tail, whole(8, 512), whole(4, 32, 128), ANY],
-        out_specs=tail,
-        input_output_aliases={7: 0},
-        compiler_params=PARAMS,
-        name="last_rows",
-    )(*tables, soil, start, edge, arrived, upper)
+    y_b, *picked = lax.optimization_barrier((y_b, *picked))
+    arrived = [picked[0]] + [
+        lax.ppermute(picked[k], "gy", [(i, (i + k) % 4) for i in range(4)]) for k in (1, 2, 3)
+    ]
 
     final = pl.pallas_call(
         region_kernel,
@@ -520,6 +508,18 @@
         compiler_params=PARAMS,
         name="region",
     )(*regional, edge_from_left, edge_from_right, mid_from_left, mid_from_right, mid_relay, y_a, y_b)
+    final, *arrived = lax.optimization_barrier((final, *arrived))
+    tail = pl.BlockSpec((8, 512), lambda i: (7, 0))
+    basin = pl.pallas_call(
+        last_rows_kernel,
+        grid=(1,),
+        out_shape=sds(64, 512),
+        in_specs=[SM] * 3 + [tail, tail, whole(8, 512)] + [whole(4, 8, 128)] * 4 + [ANY],
+        out_specs=tail,
+        input_output_aliases={10: 0},
+        compiler_params=PARAMS,
+        name="last_rows",
+    )(*tables, soil, start, edge, *arrived, upper)
     return (final, basin[None])
 
 

time: 114 us -> 106 us (0.930)
  the two profiles are of different devices: /device:TPU:4 before, /device:TPU:95 now
where the time goes in v4:
time: 106 us
  blocking collectives  32.6 us (31%)
  Pallas kernels  31.6 us (30%)
  starting transfers between devices  25.4 us (24%)
  waiting for transfers between devices  15 us (14%)
    all_to_all x1, blocking collectives, shards(): lax.all_to_all(jnp.broadcast_to(trace.reshape(1, 64, 128), (n_gx, 64, 128...  26.4 us
    pallas_call x1, Pallas kernels, shards(): pl.pallas_call(region_kernel, out_shape=sds(16, 64, 256), in_specs=[ANY]...  11.9 us
    ppermute x1, waiting for transfers between devices, shards(): edge_from_right = lax.ppermute(edge_left, XAX, left)  10.1 us
    pallas_call x1, Pallas kernels, shards(): pl.pallas_call(columns_kernel, grid=(2,), out_shape=(sds(64, 512), sds(8,...  7.53 us
    ppermute x1, starting transfers between devices, shards(): band_from_left = lax.ppermute(band_right, XAX, right)  7.33 us
    all_gather x1, blocking collectives, shards(): index = lax.all_gather(index, 'gy').reshape(16, 128)  6.18 us
    ppermute x1, waiting for transfers between devices, shards(): edge_from_left = lax.ppermute(edge_right, XAX, right)  4.88 us
    ppermute x1, starting transfers between devices, shards(): lax.ppermute(mid_left, 'gx', [(i + 1, i) for i in range(n_gx - 1)])  4.05 us
  transfers between devices with their start and end apart: 15, of which 2 were waited for; matrix products, arithmetic and copies ran while one was open for 0% of the time, Pallas kernels for 25%

profile of v4, /device:TPU:95, one launch (start us, length us, event | category | flops | bytes accessed | tf_op | source)
XLA Modules:
  0.0 105.8 jit_solution(7575393077807726555)
XLA Ops:
  0.7 2.9 %band.1 = (f32[48,8,128]{2,1,0:T(8,128)}, f32[24,8,128]{2,1,0:T(8,128)}, f32[24,8,128]{2,1,0:T(8,128)}) custom-call(f32[16,64,256]{2,1,0:T(8,128)} %u.4, f32[16,64,256]{2,1,0:T(8,128)} %p.4, f32[16,64,256]{2,1,0:T(8,128)} %c.4), custom_call_target="tpu_custom_call" | custom-call | tf_op jit(solution)/shard_map/band/pallas_call | solution.py:403
  3.5 0.5 collective-permute-start.1
  4.0 7.3 %collective-permute-start = (f32[24,8,128]{2,1,0:T(8,128)}, f32[24,8,128]{2,1,0:T(8,128)S(1)}, u32[]{:S(2)}, u32[]{:S(2)}) collective-permute-start(f32[24,8,128]{2,1,0:T(8,128)} %get-tuple-element.46), channel_id=1, source_target_pairs={{0,4},{4,8},{8,12},{12,16},{16,20},{20,24},{24,28},{28,32},{32,36}... | collective-permute-start | bytes 294920 | tf_op jit(solution)/shard_map/ppermute | solution.py:412
  11.3 6.2 %all-gather = s32[4,4,128]{2,1,0:T(4,128)S(1)} all-gather(s32[1,4,128]{2,1,0:T(4,128)S(1)} %bitcast.15), channel_id=2, replica_groups=mesh['sec'=4,'gx'=16,'gy'=4] {'gy'}, dimensions={0}, use_global_device_ids=true | all-gather | bytes 10240 | tf_op jit(solution)/shard_map/all_gather | solution.py:415
  17.5 0.0 copy-start.4
  17.5 0.0 copy-start.6
  17.6 0.0 copy-start.5
  17.6 0.7 pack_x.1
  18.3 0.2 copy-done.3
  18.4 0.1 copy-done.4
  18.5 7.5 %columns.1 = (f32[64,512]{1,0:T(8,128)}, f32[8,512]{1,0:T(8,128)S(1)}) custom-call(s32[8]{0:T(128)S(1)} %copy-done.8, f32[8,16]{1,0:T(8,128)S(1)} %copy-done.6, f32[8,16]{1,0:T(8,128)S(1)} %copy-done.7, s32[64,512]{1,0:T(8,128)S(1)} %bitcast.8, f32[64,512]{1,0:T(8,128)S(1)} %bitcast.10), custom_call_target="tpu_custom_call" | custom-call | tf_op jit(solution)/shard_map/columns/pallas_call | solution.py:435
  26.0 1.4 %collective-permute-start.8 = (f32[22,48,256]{2,1,0:T(8,128)S(1)}, f32[22,48,256]{2,1,0:T(8,128)S(1)}, u32[]{:S(2)}, u32[]{:S(2)}) collective-permute-start(f32[22,48,256]{2,1,0:T(8,128)S(1)} %get-tuple-element.71), channel_id=1, source_target_pairs={{60,12},{0,48},{61,45},{1,17},{62,14},{2,50},{63,47},{3,19},{124,7... | collective-permute-start | bytes 3244040 | tf_op jit(solution)/shard_map/ppermute | solution.py:449
  27.4 2.3 %band_edges.1 = (f32[48,32,128]{2,1,0:T(8,128)S(1)}, f32[3,32,128]{2,1,0:T(8,128)S(1)}, f32[3,32,128]{2,1,0:T(8,128)S(1)}) custom-call(f32[48,8,128]{2,1,0:T(8,128)S(1)} %copy-done.5, f32[24,8,128]{2,1,0:T(8,128)S(1)} %collective-permute-done.from_left, f32[24,8,128]{2,1,0:T(8,128)S(1)} %collective-permute-done.1.from_right), custom_call_target="tpu_custom_call" | custom-call | tf_op jit(solution)/shard_map/band_edges/pallas_call | solution.py:452
  29.7 0.3 collective-permute-start.2
  30.0 3.8 %collective-permute-start.3 = (f32[3,32,128]{2,1,0:T(8,128)S(1)}, f32[3,32,128]{2,1,0:T(8,128)S(1)}, u32[]{:S(2)}, u32[]{:S(2)}) collective-permute-start(f32[3,32,128]{2,1,0:T(8,128)S(1)} %get-tuple-element.64), channel_id=1, source_target_pairs={{0,0},{1,2},{2,1},{3,3},{4,4},{5,6},{6,5},{7,7},{8,8},{9,10},{10,9... | collective-permute-start | bytes 147464 | tf_op jit(solution)/shard_map/ppermute | solution.py:461
  33.9 0.9 collective-permute-start.4
  34.7 0.7 collective-permute-start.5
  35.4 1.3 %collective-permute-start.6 = (f32[22,48,256]{2,1,0:T(8,128)S(1)}, f32[22,48,256]{2,1,0:T(8,128)S(1)}, u32[]{:S(2)}, u32[]{:S(2)}) collective-permute-start(f32[22,48,256]{2,1,0:T(8,128)S(1)} %get-tuple-element.69), channel_id=1, source_target_pairs={{0,4},{4,8},{8,12},{12,16},{16,20},{20,24},{24,28},{28,32},{32,36}... | collective-permute-start | bytes 3244040 | tf_op jit(solution)/shard_map/ppermute | solution.py:474
  36.7 4.1 %collective-permute-start.7 = (f32[22,48,256]{2,1,0:T(8,128)S(1)}, f32[22,48,256]{2,1,0:T(8,128)S(1)}, u32[]{:S(2)}, u32[]{:S(2)}) collective-permute-start(f32[22,48,256]{2,1,0:T(8,128)S(1)} %get-tuple-element.70), channel_id=1, source_target_pairs={{4,0},{8,4},{12,8},{16,12},{20,16},{24,20},{28,24},{32,28},{36,32}... | collective-permute-start | bytes 3244040 | tf_op jit(solution)/shard_map/ppermute | solution.py:475
  40.8 1.3 %collective-permute-start.9 = (f32[22,48,256]{2,1,0:T(8,128)S(1)}, f32[22,48,256]{2,1,0:T(8,128)S(1)}, u32[]{:S(2)}, u32[]{:S(2)}) collective-permute-start(f32[22,48,256]{2,1,0:T(8,128)S(1)} %collective-permute-done.8), channel_id=1, source_target_pairs={{12,64},{45,65},{14,66},{47,67},{76,128},{112,60},{109,129},{81,61... | collective-permute-start | bytes 3244040 | tf_op jit(solution)/shard_map/ppermute | solution.py:450
  42.1 1.1 %band_steps.1 = f32[8,8,128]{2,1,0:T(8,128)S(1)} custom-call(f32[48,32,128]{2,1,0:T(8,128)S(1)} %get-tuple-element.62.ext, f32[3,32,128]{2,1,0:T(8,128)S(1)} %collective-permute-done.2.recv_a, f32[3,32,128]{2,1,0:T(8,128)S(1)} %collective-permute-done.3.recv_b), custom_call_target="tpu_custom_call" | custom-call | tf_op jit(solution)/shard_map/band_steps/pallas_call | solution.py:462
  43.2 4.9 %collective-permute-done.4.from_left.el = f32[22,16,256]{2,1,0:T(8,128)S(1)} collective-permute-done((f32[22,16,256]{2,1,0:T(8,128)S(1)}, f32[22,16,256]{2,1,0:T(8,128)S(1)}, u32[]{:S(2)}, u32[]{:S(2)}) %collective-permute-start.4) | collective-permute-done | bytes 360480 | tf_op jit(solution)/shard_map/ppermute | solution.py:427
  48.1 10.1 %collective-permute-done.5.from_right.er = f32[22,16,256]{2,1,0:T(8,128)S(1)} collective-permute-done((f32[22,16,256]{2,1,0:T(8,128)S(1)}, f32[22,16,256]{2,1,0:T(8,128)S(1)}, u32[]{:S(2)}, u32[]{:S(2)}) %collective-permute-start.5) | collective-permute-done | bytes 360480 | tf_op jit(solution)/shard_map/ppermute | solution.py:428
  58.2 0.3 pack_y.1
  58.5 1.9 %collective-permute-start.11 = (f32[92,8,256]{2,1,0:T(8,128)S(1)}, f32[92,8,256]{2,1,0:T(8,128)S(1)}, u32[]{:S(2)}, u32[]{:S(2)}) collective-permute-start(f32[92,8,256]{2,1,0:T(8,128)S(1)} %get-tuple-element.73), channel_id=1, source_target_pairs={{0,0},{1,2},{2,1},{3,3},{4,4},{5,6},{6,5},{7,7},{8,8},{9,10},{10,9... | collective-permute-start | bytes 2261000 | tf_op jit(solution)/shard_map/ppermute | solution.py:487
  60.5 0.1 collective-permute-start.10
  60.6 26.4 %all_to_all.5 = f32[16,64,128]{2,1,0:T(8,128)S(1)} all-to-all(f32[16,64,128]{2,1,0:T(8,128)S(1)} %broadcast_in_dim.11), channel_id=1, replica_groups=mesh['sec'=4,'gx'=16,'gy'=4] {'gx'}, dimensions={0} | all-to-all | bytes 1048576 | tf_op jit(solution)/shard_map/all_to_all | solution.py:472
  87.0 2.6 %pick.1 = (f32[4,8,128]{2,1,0:T(8,128)S(1)}, f32[4,8,128]{2,1,0:T(8,128)S(1)}, f32[4,8,128]{2,1,0:T(8,128)S(1)}, f32[4,8,128]{2,1,0:T(8,128)S(1)}) custom-call(f32[128,8,128]{2,1,0:T(8,128)S(1)} %bitcast.7, s32[16,128]{1,0:T(8,128)S(1)} %bitcast.13), custom_call_target="tpu_custom_call" | custom-call | tf_op jit(solution)/shard_map/pick/pallas_call | solution.py:489
  89.6 0.1 collective-permute-start.12
  89.7 1.8 %collective-permute-start.13 = (f32[4,8,128]{2,1,0:T(8,128)S(1)}, f32[4,8,128]{2,1,0:T(8,128)S(1)}, u32[]{:S(2)}, u32[]{:S(2)}) collective-permute-start(f32[4,8,128]{2,1,0:T(8,128)S(1)} %get-tuple-element.81), channel_id=1, source_target_pairs={{0,2},{1,3},{2,0},{3,1},{4,6},{5,7},{6,4},{7,5},{8,10},{9,11},{10,... | collective-permute-start | bytes 49160 | tf_op jit(solution)/shard_map/ppermute | solution.py:499
  91.6 11.9 %region.1 = f32[16,64,256]{2,1,0:T(8,128)} custom-call(f32[16,64,256]{2,1,0:T(8,128)S(1)} %copy-done, f32[16,64,256]{2,1,0:T(8,128)S(1)} %copy-done.1, f32[16,64,256]{2,1,0:T(8,128)S(1)} %copy-done.2, f32[22,16,256]{2,1,0:T(8,128)S(1)} %collective-permute-done.4.from_left.el, f32[22,16,256]{2,1,0:T(8,128)S(1)} %collective-permute-done.5.from_right.er, ...), custom_call_target="tpu_custom_call" | custom-call | tf_op jit(solution)/shard_map/region/pallas_call | solution.py:502
  103.6 2.2 %last_rows.1 = f32[64,512]{1,0:T(8,128)} custom-call(s32[8]{0:T(128)S(1)} %copy-done.8, f32[8,16]{1,0:T(8,128)S(1)} %copy-done.6, f32[8,16]{1,0:T(8,128)S(1)} %copy-done.7, s32[64,512]{1,0:T(8,128)S(1)} %bitcast.9, f32[64,512]{1,0:T(8,128)S(1)} %bitcast.11, f32[8,512]{1,0:T(8,128)S(1)} %get-tuple-element.84.edge, ...), custom_call_target="tpu_custom_call", output_to_operand_aliasing={{}: (10, {})} | custom-call | tf_op jit(solution)/shard_map/last_rows/pallas_call | solution.py:513
  (30 shorter events, 0.1 us)
Async XLA Ops:
  0.6 16.9 %copy-start.2 = (f32[16,64,256]{2,1,0:T(8,128)S(1)}, f32[16,64,256]{2,1,0:T(8,128)}, u32[]{:S(2)}) copy-start(f32[16,64,256]{2,1,0:T(8,128)} %c.4) | copy-start | bytes 3145732
  0.6 16.9 %copy-start.1 = (f32[16,64,256]{2,1,0:T(8,128)S(1)}, f32[16,64,256]{2,1,0:T(8,128)}, u32[]{:S(2)}) copy-start(f32[16,64,256]{2,1,0:T(8,128)} %p.4) | copy-start | bytes 3145732
  0.7 16.9 %copy-start = (f32[16,64,256]{2,1,0:T(8,128)S(1)}, f32[16,64,256]{2,1,0:T(8,128)}, u32[]{:S(2)}) copy-start(f32[16,64,256]{2,1,0:T(8,128)} %u.4) | copy-start | bytes 3145732
  0.7 10.7 %copy-start.9 = (s32[1,512]{1,0:T(1,128)S(1)}, s32[1,512]{1,0:T(1,128)}, u32[]{:S(2)}) copy-start(s32[1,512]{1,0:T(1,128)} %param.13) | copy-start | bytes 6148
  3.5 22.5 %collective-permute-start.1 = (f32[24,8,128]{2,1,0:T(8,128)}, f32[24,8,128]{2,1,0:T(8,128)S(1)}, u32[]{:S(2)}, u32[]{:S(2)}) collective-permute-start(f32[24,8,128]{2,1,0:T(8,128)} %get-tuple-element.57), channel_id=1, source_target_pairs={{0,252},{4,0},{8,4},{12,8},{16,12},{20,16},{24,20},{28,24},{32,28}... | collective-permute-start | bytes 294920 | tf_op jit(solution)/shard_map/ppermute | solution.py:413
  4.0 22.0 %collective-permute-start = (f32[24,8,128]{2,1,0:T(8,128)}, f32[24,8,128]{2,1,0:T(8,128)S(1)}, u32[]{:S(2)}, u32[]{:S(2)}) collective-permute-start(f32[24,8,128]{2,1,0:T(8,128)} %get-tuple-element.46), channel_id=1, source_target_pairs={{0,4},{4,8},{8,12},{12,16},{16,20},{20,24},{24,28},{28,32},{32,36}... | collective-permute-start | bytes 294920 | tf_op jit(solution)/shard_map/ppermute | solution.py:412
  17.5 0.9 copy-start.3
  17.5 1.0 copy-start.4
  17.5 1.0 copy-start.6
  17.6 0.9 copy-start.7
  17.6 0.9 copy-start.8
  17.6 9.8 %copy-start.5 = (f32[48,8,128]{2,1,0:T(8,128)S(1)}, f32[48,8,128]{2,1,0:T(8,128)}, u32[]{:S(2)}) copy-start(f32[48,8,128]{2,1,0:T(8,128)} %get-tuple-element.51.band) | copy-start | bytes 589828
  26.0 14.7 %collective-permute-start.8 = (f32[22,48,256]{2,1,0:T(8,128)S(1)}, f32[22,48,256]{2,1,0:T(8,128)S(1)}, u32[]{:S(2)}, u32[]{:S(2)}) collective-permute-start(f32[22,48,256]{2,1,0:T(8,128)S(1)} %get-tuple-element.71), channel_id=1, source_target_pairs={{60,12},{0,48},{61,45},{1,17},{62,14},{2,50},{63,47},{3,19},{124,7... | collective-permute-start | bytes 3244040 | tf_op jit(solution)/shard_map/ppermute | solution.py:449
  29.7 5.7 %collective-permute-start.2 = (f32[3,32,128]{2,1,0:T(8,128)S(1)}, f32[3,32,128]{2,1,0:T(8,128)S(1)}, u32[]{:S(2)}, u32[]{:S(2)}) collective-permute-start(f32[3,32,128]{2,1,0:T(8,128)S(1)} %get-tuple-element.63), channel_id=1, source_target_pairs={{0,1},{1,0},{2,3},{3,2},{4,5},{5,4},{6,7},{7,6},{8,9},{9,8},{10,11... | collective-permute-start | bytes 147464 | tf_op jit(solution)/shard_map/ppermute | solution.py:460
  30.0 6.7 %collective-permute-start.3 = (f32[3,32,128]{2,1,0:T(8,128)S(1)}, f32[3,32,128]{2,1,0:T(8,128)S(1)}, u32[]{:S(2)}, u32[]{:S(2)}) collective-permute-start(f32[3,32,128]{2,1,0:T(8,128)S(1)} %get-tuple-element.64), channel_id=1, source_target_pairs={{0,0},{1,2},{2,1},{3,3},{4,4},{5,6},{6,5},{7,7},{8,8},{9,10},{10,9... | collective-permute-start | bytes 147464 | tf_op jit(solution)/shard_map/ppermute | solution.py:461
  33.9 14.3 %collective-permute-start.4 = (f32[22,16,256]{2,1,0:T(8,128)S(1)}, f32[22,16,256]{2,1,0:T(8,128)S(1)}, u32[]{:S(2)}, u32[]{:S(2)}) collective-permute-start(f32[22,16,256]{2,1,0:T(8,128)S(1)} %get-tuple-element.65), channel_id=1, source_target_pairs={{0,4},{4,8},{8,12},{12,16},{16,20},{20,24},{24,28},{28,32},{32,36}... | collective-permute-start | bytes 1081352 | tf_op jit(solution)/shard_map/ppermute | solution.py:427
  34.7 23.5 %collective-permute-start.5 = (f32[22,16,256]{2,1,0:T(8,128)S(1)}, f32[22,16,256]{2,1,0:T(8,128)S(1)}, u32[]{:S(2)}, u32[]{:S(2)}) collective-permute-start(f32[22,16,256]{2,1,0:T(8,128)S(1)} %get-tuple-element.66), channel_id=1, source_target_pairs={{0,252},{4,0},{8,4},{12,8},{16,12},{20,16},{24,20},{28,24},{32,28}... | collective-permute-start | bytes 1081352 | tf_op jit(solution)/shard_map/ppermute | solution.py:428
  35.4 54.3 %collective-permute-start.6 = (f32[22,48,256]{2,1,0:T(8,128)S(1)}, f32[22,48,256]{2,1,0:T(8,128)S(1)}, u32[]{:S(2)}, u32[]{:S(2)}) collective-permute-start(f32[22,48,256]{2,1,0:T(8,128)S(1)} %get-tuple-element.69), channel_id=1, source_target_pairs={{0,4},{4,8},{8,12},{12,16},{16,20},{20,24},{24,28},{28,32},{32,36}... | collective-permute-start | bytes 3244040 | tf_op jit(solution)/shard_map/ppermute | solution.py:474
  36.7 54.9 %collective-permute-start.7 = (f32[22,48,256]{2,1,0:T(8,128)S(1)}, f32[22,48,256]{2,1,0:T(8,128)S(1)}, u32[]{:S(2)}, u32[]{:S(2)}) collective-permute-start(f32[22,48,256]{2,1,0:T(8,128)S(1)} %get-tuple-element.70), channel_id=1, source_target_pairs={{4,0},{8,4},{12,8},{16,12},{20,16},{24,20},{28,24},{32,28},{36,32}... | collective-permute-start | bytes 3244040 | tf_op jit(solution)/shard_map/ppermute | solution.py:475
  40.8 50.8 %collective-permute-start.9 = (f32[22,48,256]{2,1,0:T(8,128)S(1)}, f32[22,48,256]{2,1,0:T(8,128)S(1)}, u32[]{:S(2)}, u32[]{:S(2)}) collective-permute-start(f32[22,48,256]{2,1,0:T(8,128)S(1)} %collective-permute-done.8), channel_id=1, source_target_pairs={{12,64},{45,65},{14,66},{47,67},{76,128},{112,60},{109,129},{81,61... | collective-permute-start | bytes 3244040 | tf_op jit(solution)/shard_map/ppermute | solution.py:450
  58.5 31.1 %collective-permute-start.11 = (f32[92,8,256]{2,1,0:T(8,128)S(1)}, f32[92,8,256]{2,1,0:T(8,128)S(1)}, u32[]{:S(2)}, u32[]{:S(2)}) collective-permute-start(f32[92,8,256]{2,1,0:T(8,128)S(1)} %get-tuple-element.73), channel_id=1, source_target_pairs={{0,0},{1,2},{2,1},{3,3},{4,4},{5,6},{6,5},{7,7},{8,8},{9,10},{10,9... | collective-permute-start | bytes 2261000 | tf_op jit(solution)/shard_map/ppermute | solution.py:487
  60.5 31.1 %collective-permute-start.10 = (f32[92,8,256]{2,1,0:T(8,128)S(1)}, f32[92,8,256]{2,1,0:T(8,128)S(1)}, u32[]{:S(2)}, u32[]{:S(2)}) collective-permute-start(f32[92,8,256]{2,1,0:T(8,128)S(1)} %get-tuple-element.72), channel_id=1, source_target_pairs={{0,1},{1,0},{2,3},{3,2},{4,5},{5,4},{6,7},{7,6},{8,9},{9,8},{10,11... | collective-permute-start | bytes 2261000 | tf_op jit(solution)/shard_map/ppermute | solution.py:486
  89.6 13.9 %collective-permute-start.12 = (f32[4,8,128]{2,1,0:T(8,128)S(1)}, f32[4,8,128]{2,1,0:T(8,128)S(1)}, u32[]{:S(2)}, u32[]{:S(2)}) collective-permute-start(f32[4,8,128]{2,1,0:T(8,128)S(1)} %get-tuple-element.80), channel_id=1, source_target_pairs={{0,1},{1,2},{2,3},{3,0},{4,5},{5,6},{6,7},{7,4},{8,9},{9,10},{10,1... | collective-permute-start | bytes 49160 | tf_op jit(solution)/shard_map/ppermute | solution.py:499
  89.7 13.8 %collective-permute-start.13 = (f32[4,8,128]{2,1,0:T(8,128)S(1)}, f32[4,8,128]{2,1,0:T(8,128)S(1)}, u32[]{:S(2)}, u32[]{:S(2)}) collective-permute-start(f32[4,8,128]{2,1,0:T(8,128)S(1)} %get-tuple-element.81), channel_id=1, source_target_pairs={{0,2},{1,3},{2,0},{3,1},{4,6},{5,7},{6,4},{7,5},{8,10},{9,11},{10,... | collective-permute-start | bytes 49160 | tf_op jit(solution)/shard_map/ppermute | solution.py:499
  91.6 12.0 %collective-permute-start.14 = (f32[4,8,128]{2,1,0:T(8,128)S(1)}, f32[4,8,128]{2,1,0:T(8,128)S(1)}, u32[]{:S(2)}, u32[]{:S(2)}) collective-permute-start(f32[4,8,128]{2,1,0:T(8,128)S(1)} %get-tuple-element.82), channel_id=1, source_target_pairs={{0,3},{1,0},{2,1},{3,2},{4,7},{5,4},{6,5},{7,6},{8,11},{9,8},{10,9... | collective-permute-start | bytes 49160 | tf_op jit(solution)/shard_map/ppermute | solution.py:499

commit v5 on v4

--- a/solution.py
+++ b/solution.py
@@ -86,7 +86,7 @@
         send_b[g] = jnp.where(even, low, high)
 
 
-def band_steps_kernel(ext, recv_a, recv_b, trace, one, two, coef):
+def band_steps_kernel(ext, recv_a, recv_b, copies, one, two, coef, trace):
     low_edge, high_edge = y_edges()
     even = lax.rem(lax.axis_index("gy"), 2) == 0
     lane = lanes((32, 128))
@@ -124,6 +124,8 @@
         now, old = old, now
         plane = now[8]
         trace[:, step - 1, :] = jnp.where(first, plane[0:8], pltpu.roll(plane[8:16], 64, 1))
+    for peer in range(copies.shape[0]):
+        copies[peer] = trace[...]
 
 
 def pick_kernel(table, index, *outs):
@@ -461,15 +463,15 @@
     band_b = lax.ppermute(band_b, "gy", swap_b)
     trace = pl.pallas_call(
         band_steps_kernel,
-        out_shape=sds(8, 8, 128),
+        out_shape=sds(n_gx, 8, 8, 128),
         in_specs=[VM] * 3,
         out_specs=VM,
-        scratch_shapes=[pltpu.VMEM((17, 32, 128), F32)] * 3,
+        scratch_shapes=[pltpu.VMEM((17, 32, 128), F32)] * 3 + [pltpu.VMEM((8, 8, 128), F32)],
         compiler_params=PARAMS,
         name="band_steps",
     )(ext, band_a, band_b)
 
-    table = lax.all_to_all(jnp.broadcast_to(trace.reshape(1, 64, 128), (n_gx, 64, 128)), "gx", 0, 0)
+    table = lax.all_to_all(trace.reshape(n_gx, 64, 128), "gx", 0, 0)
     table = table.reshape(n_gx * 8, 8, 128)
     mid_from_left = lax.ppermute(mid_right, "gx", [(i, i + 1) for i in range(n_gx - 1)])
     mid_from_right = lax.ppermute(mid_left, "gx", [(i + 1, i) for i in range(n_gx - 1)])

time: 106 us -> 106 us (level)
  no operation moved by 1% of the time
where the time goes in v5:
time: 106 us
  blocking collectives  32.7 us (31%)
  Pallas kernels  31.7 us (30%)
  starting transfers between devices  25.4 us (24%)
  waiting for transfers between devices  15 us (14%)
    all_to_all x1, blocking collectives, shards(): table = lax.all_to_all(trace.reshape(n_gx, 64, 128), 'gx', 0, 0)  26.5 us
    pallas_call x1, Pallas kernels, shards(): pl.pallas_call(region_kernel, out_shape=sds(16, 64, 256), in_specs=[ANY]...  11.9 us
    ppermute x1, waiting for transfers between devices, shards(): edge_from_right = lax.ppermute(edge_left, XAX, left)  10.1 us
    pallas_call x1, Pallas kernels, shards(): pl.pallas_call(columns_kernel, grid=(2,), out_shape=(sds(64, 512), sds(8,...  7.53 us
    ppermute x1, starting transfers between devices, shards(): band_from_left = lax.ppermute(band_right, XAX, right)  7.33 us
    all_gather x1, blocking collectives, shards(): index = lax.all_gather(index, 'gy').reshape(16, 128)  6.18 us
    ppermute x1, waiting for transfers between devices, shards(): edge_from_left = lax.ppermute(edge_right, XAX, right)  4.84 us
    ppermute x1, starting transfers between devices, shards(): lax.ppermute(mid_left, 'gx', [(i + 1, i) for i in range(n_gx - 1)])  4.05 us
  transfers between devices with their start and end apart: 15, of which 2 were waited for; matrix products, arithmetic and copies ran while one was open for 0% of the time, Pallas kernels for 25%

profile of v5, /device:TPU:95, one launch (start us, length us, event | category | flops | bytes accessed | tf_op | source)
XLA Modules:
  0.0 105.9 jit_solution(8637719505346209819)
XLA Ops:
  0.7 2.9 %band.1 = (f32[48,8,128]{2,1,0:T(8,128)}, f32[24,8,128]{2,1,0:T(8,128)}, f32[24,8,128]{2,1,0:T(8,128)}) custom-call(f32[16,64,256]{2,1,0:T(8,128)} %u.4, f32[16,64,256]{2,1,0:T(8,128)} %p.4, f32[16,64,256]{2,1,0:T(8,128)} %c.4), custom_call_target="tpu_custom_call" | custom-call | tf_op jit(solution)/shard_map/band/pallas_call | solution.py:405
  3.5 0.5 collective-permute-start.1
  4.0 7.3 %collective-permute-start = (f32[24,8,128]{2,1,0:T(8,128)}, f32[24,8,128]{2,1,0:T(8,128)S(1)}, u32[]{:S(2)}, u32[]{:S(2)}) collective-permute-start(f32[24,8,128]{2,1,0:T(8,128)} %get-tuple-element.46), channel_id=1, source_target_pairs={{0,4},{4,8},{8,12},{12,16},{16,20},{20,24},{24,28},{28,32},{32,36}... | collective-permute-start | bytes 294920 | tf_op jit(solution)/shard_map/ppermute | solution.py:414
  11.3 6.2 %all-gather = s32[4,4,128]{2,1,0:T(4,128)S(1)} all-gather(s32[1,4,128]{2,1,0:T(4,128)S(1)} %bitcast.15), channel_id=2, replica_groups=mesh['sec'=4,'gx'=16,'gy'=4] {'gy'}, dimensions={0}, use_global_device_ids=true | all-gather | bytes 10240 | tf_op jit(solution)/shard_map/all_gather | solution.py:417
  17.5 0.0 copy-start.4
  17.5 0.0 copy-start.6
  17.6 0.0 copy-start.5
  17.6 0.7 pack_x.1
  18.3 0.2 copy-done.3
  18.4 0.1 copy-done.4
  18.5 7.5 %columns.1 = (f32[64,512]{1,0:T(8,128)}, f32[8,512]{1,0:T(8,128)S(1)}) custom-call(s32[8]{0:T(128)S(1)} %copy-done.8, f32[8,16]{1,0:T(8,128)S(1)} %copy-done.6, f32[8,16]{1,0:T(8,128)S(1)} %copy-done.7, s32[64,512]{1,0:T(8,128)S(1)} %bitcast.9, f32[64,512]{1,0:T(8,128)S(1)} %bitcast.11), custom_call_target="tpu_custom_call" | custom-call | tf_op jit(solution)/shard_map/columns/pallas_call | solution.py:437
  26.0 1.4 %collective-permute-start.8 = (f32[22,48,256]{2,1,0:T(8,128)S(1)}, f32[22,48,256]{2,1,0:T(8,128)S(1)}, u32[]{:S(2)}, u32[]{:S(2)}) collective-permute-start(f32[22,48,256]{2,1,0:T(8,128)S(1)} %get-tuple-element.71), channel_id=1, source_target_pairs={{60,12},{0,48},{61,45},{1,17},{62,14},{2,50},{63,47},{3,19},{124,7... | collective-permute-start | bytes 3244040 | tf_op jit(solution)/shard_map/ppermute | solution.py:451
  27.4 2.3 %band_edges.1 = (f32[48,32,128]{2,1,0:T(8,128)S(1)}, f32[3,32,128]{2,1,0:T(8,128)S(1)}, f32[3,32,128]{2,1,0:T(8,128)S(1)}) custom-call(f32[48,8,128]{2,1,0:T(8,128)S(1)} %copy-done.5, f32[24,8,128]{2,1,0:T(8,128)S(1)} %collective-permute-done.from_left, f32[24,8,128]{2,1,0:T(8,128)S(1)} %collective-permute-done.1.from_right), custom_call_target="tpu_custom_call" | custom-call | tf_op jit(solution)/shard_map/band_edges/pallas_call | solution.py:454
  29.7 0.3 collective-permute-start.2
  30.0 3.8 %collective-permute-start.3 = (f32[3,32,128]{2,1,0:T(8,128)S(1)}, f32[3,32,128]{2,1,0:T(8,128)S(1)}, u32[]{:S(2)}, u32[]{:S(2)}) collective-permute-start(f32[3,32,128]{2,1,0:T(8,128)S(1)} %get-tuple-element.64), channel_id=1, source_target_pairs={{0,0},{1,2},{2,1},{3,3},{4,4},{5,6},{6,5},{7,7},{8,8},{9,10},{10,9... | collective-permute-start | bytes 147464 | tf_op jit(solution)/shard_map/ppermute | solution.py:463
  33.9 0.9 collective-permute-start.4
  34.7 0.7 collective-permute-start.5
  35.4 1.3 %collective-permute-start.6 = (f32[22,48,256]{2,1,0:T(8,128)S(1)}, f32[22,48,256]{2,1,0:T(8,128)S(1)}, u32[]{:S(2)}, u32[]{:S(2)}) collective-permute-start(f32[22,48,256]{2,1,0:T(8,128)S(1)} %get-tuple-element.69), channel_id=1, source_target_pairs={{0,4},{4,8},{8,12},{12,16},{16,20},{20,24},{24,28},{28,32},{32,36}... | collective-permute-start | bytes 3244040 | tf_op jit(solution)/shard_map/ppermute | solution.py:476
  36.7 4.1 %collective-permute-start.7 = (f32[22,48,256]{2,1,0:T(8,128)S(1)}, f32[22,48,256]{2,1,0:T(8,128)S(1)}, u32[]{:S(2)}, u32[]{:S(2)}) collective-permute-start(f32[22,48,256]{2,1,0:T(8,128)S(1)} %get-tuple-element.70), channel_id=1, source_target_pairs={{4,0},{8,4},{12,8},{16,12},{20,16},{24,20},{28,24},{32,28},{36,32}... | collective-permute-start | bytes 3244040 | tf_op jit(solution)/shard_map/ppermute | solution.py:477
  40.8 1.3 %collective-permute-start.9 = (f32[22,48,256]{2,1,0:T(8,128)S(1)}, f32[22,48,256]{2,1,0:T(8,128)S(1)}, u32[]{:S(2)}, u32[]{:S(2)}) collective-permute-start(f32[22,48,256]{2,1,0:T(8,128)S(1)} %collective-permute-done.8), channel_id=1, source_target_pairs={{12,64},{45,65},{14,66},{47,67},{76,128},{112,60},{109,129},{81,61... | collective-permute-start | bytes 3244040 | tf_op jit(solution)/shard_map/ppermute | solution.py:452
  42.1 1.2 %band_steps.1 = f32[16,8,8,128]{3,2,1,0:T(8,128)S(1)} custom-call(f32[48,32,128]{2,1,0:T(8,128)S(1)} %get-tuple-element.62.ext, f32[3,32,128]{2,1,0:T(8,128)S(1)} %collective-permute-done.2.recv_a, f32[3,32,128]{2,1,0:T(8,128)S(1)} %collective-permute-done.3.recv_b), custom_call_target="tpu_custom_call" | custom-call | tf_op jit(solution)/shard_map/band_steps/pallas_call | solution.py:464
  43.3 4.8 %collective-permute-done.4.from_left.el = f32[22,16,256]{2,1,0:T(8,128)S(1)} collective-permute-done((f32[22,16,256]{2,1,0:T(8,128)S(1)}, f32[22,16,256]{2,1,0:T(8,128)S(1)}, u32[]{:S(2)}, u32[]{:S(2)}) %collective-permute-start.4) | collective-permute-done | bytes 360480 | tf_op jit(solution)/shard_map/ppermute | solution.py:429
  48.1 10.1 %collective-permute-done.5.from_right.er = f32[22,16,256]{2,1,0:T(8,128)S(1)} collective-permute-done((f32[22,16,256]{2,1,0:T(8,128)S(1)}, f32[22,16,256]{2,1,0:T(8,128)S(1)}, u32[]{:S(2)}, u32[]{:S(2)}) %collective-permute-start.5) | collective-permute-done | bytes 360480 | tf_op jit(solution)/shard_map/ppermute | solution.py:430
  58.2 0.3 pack_y.1
  58.5 1.9 %collective-permute-start.11 = (f32[92,8,256]{2,1,0:T(8,128)S(1)}, f32[92,8,256]{2,1,0:T(8,128)S(1)}, u32[]{:S(2)}, u32[]{:S(2)}) collective-permute-start(f32[92,8,256]{2,1,0:T(8,128)S(1)} %get-tuple-element.73), channel_id=1, source_target_pairs={{0,0},{1,2},{2,1},{3,3},{4,4},{5,6},{6,5},{7,7},{8,8},{9,10},{10,9... | collective-permute-start | bytes 2261000 | tf_op jit(solution)/shard_map/ppermute | solution.py:489
  60.5 0.1 collective-permute-start.10
  60.6 26.5 %all_to_all.5 = f32[16,64,128]{2,1,0:T(8,128)S(1)} all-to-all(f32[16,64,128]{2,1,0:T(8,128)S(1)} %bitcast.8), channel_id=1, replica_groups=mesh['sec'=4,'gx'=16,'gy'=4] {'gx'}, dimensions={0} | all-to-all | bytes 1048576 | tf_op jit(solution)/shard_map/all_to_all | solution.py:474
  87.1 2.6 %pick.1 = (f32[4,8,128]{2,1,0:T(8,128)S(1)}, f32[4,8,128]{2,1,0:T(8,128)S(1)}, f32[4,8,128]{2,1,0:T(8,128)S(1)}, f32[4,8,128]{2,1,0:T(8,128)S(1)}) custom-call(f32[128,8,128]{2,1,0:T(8,128)S(1)} %bitcast.7, s32[16,128]{1,0:T(8,128)S(1)} %bitcast.13), custom_call_target="tpu_custom_call" | custom-call | tf_op jit(solution)/shard_map/pick/pallas_call | solution.py:491
  89.7 0.1 collective-permute-start.12
  89.8 1.8 %collective-permute-start.13 = (f32[4,8,128]{2,1,0:T(8,128)S(1)}, f32[4,8,128]{2,1,0:T(8,128)S(1)}, u32[]{:S(2)}, u32[]{:S(2)}) collective-permute-start(f32[4,8,128]{2,1,0:T(8,128)S(1)} %get-tuple-element.81), channel_id=1, source_target_pairs={{0,2},{1,3},{2,0},{3,1},{4,6},{5,7},{6,4},{7,5},{8,10},{9,11},{10,... | collective-permute-start | bytes 49160 | tf_op jit(solution)/shard_map/ppermute | solution.py:501
  91.6 11.9 %region.1 = f32[16,64,256]{2,1,0:T(8,128)} custom-call(f32[16,64,256]{2,1,0:T(8,128)S(1)} %copy-done, f32[16,64,256]{2,1,0:T(8,128)S(1)} %copy-done.1, f32[16,64,256]{2,1,0:T(8,128)S(1)} %copy-done.2, f32[22,16,256]{2,1,0:T(8,128)S(1)} %collective-permute-done.4.from_left.el, f32[22,16,256]{2,1,0:T(8,128)S(1)} %collective-permute-done.5.from_right.er, ...), custom_call_target="tpu_custom_call" | custom-call | tf_op jit(solution)/shard_map/region/pallas_call | solution.py:504
  103.6 2.2 %last_rows.1 = f32[64,512]{1,0:T(8,128)} custom-call(s32[8]{0:T(128)S(1)} %copy-done.8, f32[8,16]{1,0:T(8,128)S(1)} %copy-done.6, f32[8,16]{1,0:T(8,128)S(1)} %copy-done.7, s32[64,512]{1,0:T(8,128)S(1)} %bitcast.10, f32[64,512]{1,0:T(8,128)S(1)} %bitcast.12, f32[8,512]{1,0:T(8,128)S(1)} %get-tuple-element.84.edge, ...), custom_call_target="tpu_custom_call", output_to_operand_aliasing={{}: (10, {})} | custom-call | tf_op jit(solution)/shard_map/last_rows/pallas_call | solution.py:515
  (29 shorter events, 0.1 us)
Async XLA Ops:
  0.6 16.9 %copy-start.2 = (f32[16,64,256]{2,1,0:T(8,128)S(1)}, f32[16,64,256]{2,1,0:T(8,128)}, u32[]{:S(2)}) copy-start(f32[16,64,256]{2,1,0:T(8,128)} %c.4) | copy-start | bytes 3145732
  0.6 16.9 %copy-start.1 = (f32[16,64,256]{2,1,0:T(8,128)S(1)}, f32[16,64,256]{2,1,0:T(8,128)}, u32[]{:S(2)}) copy-start(f32[16,64,256]{2,1,0:T(8,128)} %p.4) | copy-start | bytes 3145732
  0.7 16.9 %copy-start = (f32[16,64,256]{2,1,0:T(8,128)S(1)}, f32[16,64,256]{2,1,0:T(8,128)}, u32[]{:S(2)}) copy-start(f32[16,64,256]{2,1,0:T(8,128)} %u.4) | copy-start | bytes 3145732
  0.7 10.7 %copy-start.9 = (s32[1,512]{1,0:T(1,128)S(1)}, s32[1,512]{1,0:T(1,128)}, u32[]{:S(2)}) copy-start(s32[1,512]{1,0:T(1,128)} %param.13) | copy-start | bytes 6148
  3.5 22.5 %collective-permute-start.1 = (f32[24,8,128]{2,1,0:T(8,128)}, f32[24,8,128]{2,1,0:T(8,128)S(1)}, u32[]{:S(2)}, u32[]{:S(2)}) collective-permute-start(f32[24,8,128]{2,1,0:T(8,128)} %get-tuple-element.57), channel_id=1, source_target_pairs={{0,252},{4,0},{8,4},{12,8},{16,12},{20,16},{24,20},{28,24},{32,28}... | collective-permute-start | bytes 294920 | tf_op jit(solution)/shard_map/ppermute | solution.py:415
  4.0 22.0 %collective-permute-start = (f32[24,8,128]{2,1,0:T(8,128)}, f32[24,8,128]{2,1,0:T(8,128)S(1)}, u32[]{:S(2)}, u32[]{:S(2)}) collective-permute-start(f32[24,8,128]{2,1,0:T(8,128)} %get-tuple-element.46), channel_id=1, source_target_pairs={{0,4},{4,8},{8,12},{12,16},{16,20},{20,24},{24,28},{28,32},{32,36}... | collective-permute-start | bytes 294920 | tf_op jit(solution)/shard_map/ppermute | solution.py:414
  17.5 0.9 copy-start.3
  17.5 1.0 copy-start.4
  17.5 1.0 copy-start.6
  17.6 0.9 copy-start.7
  17.6 0.9 copy-start.8
  17.6 9.8 %copy-start.5 = (f32[48,8,128]{2,1,0:T(8,128)S(1)}, f32[48,8,128]{2,1,0:T(8,128)}, u32[]{:S(2)}) copy-start(f32[48,8,128]{2,1,0:T(8,128)} %get-tuple-element.51.band) | copy-start | bytes 589828
  26.0 14.7 %collective-permute-start.8 = (f32[22,48,256]{2,1,0:T(8,128)S(1)}, f32[22,48,256]{2,1,0:T(8,128)S(1)}, u32[]{:S(2)}, u32[]{:S(2)}) collective-permute-start(f32[22,48,256]{2,1,0:T(8,128)S(1)} %get-tuple-element.71), channel_id=1, source_target_pairs={{60,12},{0,48},{61,45},{1,17},{62,14},{2,50},{63,47},{3,19},{124,7... | collective-permute-start | bytes 3244040 | tf_op jit(solution)/shard_map/ppermute | solution.py:451
  29.7 5.7 %collective-permute-start.2 = (f32[3,32,128]{2,1,0:T(8,128)S(1)}, f32[3,32,128]{2,1,0:T(8,128)S(1)}, u32[]{:S(2)}, u32[]{:S(2)}) collective-permute-start(f32[3,32,128]{2,1,0:T(8,128)S(1)} %get-tuple-element.63), channel_id=1, source_target_pairs={{0,1},{1,0},{2,3},{3,2},{4,5},{5,4},{6,7},{7,6},{8,9},{9,8},{10,11... | collective-permute-start | bytes 147464 | tf_op jit(solution)/shard_map/ppermute | solution.py:462
  30.0 6.7 %collective-permute-start.3 = (f32[3,32,128]{2,1,0:T(8,128)S(1)}, f32[3,32,128]{2,1,0:T(8,128)S(1)}, u32[]{:S(2)}, u32[]{:S(2)}) collective-permute-start(f32[3,32,128]{2,1,0:T(8,128)S(1)} %get-tuple-element.64), channel_id=1, source_target_pairs={{0,0},{1,2},{2,1},{3,3},{4,4},{5,6},{6,5},{7,7},{8,8},{9,10},{10,9... | collective-permute-start | bytes 147464 | tf_op jit(solution)/shard_map/ppermute | solution.py:463
  33.9 14.3 %collective-permute-start.4 = (f32[22,16,256]{2,1,0:T(8,128)S(1)}, f32[22,16,256]{2,1,0:T(8,128)S(1)}, u32[]{:S(2)}, u32[]{:S(2)}) collective-permute-start(f32[22,16,256]{2,1,0:T(8,128)S(1)} %get-tuple-element.65), channel_id=1, source_target_pairs={{0,4},{4,8},{8,12},{12,16},{16,20},{20,24},{24,28},{28,32},{32,36}... | collective-permute-start | bytes 1081352 | tf_op jit(solution)/shard_map/ppermute | solution.py:429
  34.7 23.5 %collective-permute-start.5 = (f32[22,16,256]{2,1,0:T(8,128)S(1)}, f32[22,16,256]{2,1,0:T(8,128)S(1)}, u32[]{:S(2)}, u32[]{:S(2)}) collective-permute-start(f32[22,16,256]{2,1,0:T(8,128)S(1)} %get-tuple-element.66), channel_id=1, source_target_pairs={{0,252},{4,0},{8,4},{12,8},{16,12},{20,16},{24,20},{28,24},{32,28}... | collective-permute-start | bytes 1081352 | tf_op jit(solution)/shard_map/ppermute | solution.py:430
  35.4 54.4 %collective-permute-start.6 = (f32[22,48,256]{2,1,0:T(8,128)S(1)}, f32[22,48,256]{2,1,0:T(8,128)S(1)}, u32[]{:S(2)}, u32[]{:S(2)}) collective-permute-start(f32[22,48,256]{2,1,0:T(8,128)S(1)} %get-tuple-element.69), channel_id=1, source_target_pairs={{0,4},{4,8},{8,12},{12,16},{16,20},{20,24},{24,28},{28,32},{32,36}... | collective-permute-start | bytes 3244040 | tf_op jit(solution)/shard_map/ppermute | solution.py:476
  36.7 54.9 %collective-permute-start.7 = (f32[22,48,256]{2,1,0:T(8,128)S(1)}, f32[22,48,256]{2,1,0:T(8,128)S(1)}, u32[]{:S(2)}, u32[]{:S(2)}) collective-permute-start(f32[22,48,256]{2,1,0:T(8,128)S(1)} %get-tuple-element.70), channel_id=1, source_target_pairs={{4,0},{8,4},{12,8},{16,12},{20,16},{24,20},{28,24},{32,28},{36,32}... | collective-permute-start | bytes 3244040 | tf_op jit(solution)/shard_map/ppermute | solution.py:477
  40.8 50.8 %collective-permute-start.9 = (f32[22,48,256]{2,1,0:T(8,128)S(1)}, f32[22,48,256]{2,1,0:T(8,128)S(1)}, u32[]{:S(2)}, u32[]{:S(2)}) collective-permute-start(f32[22,48,256]{2,1,0:T(8,128)S(1)} %collective-permute-done.8), channel_id=1, source_target_pairs={{12,64},{45,65},{14,66},{47,67},{76,128},{112,60},{109,129},{81,61... | collective-permute-start | bytes 3244040 | tf_op jit(solution)/shard_map/ppermute | solution.py:452
  58.5 31.1 %collective-permute-start.11 = (f32[92,8,256]{2,1,0:T(8,128)S(1)}, f32[92,8,256]{2,1,0:T(8,128)S(1)}, u32[]{:S(2)}, u32[]{:S(2)}) collective-permute-start(f32[92,8,256]{2,1,0:T(8,128)S(1)} %get-tuple-element.73), channel_id=1, source_target_pairs={{0,0},{1,2},{2,1},{3,3},{4,4},{5,6},{6,5},{7,7},{8,8},{9,10},{10,9... | collective-permute-start | bytes 2261000 | tf_op jit(solution)/shard_map/ppermute | solution.py:489
  60.5 31.1 %collective-permute-start.10 = (f32[92,8,256]{2,1,0:T(8,128)S(1)}, f32[92,8,256]{2,1,0:T(8,128)S(1)}, u32[]{:S(2)}, u32[]{:S(2)}) collective-permute-start(f32[92,8,256]{2,1,0:T(8,128)S(1)} %get-tuple-element.72), channel_id=1, source_target_pairs={{0,1},{1,0},{2,3},{3,2},{4,5},{5,4},{6,7},{7,6},{8,9},{9,8},{10,11... | collective-permute-start | bytes 2261000 | tf_op jit(solution)/shard_map/ppermute | solution.py:488
  89.7 13.9 %collective-permute-start.12 = (f32[4,8,128]{2,1,0:T(8,128)S(1)}, f32[4,8,128]{2,1,0:T(8,128)S(1)}, u32[]{:S(2)}, u32[]{:S(2)}) collective-permute-start(f32[4,8,128]{2,1,0:T(8,128)S(1)} %get-tuple-element.80), channel_id=1, source_target_pairs={{0,1},{1,2},{2,3},{3,0},{4,5},{5,6},{6,7},{7,4},{8,9},{9,10},{10,1... | collective-permute-start | bytes 49160 | tf_op jit(solution)/shard_map/ppermute | solution.py:501
  89.8 13.8 %collective-permute-start.13 = (f32[4,8,128]{2,1,0:T(8,128)S(1)}, f32[4,8,128]{2,1,0:T(8,128)S(1)}, u32[]{:S(2)}, u32[]{:S(2)}) collective-permute-start(f32[4,8,128]{2,1,0:T(8,128)S(1)} %get-tuple-element.81), channel_id=1, source_target_pairs={{0,2},{1,3},{2,0},{3,1},{4,6},{5,7},{6,4},{7,5},{8,10},{9,11},{10,... | collective-permute-start | bytes 49160 | tf_op jit(solution)/shard_map/ppermute | solution.py:501
  91.6 12.0 %collective-permute-start.14 = (f32[4,8,128]{2,1,0:T(8,128)S(1)}, f32[4,8,128]{2,1,0:T(8,128)S(1)}, u32[]{:S(2)}, u32[]{:S(2)}) collective-permute-start(f32[4,8,128]{2,1,0:T(8,128)S(1)} %get-tuple-element.82), channel_id=1, source_target_pairs={{0,3},{1,0},{2,1},{3,2},{4,7},{5,4},{6,5},{7,6},{8,11},{9,8},{10,9... | collective-permute-start | bytes 49160 | tf_op jit(solution)/shard_map/ppermute | solution.py:501
